TPU v7x, 32 devices: a whole 2x2x4 slice. The times are simulated.
32 devices in a mesh: replica: 4 (over z), tensor: 2 (over core), section: 4 (over y, x).
Axes of the slice: x: 2, y: 2, z: 4, core: 2. Of those that a mesh axis runs over, the one named last changes fastest.
Arguments:
- weight: bfloat16 [4096, 1024], P('section', 'tensor'), may hold values from -3 to 3
- grads: bfloat16 [4, 4096, 1024], P('replica', 'section', 'tensor'), may hold values from -83 to 83
- error: bfloat16 [4, 4096, 1024], P('replica', 'section', 'tensor'), may hold values from -3 to 3
- momentum: float32 [4096, 1024], P('section', 'tensor'), may hold values from -6 to 6
- basis: float32 [1024, 32], P('tensor'), may hold values from -6 to 6
- gram_root: float32 [32, 32], replicated, may hold values from -1 to 1
- gain: float32 [2, 4096], P(None, ('tensor', 'section')), may hold values from 0.5 to 1.5
- gain_momentum: float32 [2, 4096], P(None, ('tensor', 'section')), may hold values from -3 to 3
- gain_grads: float32 [4, 2, 4096], P('replica', None, ('tensor', 'section')), may hold values from -176 to 176
Outputs:
- new_weight: bfloat16 [4096, 1024], P(None, 'tensor')
- new_error: bfloat16 [4, 4096, 1024], P('replica', 'section', 'tensor')
- new_momentum: float32 [4096, 1024], P('section', 'tensor')
- new_gain: float32 [2, 4096], replicated
- new_gain_momentum: float32 [2, 4096], P(None, ('tensor', 'section'))
All inputs are finite; a program needn't handle non-finite values.
Results may differ from a plain program's by a relative error of at most 0.0004.
Values may be sent and summed in bfloat16 or wider, within the bound.
No kernel may reach another device: no remote copies, remote signals or barrier semaphores. Data moves between devices by JAX's collectives and lax.ppermute only.
A program may use at most 64 MiB of HBM per device.

v0:
```python
import jax
import jax.numpy as jnp
from jax import lax
from jax.sharding import PartitionSpec as P


def on_device(weight, grads, error, momentum, basis, gram_root, gain, gain_momentum, gain_grads):
    highest = lax.Precision.HIGHEST
    replicas = lax.axis_size("replica")
    tensors = lax.axis_size("tensor")
    sections = lax.axis_size("section")
    merged = grads[0].astype(jnp.float32) + error[0].astype(jnp.float32)
    lowp_term = jnp.dot(merged, basis, precision=highest)
    lowp_total = lax.psum(lowp_term, ("replica", "tensor"))
    gain_total = lax.psum(gain_grads[0], "replica")
    lowp = lowp_total / replicas
    ortho = jnp.dot(lowp, gram_root, precision=highest)
    basis_term = jnp.dot(merged.T, ortho, precision=highest)
    newbasis = lax.psum(basis_term, ("replica", "section")) / replicas
    approx = jnp.dot(ortho, newbasis.T, precision=highest)
    new_error = (merged - approx).astype(jnp.bfloat16)[None]
    square_sum = lax.psum(jnp.sum(approx * approx), ("tensor", "section"))
    entries = approx.shape[0] * approx.shape[1] * tensors * sections
    scale = lax.rsqrt(square_sum / entries + 1e-06)
    update = scale * approx
    new_momentum = 0.9 * momentum + update
    local_weight = (weight.astype(jnp.float32) - 0.05 * (update + 0.9 * new_momentum)).astype(
        jnp.bfloat16
    )
    new_weight = lax.all_gather(local_weight, "section", axis=0, tiled=True)
    gain_mean = gain_total / replicas
    new_gain_momentum = 0.9 * gain_momentum + gain_mean
    local_gain = gain - 0.02 * (gain_mean + 0.9 * new_gain_momentum)
    new_gain = lax.all_gather(local_gain, ("tensor", "section"), axis=1, tiled=True)
    return (new_weight, new_error, new_momentum, new_gain, new_gain_momentum)


def solution(mesh):
    placed = (
        P("section", "tensor"),
        P("replica", "section", "tensor"),
        P("replica", "section", "tensor"),
        P("section", "tensor"),
        P("tensor", None),
        P(),
        P(None, ("tensor", "section")),
        P(None, ("tensor", "section")),
        P("replica", None, ("tensor", "section")),
    )
    return jax.shard_map(
        on_device,
        mesh=mesh,
        in_specs=placed,
        out_specs=(
            P(None, "tensor"),
            P("replica", "section", "tensor"),
            P("section", "tensor"),
            P(),
            P(None, ("tensor", "section")),
        ),
        check_vma=False,
    )
```

profile of v0, /device:TPU:0, one launch (start us, length us, event | category | flops | bytes accessed | tf_op | source)
XLA Modules:
  0.0 273.3 jit_solution(196547886379686302)
XLA Ops:
  7.2 0.0 copy-start
  7.2 0.0 copy-start.2
  7.2 0.0 copy-start.1
  7.2 0.0 copy-start.4
  7.2 0.0 all-reduce.3.cloned.1.call-start
  7.3 0.8 copy-done
  8.0 4.1 %fusion.2 = f32[1024,32]{1,0:T(8,128)} fusion(f32[512,32]{0,1:T(8,128)S(1)} %copy-done, bf16[1,1024,512]{2,1,0:T(8,128)(2,1)} %param.11, bf16[1,1024,512]{2,1,0:T(8,128)(2,1)} %param.10), kind=kOutput, calls=%fused_computation.3 | convolution fusion | flops 202899456 | bytes 2293760 | tf_op jit(solution)/shard_map/dot_general | solution.py:13
  12.1 0.0 all-reduce.3.cloned.1.call-update
  12.2 0.0 all-reduce.5.cloned.1.call-start
  12.2 58.9 %all-reduce.3.cloned.1.call-done = f32[1024,32]{1,0:T(8,128)} async-done(((f32[1024,32]{1,0:T(8,128)}), f32[1024,32]{1,0:T(8,128)}) %all-reduce.3.cloned.1.call-update) | async-done | bytes 131088 | tf_op jit(solution)/shard_map/psum | solution.py:14
  71.1 0.0 copy-done.4
  71.1 1.7 fusion.6
  72.9 0.0 copy-done.2
  72.9 0.0 copy-done.1
  72.9 0.0 copy-start.3
  72.9 4.1 %fusion = f32[512,32]{1,0:T(8,128)} fusion(f32[1024,32]{0,1:T(8,128)S(1)} %fusion.6, bf16[1,1024,512]{2,1,0:T(8,128)(2,1)S(1)} %copy-done.1, bf16[1,1024,512]{2,1,0:T(8,128)(2,1)S(1)} %copy-done.2), kind=kOutput, calls=%fused_computation.1 | convolution fusion | flops 202899456 | bytes 2293760 | tf_op jit(solution)/shard_map/dot_general | solution.py:18
  77.0 0.0 all-reduce.5.cloned.1.call-update
  77.1 0.0 all-gather.2.cloned.1.call-start
  77.1 106.4 %all-reduce.5.cloned.1.call-done = f32[512,32]{1,0:T(8,128)} async-done(((f32[512,32]{1,0:T(8,128)}), f32[512,32]{1,0:T(8,128)}) %all-reduce.5.cloned.1.call-update) | async-done | bytes 65552 | tf_op jit(solution)/shard_map/psum | solution.py:19
  183.5 4.8 %multiply_reduce_fusion = (f32[]{:T(128)}, f32[1024,512]{1,0:T(8,128)}) fusion(f32[1024,32]{0,1:T(8,128)S(1)} %fusion.6, f32[512,32]{1,0:T(8,128)} %all-reduce.5.cloned.1.call-done), kind=kOutput, calls=%fused_computation.8 | convolution fusion | flops 202391552 | bytes 2293764 | tf_op jit(solution)/shard_map/dot_general | solution.py:20
  188.3 14.8 %psum.30 = f32[]{:T(128)} all-reduce(f32[]{:T(128)} %get-tuple-element.10), channel_id=1, replica_groups=mesh['replica'=4,'tensor'=2,'section'=4] {'tensor','section'}, use_global_device_ids=true, to_apply=%region_3.0 | all-reduce | flops 1 | bytes 8 | tf_op jit(solution)/shard_map/psum | solution.py:22
  203.8 0.0 copy-done.3
  203.8 0.0 copy-start.7
  203.8 0.0 copy-start.5
  203.8 0.0 copy-start.6
  203.8 4.9 %subtract_convert_fusion = (bf16[1024,512]{1,0:T(8,128)(2,1)}, f32[1024,512]{1,0:T(8,128)}, bf16[1,1024,512]{2,1,0:T(8,128)(2,1)}) fusion(bf16[1024,512]{1,0:T(8,128)(2,1)S(1)} %copy-done.3, f32[1024,512]{1,0:T(8,128)} %get-tuple-element.11, f32[]{:T(128)S(6)} %rsqrt.3, f32[1024,512]{1,0:T(8,128)} %param.12, bf16[1,1024,512]{2,1,0:T(8,128)(2,1)S(1)} %copy-done.1, ...), kind=kLoop, calls=%fused_computation.6 | loop fusion | flops 7340032 | bytes 11534340 | tf_op jit(solution)/shard_map/convert_element_type | solution.py:27
  208.7 0.0 all-gather.2.cloned.1.call-update
  208.8 0.0 copy-done.7
  208.8 10.7 %psum.31 = f32[2,512]{1,0:T(2,128)S(1)} all-reduce(f32[2,512]{1,0:T(2,128)S(1)} %bitcast.17), channel_id=1, replica_groups=mesh['replica'=4,'tensor'=2,'section'=4] {'replica'}, use_global_device_ids=true, to_apply=%region_4.0 | all-reduce | flops 1024 | bytes 8192 | tf_op jit(solution)/shard_map/psum | solution.py:15
  219.5 0.0 copy-done.5
  219.5 0.0 copy-done.6
  219.5 0.6 multiply_subtract_fusion
  220.1 24.1 %all_gather.7 = f32[2,4096]{1,0:T(2,128)S(1)} all-gather(f32[2,512]{1,0:T(2,128)S(1)} %get-tuple-element.5), channel_id=1, replica_groups=mesh['replica'=4,'tensor'=2,'section'=4] {'tensor','section'}, dimensions={1}, use_global_device_ids=true | all-gather | bytes 36864 | tf_op jit(solution)/shard_map/all_gather | solution.py:34
  244.2 17.5 %all-gather.2.cloned.1.call-done = bf16[4096,512]{1,0:T(8,128)(2,1)} async-done(((bf16[1024,512]{1,0:T(8,128)(2,1)}), bf16[4096,512]{1,0:T(8,128)(2,1)}) %all-gather.2.cloned.1.call-update) | async-done | bytes 4194320 | tf_op jit(solution)/shard_map/all_gather | solution.py:30
  261.7 4.5 %copy.18 = bf16[4096,512]{1,0:T(8,128)(2,1)} copy(bf16[4096,512]{1,0:T(8,128)(2,1)} %all-gather.2.cloned.1.call-done) | data formatting | bytes 8388608
  266.2 0.6 copy.19
Async XLA Ops:
  7.2 0.8 copy-start
  7.2 65.7 %copy-start.2 = (bf16[1,1024,512]{2,1,0:T(8,128)(2,1)S(1)}, bf16[1,1024,512]{2,1,0:T(8,128)(2,1)}, u32[]{:S(2)}) copy-start(bf16[1,1024,512]{2,1,0:T(8,128)(2,1)} %param.10) | copy-start | bytes 3145732
  7.2 65.7 %copy-start.1 = (bf16[1,1024,512]{2,1,0:T(8,128)(2,1)S(1)}, bf16[1,1024,512]{2,1,0:T(8,128)(2,1)}, u32[]{:S(2)}) copy-start(bf16[1,1024,512]{2,1,0:T(8,128)(2,1)} %param.11) | copy-start | bytes 3145732
  7.2 63.9 %copy-start.4 = (f32[32,32]{1,0:T(8,128)S(1)}, f32[32,32]{1,0:T(8,128)}, u32[]{:S(2)}) copy-start(f32[32,32]{1,0:T(8,128)} %param.14) | copy-start | bytes 12292
  7.2 63.9 %all-reduce.3.cloned.1.call-start = ((), (), s32[]{:S(2)}) async-start(), calls=%async_computation | async-start | bytes 1048576 | tf_op jit(solution)/shard_map/psum | solution.py:14
  12.2 171.3 %all-reduce.5.cloned.1.call-start = ((), (), s32[]{:S(2)}) async-start(), calls=%async_computation.1 | async-start | bytes 524288 | tf_op jit(solution)/shard_map/psum | solution.py:19
  72.9 130.9 %copy-start.3 = (bf16[1024,512]{1,0:T(8,128)(2,1)S(1)}, bf16[1024,512]{1,0:T(8,128)(2,1)}, u32[]{:S(2)}) copy-start(bf16[1024,512]{1,0:T(8,128)(2,1)} %param.9) | copy-start | bytes 3145732
  77.1 184.6 %all-gather.2.cloned.1.call-start = ((), (), s32[]{:S(2)}) async-start(), calls=%async_computation.2 | async-start | bytes 5242880 | tf_op jit(solution)/shard_map/all_gather | solution.py:30
  203.8 4.9 %copy-start.7 = (f32[1,2,512]{2,1,0:T(2,128)S(1)}, f32[1,2,512]{2,1,0:T(2,128)}, u32[]{:S(2)}) copy-start(f32[1,2,512]{2,1,0:T(2,128)} %param.17) | copy-start | bytes 12292
  203.8 15.6 %copy-start.5 = (f32[2,512]{1,0:T(2,128)S(1)}, f32[2,512]{1,0:T(2,128)}, u32[]{:S(2)}) copy-start(f32[2,512]{1,0:T(2,128)} %param.15) | copy-start | bytes 12292
  203.8 15.6 %copy-start.6 = (f32[2,512]{1,0:T(2,128)S(1)}, f32[2,512]{1,0:T(2,128)}, u32[]{:S(2)}) copy-start(f32[2,512]{1,0:T(2,128)} %param.16) | copy-start | bytes 12292
Sparse Core Ops, SparseCore 0:
  12.3 58.8 all-reduce.2
  77.8 105.6 all-reduce.4
  208.9 52.7 all-gather.1
where the time goes:
time: 274 us; the launch traced here: 273 us
  waiting for transfers between devices  183 us (67%)
  blocking collectives  49.7 us (18%)
  matrix products  14.8 us (5%)
  between operations  14.5 us (5%)
  local copies, waits for them, and re-layouts  5.88 us (2%)
  other arithmetic  5.48 us (2%)
    psum x1, waiting for transfers between devices, on_device(): newbasis = lax.psum(basis_term, ('replica', 'section')) / replicas  106 us
    psum x1, waiting for transfers between devices, on_device(): lowp_total = lax.psum(lowp_term, ('replica', 'tensor'))  58.9 us
    all_gather x1, blocking collectives, on_device(): lax.all_gather(local_gain, ('tensor', 'section'), axis=1, tiled=True)  24.1 us
    all_gather x1, waiting for transfers between devices, on_device(): new_weight = lax.all_gather(local_weight, 'section', axis=0, tiled=True)  17.5 us
    psum x1, blocking collectives, on_device(): square_sum = lax.psum(jnp.sum(approx * approx), ('tensor', 'section'))  14.8 us
    psum x1, blocking collectives, on_device(): gain_total = lax.psum(gain_grads[0], 'replica')  10.7 us
    unnamed x18, local copies, waits for them, and re-layouts  5.88 us
  transfers between devices with their start and end apart: 3, of which 3 were waited for; matrix products, arithmetic and copies ran while one was open for 0% of the time, Pallas kernels for 0%

commit v1 on v0

v1 whole, which is shorter than its diff:
```python
import jax
import jax.numpy as jnp
from jax import lax
from jax.sharding import PartitionSpec as P

HIGHEST = lax.Precision.HIGHEST


def swap(x, axis, distance):
    count = lax.axis_size(axis)
    return lax.ppermute(x, axis, [(i, i ^ distance) for i in range(count)])


def total(x, axis):
    count = lax.axis_size(axis)
    distance = 1
    while distance < count:
        if count // distance >= 4:
            a = swap(x, axis, distance)
            b = swap(x, axis, 2 * distance)
            c = swap(x, axis, 3 * distance)
            x = (x + a) + (b + c)
            distance *= 4
        else:
            x = x + swap(x, axis, distance)
            distance *= 2
    return x


def gathered(x, axis):
    count = lax.axis_size(axis)
    me = lax.axis_index(axis)
    half = x.shape[0] // 2
    if count == 4:
        one = swap(x, axis, 1)
        two = swap(x, axis, 2)
        low = swap(two[:half], axis, 1)
        high = swap(one[half:], axis, 2)
        parts = [x, one, two, jnp.concatenate([low, high], axis=0)]
    else:
        parts = [x] + [swap(x, axis, d) for d in range(1, count)]
    rows = x.shape[0]
    out = jnp.zeros((count * rows,) + x.shape[1:], x.dtype)
    for distance, part in enumerate(parts):
        out = lax.dynamic_update_slice(out, part, ((me ^ distance) * rows, 0))
    return out


def on_device(weight, grads, error, momentum, basis, gram_root, gain, gain_momentum, gain_grads):
    replicas = lax.axis_size("replica")
    tensors = lax.axis_size("tensor")
    sections = lax.axis_size("section")
    tensor = lax.axis_index("tensor")
    section = lax.axis_index("section")
    rows, cols = weight.shape
    rank = basis.shape[1]
    merged = grads[0].astype(jnp.float32) + error[0].astype(jnp.float32)
    lowp_term = lax.dot_general(basis, merged, (((0,), (1,)), ((), ())), precision=HIGHEST)
    half = rows // 2
    kept = lax.dynamic_slice(lowp_term, (0, tensor * half), (rank, half))
    given = lax.dynamic_slice(lowp_term, (0, (1 - tensor) * half), (rank, half))
    pair = kept + swap(given, "tensor", 1)
    pair = jnp.concatenate([pair, gain_grads[0]], axis=0)
    pair = total(pair, "replica")
    gain_mean = pair[rank:] / replicas
    mine = pair[:rank]
    other = swap(mine, "tensor", 1)
    first = jnp.where(tensor == 0, mine, other)
    second = jnp.where(tensor == 0, other, mine)
    lowp = jnp.concatenate([first, second], axis=1) / replicas
    ortho = lax.dot_general(gram_root, lowp, (((0,), (0,)), ((), ())), precision=HIGHEST)
    new_gain_momentum = 0.9 * gain_momentum + gain_mean
    local_gain = gain - 0.02 * (gain_mean + 0.9 * new_gain_momentum)
    basis_term = jnp.dot(ortho, merged, precision=HIGHEST)
    gram = lax.dot_general(ortho, ortho, (((1,), (1,)), ((), ())), precision=HIGHEST)
    joined = jnp.concatenate([basis_term, gram], axis=1)
    joined = total(total(joined, "section"), "replica") / replicas
    newbasis = joined[:, :cols]
    gram = joined[:, cols:]
    approx = lax.dot_general(ortho, newbasis, (((0,), (0,)), ((), ())), precision=HIGHEST)
    merged = grads[0].astype(jnp.float32) + error[0].astype(jnp.float32)
    new_error = (merged - approx).astype(jnp.bfloat16)[None]
    right = lax.dot_general(newbasis, newbasis, (((1,), (1,)), ((), ())), precision=HIGHEST)
    right = right + swap(right, "tensor", 1)
    entries = rows * cols * tensors * sections
    scale = lax.rsqrt(jnp.sum((gram / entries) * right) + 1e-06)
    update = scale * approx
    new_momentum = 0.9 * momentum + update
    local_weight = (weight.astype(jnp.float32) - 0.05 * (update + 0.9 * new_momentum)).astype(
        jnp.bfloat16
    )
    new_weight = gathered(local_weight, "section")
    wide = gathered(local_gain, "section")
    wide = wide.reshape(sections, 2, cols).transpose(1, 0, 2).reshape(2, sections * cols)
    other = swap(wide, "tensor", 1)
    new_gain = jnp.where(
        tensor == 0,
        jnp.concatenate([wide, other], axis=1),
        jnp.concatenate([other, wide], axis=1),
    )
    return (new_weight, new_error, new_momentum, new_gain, new_gain_momentum)


def solution(mesh):
    placed = (
        P("section", "tensor"),
        P("replica", "section", "tensor"),
        P("replica", "section", "tensor"),
        P("section", "tensor"),
        P("tensor", None),
        P(),
        P(None, ("tensor", "section")),
        P(None, ("tensor", "section")),
        P("replica", None, ("tensor", "section")),
    )
    return jax.shard_map(
        on_device,
        mesh=mesh,
        in_specs=placed,
        out_specs=(
            P(None, "tensor"),
            P("replica", "section", "tensor"),
            P("section", "tensor"),
            P(),
            P(None, ("tensor", "section")),
        ),
        check_vma=False,
    )
```

time: 274 us -> 101 us (0.37)
  waiting for transfers between devices: 183 us -> 52 us
  blocking collectives: 49.7 us -> 0 us
  starting transfers between devices: 0.12 us -> 22.7 us
  between operations: 14.5 us -> 1.61 us
  matrix products: 14.8 us -> 10.9 us
  local copies, waits for them, and re-layouts: 5.88 us -> 8.64 us
    psum x2 -> x0, waiting for transfers between devices: 165 us -> none  [the longest x1 106 us: on_device(): newbasis = lax.psum(basis_term, ('replica', 'section')) / replicas]
    ppermute x0 -> x21, waiting for transfers between devices: none -> 52 us  [swap(): return lax.ppermute(x, axis, [(i, i ^ distance) for i in range(count)])]
    psum x2 -> x0, blocking collectives: 25.5 us -> none  [the longest x1 14.8 us: on_device(): square_sum = lax.psum(jnp.sum(approx * approx), ('tensor', 'section'))]
    all_gather x1 -> x0, blocking collectives: 24.1 us -> none  [on_device(): lax.all_gather(local_gain, ('tensor', 'section'), axis=1, tiled=True)]
    ppermute x0 -> x21, starting transfers between devices: none -> 22.7 us  [swap(): return lax.ppermute(x, axis, [(i, i ^ distance) for i in range(count)])]
    all_gather x1 -> x0, waiting for transfers between devices: 17.5 us -> none  [on_device(): new_weight = lax.all_gather(local_weight, 'section', axis=0, tiled=True)]
    convert_element_type x1 -> x0, other arithmetic: 4.88 us -> none  [on_device(): (weight.astype(jnp.float32) - 0.05 * (update + 0.9 * new_momentum)).astyp...]
    unnamed x18 -> x20, local copies, waits for them, and re-layouts: 5.88 us -> 1.77 us
  transfers between devices with their start and end apart: 3 -> 21, of which waited for: 3 -> 16; matrix products, arithmetic and copies ran while one was open for 0% -> 7% of each run, Pallas kernels for 0% -> 0%
where the time goes in v1:
time: 101 us; the launch traced here: 100 us
  waiting for transfers between devices  52 us (51%)
  starting transfers between devices  22.7 us (22%)
  matrix products  10.9 us (11%)
  local copies, waits for them, and re-layouts  8.64 us (9%)
  other arithmetic  4.45 us (4%)
  between operations  1.61 us (2%)
    ppermute x21, waiting for transfers between devices, swap(): return lax.ppermute(x, axis, [(i, i ^ distance) for i in range(count)])  52 us
    ppermute x21, starting transfers between devices, swap(): return lax.ppermute(x, axis, [(i, i ^ distance) for i in range(count)])  22.7 us
    dot_general x1, matrix products, on_device(): lax.dot_general(ortho, newbasis, (((0,), (0,)), ((), ())), precision=HIGH...  5 us
    dot_general x1, matrix products, on_device(): lax.dot_general(basis, merged, (((0,), (1,)), ((), ())), precision=HIGHEST)  3.73 us
    dynamic_update_slice x4, local copies, waits for them, and re-layouts, gathered(): out = lax.dynamic_update_slice(out, part, ((me ^ distance) * rows, 0))  3.31 us
    broadcast_in_dim x2, local copies, waits for them, and re-layouts, gathered(): out = jnp.zeros((count * rows,) + x.shape[1:], x.dtype)  2.41 us
  transfers between devices with their start and end apart: 21, of which 16 were waited for; matrix products, arithmetic and copies ran while one was open for 7% of the time, Pallas kernels for 0%

profile of v1, /device:TPU:0, one launch (start us, length us, event | category | flops | bytes accessed | tf_op | source)
XLA Modules:
  0.0 100.3 jit_solution(387148010776484739)
XLA Ops:
  0.6 0.0 copy-start
  0.6 0.0 copy-start.1
  0.7 0.0 copy-start.2
  0.7 0.8 copy-done
  1.5 3.7 %fusion.2 = f32[1024,32]{0,1:T(8,128)S(1)} fusion(f32[512,32]{0,1:T(8,128)S(1)} %copy-done, bf16[1,1024,512]{2,1,0:T(8,128)(2,1)} %param.11, bf16[1,1024,512]{2,1,0:T(8,128)(2,1)} %param.10), kind=kOutput, calls=%fused_computation.3 | convolution fusion | flops 202899456 | bytes 2293760 | tf_op jit(solution)/shard_map/dot_general | solution.py:58
  5.2 0.5 collective-permute-start
  5.8 0.9 collective-permute-done
  6.7 4.0 %collective-permute-start.2 = (f32[34,512]{1,0:T(8,128)S(1)}, f32[34,512]{1,0:T(8,128)S(1)}, u32[]{:S(2)}, u32[]{:S(2)}) collective-permute-start(f32[34,512]{1,0:T(8,128)S(1)} %pad_maximum_fusion), channel_id=1, source_target_pairs={{0,16},{8,24},{16,0},{24,8},{1,17},{9,25},{17,1},{25,9},{2,18},{10... | collective-permute-start | bytes 208904 | tf_op jit(solution)/shard_map/ppermute | solution.py:11
  10.7 1.3 %collective-permute-start.3 = (f32[34,512]{1,0:T(8,128)S(1)}, f32[34,512]{1,0:T(8,128)S(1)}, u32[]{:S(2)}, u32[]{:S(2)}) collective-permute-start(f32[34,512]{1,0:T(8,128)S(1)} %pad_maximum_fusion), channel_id=1, source_target_pairs={{0,24},{8,16},{16,8},{24,0},{1,25},{9,17},{17,9},{25,1},{2,26},{10... | collective-permute-start | bytes 208904 | tf_op jit(solution)/shard_map/ppermute | solution.py:11
  12.1 0.2 collective-permute-start.1
  12.3 4.8 %collective-permute-done.2 = f32[34,512]{1,0:T(8,128)S(1)} collective-permute-done((f32[34,512]{1,0:T(8,128)S(1)}, f32[34,512]{1,0:T(8,128)S(1)}, u32[]{:S(2)}, u32[]{:S(2)}) %collective-permute-start.2) | collective-permute-done | bytes 69664 | tf_op jit(solution)/shard_map/ppermute | solution.py:11
  17.1 0.6 collective-permute-done.3
  17.6 0.7 collective-permute-done.1
  18.4 0.1 collective-permute-start.4
  18.5 1.2 %collective-permute-done.4 = f32[32,512]{1,0:T(8,128)S(1)} collective-permute-done((f32[32,512]{1,0:T(8,128)S(1)}, f32[32,512]{1,0:T(8,128)S(1)}, u32[]{:S(2)}, u32[]{:S(2)}) %collective-permute-start.4) | collective-permute-done | bytes 65568 | tf_op jit(solution)/shard_map/ppermute | solution.py:11
  19.8 0.3 fusion.6
  20.1 0.2 fusion.18
  20.4 1.5 %fusion = f32[32,512]{1,0:T(8,128)S(1)} fusion(f32[1024,32]{0,1:T(8,128)S(1)} %fusion.6, bf16[1,1024,512]{2,1,0:T(8,128)(2,1)S(1)} %copy-done.1, bf16[1,1024,512]{2,1,0:T(8,128)(2,1)S(1)} %copy-done.2), kind=kOutput, calls=%fused_computation.1 | convolution fusion | flops 202899456 | bytes 2293760 | tf_op jit(solution)/shard_map/dot_general | solution.py:74
  21.8 1.6 %collective-permute-start.6 = (f32[32,544]{1,0:T(8,128)S(1)}, f32[32,544]{1,0:T(8,128)S(1)}, u32[]{:S(2)}, u32[]{:S(2)}) collective-permute-start(f32[32,544]{1,0:T(8,128)S(1)} %pad_maximum_fusion.1), channel_id=1, source_target_pairs={{0,2},{1,3},{2,0},{3,1},{4,6},{5,7},{6,4},{7,5},{8,10},{9,11},{10,... | collective-permute-start | bytes 208904 | tf_op jit(solution)/shard_map/ppermute | solution.py:11
  23.5 1.4 %collective-permute-start.7 = (f32[32,544]{1,0:T(8,128)S(1)}, f32[32,544]{1,0:T(8,128)S(1)}, u32[]{:S(2)}, u32[]{:S(2)}) collective-permute-start(f32[32,544]{1,0:T(8,128)S(1)} %pad_maximum_fusion.1), channel_id=1, source_target_pairs={{0,3},{1,2},{2,1},{3,0},{4,7},{5,6},{6,5},{7,4},{8,11},{9,10},{10,... | collective-permute-start | bytes 208904 | tf_op jit(solution)/shard_map/ppermute | solution.py:11
  24.9 0.5 collective-permute-start.5
  25.4 1.5 %collective-permute-done.6 = f32[32,544]{1,0:T(8,128)S(1)} collective-permute-done((f32[32,544]{1,0:T(8,128)S(1)}, f32[32,544]{1,0:T(8,128)S(1)}, u32[]{:S(2)}, u32[]{:S(2)}) %collective-permute-start.6) | collective-permute-done | bytes 69664 | tf_op jit(solution)/shard_map/ppermute | solution.py:11
  26.9 2.7 %collective-permute-done.7 = f32[32,544]{1,0:T(8,128)S(1)} collective-permute-done((f32[32,544]{1,0:T(8,128)S(1)}, f32[32,544]{1,0:T(8,128)S(1)}, u32[]{:S(2)}, u32[]{:S(2)}) %collective-permute-start.7) | collective-permute-done | bytes 69664 | tf_op jit(solution)/shard_map/ppermute | solution.py:11
  29.6 0.0 collective-permute-done.5
  29.6 3.4 %collective-permute-start.10 = (f32[32,544]{1,0:T(8,128)S(1)}, f32[32,544]{1,0:T(8,128)S(1)}, u32[]{:S(2)}, u32[]{:S(2)}) collective-permute-start(f32[32,544]{1,0:T(8,128)S(1)} %add_add_fusion), channel_id=1, source_target_pairs={{0,24},{8,16},{16,8},{24,0},{1,25},{9,17},{17,9},{25,1},{2,26},{10... | collective-permute-start | bytes 208904 | tf_op jit(solution)/shard_map/ppermute | solution.py:11
  33.0 0.0 collective-permute-start.9
  33.0 1.0 %collective-permute-start.8 = (f32[32,544]{1,0:T(8,128)S(1)}, f32[32,544]{1,0:T(8,128)S(1)}, u32[]{:S(2)}, u32[]{:S(2)}) collective-permute-start(f32[32,544]{1,0:T(8,128)S(1)} %add_add_fusion), channel_id=1, source_target_pairs={{0,8},{8,0},{16,24},{24,16},{1,9},{9,1},{17,25},{25,17},{2,10},{10... | collective-permute-start | bytes 208904 | tf_op jit(solution)/shard_map/ppermute | solution.py:11
  34.1 2.6 %collective-permute-done.10 = f32[32,544]{1,0:T(8,128)S(1)} collective-permute-done((f32[32,544]{1,0:T(8,128)S(1)}, f32[32,544]{1,0:T(8,128)S(1)}, u32[]{:S(2)}, u32[]{:S(2)}) %collective-permute-start.10) | collective-permute-done | bytes 69664 | tf_op jit(solution)/shard_map/ppermute | solution.py:11
  36.7 3.3 %collective-permute-done.9 = f32[32,544]{1,0:T(8,128)S(1)} collective-permute-done((f32[32,544]{1,0:T(8,128)S(1)}, f32[32,544]{1,0:T(8,128)S(1)}, u32[]{:S(2)}, u32[]{:S(2)}) %collective-permute-start.9) | collective-permute-done | bytes 69664 | tf_op jit(solution)/shard_map/ppermute | solution.py:11
  39.9 0.0 collective-permute-done.8
  40.0 0.2 fusion.12
  40.2 0.1 collective-permute-start.11
  40.2 1.2 %collective-permute-done.11 = f32[32,32]{1,0:T(8,128)S(1)} collective-permute-done((f32[32,32]{1,0:T(8,128)S(1)}, f32[32,32]{1,0:T(8,128)S(1)}, u32[]{:S(2)}, u32[]{:S(2)}) %collective-permute-start.11) | collective-permute-done | bytes 4128 | tf_op jit(solution)/shard_map/ppermute | solution.py:11
  41.4 0.6 fusion.15
  42.7 0.0 copy-start.4
  42.7 0.0 copy-start.5
  42.7 2.4 %broadcast_in_dim.9 = bf16[4096,512]{1,0:T(8,128)(2,1)} broadcast(bf16[]{:T(256)} %constant.19.clone.1), dimensions={} | broadcast | bytes 4194306 | tf_op jit(solution)/shard_map/broadcast_in_dim | solution.py:43
  45.1 0.9 copy-done.5
  46.1 5.0 %constant_dynamic-update-slice_fusion.5 = (bf16[4096,512]{1,0:T(8,128)(2,1)}, bf16[1024,512]{1,0:T(8,128)(2,1)}, f32[1024,512]{1,0:T(8,128)}, f32[1024,512]{1,0:T(8,128)}) fusion(bf16[4096,512]{1,0:T(8,128)(2,1)} %broadcast_in_dim.9, s32[]{:T(128)S(6)} %select_n.55, f32[]{:T(128)S(6)} %rsqrt.3, bf16[1024,512]{1,0:T(8,128)(2,1)S(1)} %copy-done.5, ...), kind=kOutput, calls=%fused_computation.42 | convolution fusion | flops 206045184 | bytes 9633800 | tf_op jit(solution)/shard_map/dot_general | solution.py:80
  51.1 0.9 collective-permute-start.12
  52.0 1.5 %collective-permute-start.13 = (bf16[1024,512]{1,0:T(8,128)(2,1)}, bf16[1024,512]{1,0:T(8,128)(2,1)}, u32[]{:S(2)}, u32[]{:S(2)}) collective-permute-start(bf16[1024,512]{1,0:T(8,128)(2,1)} %get-tuple-element.9), channel_id=1, source_target_pairs={{0,2},{1,3},{2,0},{3,1},{4,6},{5,7},{6,4},{7,5},{8,10},{9,11},{10,... | collective-permute-start | bytes 3145736 | tf_op jit(solution)/shard_map/ppermute | solution.py:11
  53.5 0.6 constant_dynamic-update-slice_fusion.2
  54.1 1.1 %collective-permute-start.16 = (f32[2,512]{1,0:T(2,128)S(1)}, f32[2,512]{1,0:T(2,128)S(1)}, u32[]{:S(2)}, u32[]{:S(2)}) collective-permute-start(f32[2,512]{1,0:T(2,128)S(1)} %get-tuple-element.6), channel_id=1, source_target_pairs={{0,1},{1,0},{2,3},{3,2},{4,5},{5,4},{6,7},{7,6},{8,9},{9,8},{10,11... | collective-permute-start | bytes 12296 | tf_op jit(solution)/shard_map/ppermute | solution.py:11
  55.2 0.5 collective-permute-start.17
  55.7 20.9 %collective-permute-done.16 = f32[2,512]{1,0:T(2,128)S(1)} collective-permute-done((f32[2,512]{1,0:T(2,128)S(1)}, f32[2,512]{1,0:T(2,128)S(1)}, u32[]{:S(2)}, u32[]{:S(2)}) %collective-permute-start.16) | collective-permute-done | bytes 4128 | tf_op jit(solution)/shard_map/ppermute | solution.py:11
  76.6 1.5 %collective-permute-start.19 = (f32[1,512]{1,0:T(1,128)S(1)}, f32[1,512]{1,0:T(1,128)S(1)}, u32[]{:S(2)}, u32[]{:S(2)}) collective-permute-start(f32[1,512]{1,0:T(1,128)S(1)} %slice.39), channel_id=1, source_target_pairs={{0,2},{1,3},{2,0},{3,1},{4,6},{5,7},{6,4},{7,5},{8,10},{9,11},{10,... | collective-permute-start | bytes 6152 | tf_op jit(solution)/shard_map/ppermute | solution.py:11
  78.1 0.0 collective-permute-done.17
  78.1 0.9 collective-permute-start.18
  79.1 1.1 %collective-permute-done.19 = f32[1,512]{1,0:T(1,128)S(1)} collective-permute-done((f32[1,512]{1,0:T(1,128)S(1)}, f32[1,512]{1,0:T(1,128)S(1)}, u32[]{:S(2)}, u32[]{:S(2)}) %collective-permute-start.19) | collective-permute-done | bytes 2080 | tf_op jit(solution)/shard_map/ppermute | solution.py:11
  80.2 1.5 %collective-permute-done.18 = f32[1,512]{1,0:T(1,128)S(1)} collective-permute-done((f32[1,512]{1,0:T(1,128)S(1)}, f32[1,512]{1,0:T(1,128)S(1)}, u32[]{:S(2)}, u32[]{:S(2)}) %collective-permute-start.18) | collective-permute-done | bytes 2080 | tf_op jit(solution)/shard_map/ppermute | solution.py:11
  81.8 0.1 collective-permute-start.20
  81.9 1.1 %collective-permute-done.20 = f32[2,2048]{1,0:T(2,128)S(1)} collective-permute-done((f32[2,2048]{1,0:T(2,128)S(1)}, f32[2,2048]{1,0:T(2,128)S(1)}, u32[]{:S(2)}, u32[]{:S(2)}) %collective-permute-start.20) | collective-permute-done | bytes 16416 | tf_op jit(solution)/shard_map/ppermute | solution.py:11
  83.0 0.6 maximum_select_fusion
  83.6 0.0 collective-permute-done.12
  83.7 0.8 collective-permute-start.15
  84.4 0.0 collective-permute-done.13
  84.4 1.1 %slice.35 = bf16[512,512]{1,0:T(8,128)(2,1)S(1)} slice(bf16[1024,512]{1,0:T(8,128)(2,1)} %collective-permute-done.13), slice={[0:512], [0:512]} | slice | bytes 1048576 | tf_op jit(solution)/shard_map/slice | solution.py:37
  85.5 1.2 %collective-permute-start.14 = (bf16[512,512]{1,0:T(8,128)(2,1)S(1)}, bf16[512,512]{1,0:T(8,128)(2,1)S(1)}, u32[]{:S(2)}, u32[]{:S(2)}) collective-permute-start(bf16[512,512]{1,0:T(8,128)(2,1)S(1)} %slice.35), channel_id=1, source_target_pairs={{0,1},{1,0},{2,3},{3,2},{4,5},{5,4},{6,7},{7,6},{8,9},{9,8},{10,11... | collective-permute-start | bytes 1572872 | tf_op jit(solution)/shard_map/ppermute | solution.py:11
  86.7 1.5 %fusion.5 = bf16[1,1024,512]{2,1,0:T(8,128)(2,1)} fusion(f32[1024,512]{1,0:T(8,128)S(1)} %copy-done.3, bf16[1,1024,512]{2,1,0:T(8,128)(2,1)S(1)} %copy-done.1, bf16[1,1024,512]{2,1,0:T(8,128)(2,1)S(1)} %copy-done.2), kind=kLoop, calls=%fused_computation.9 | loop fusion | flops 2621440 | bytes 5242880 | tf_op jit(solution)/shard_map/broadcast_in_dim | solution.py:82
  88.2 1.0 %constant_dynamic-update-slice_fusion.4 = bf16[4096,512]{1,0:T(8,128)(2,1)} fusion(bf16[4096,512]{1,0:T(8,128)(2,1)} %get-tuple-element.8, bf16[1024,512]{1,0:T(8,128)(2,1)S(1)} %collective-permute-done.12, s32[]{:T(128)S(6)} %select_n.56), kind=kLoop, calls=%fused_computation.41 | loop fusion | bytes 2097156 | tf_op jit(solution)/shard_map/dynamic_update_slice | solution.py:45
  89.2 2.3 %constant_dynamic-update-slice_fusion.3 = bf16[4096,512]{1,0:T(8,128)(2,1)} fusion(bf16[4096,512]{1,0:T(8,128)(2,1)} %constant_dynamic-update-slice_fusion.4, bf16[1024,512]{1,0:T(8,128)(2,1)} %collective-permute-done.13, s32[]{:T(128)S(6)} %select_n.57), kind=kLoop, calls=%fused_computation.40 | loop fusion | bytes 2097156 | tf_op jit(solution)/shard_map/dynamic_update_slice | solution.py:45
  91.5 6.3 %collective-permute-done.15 = bf16[512,512]{1,0:T(8,128)(2,1)S(1)} collective-permute-done((bf16[512,512]{1,0:T(8,128)(2,1)S(1)}, bf16[512,512]{1,0:T(8,128)(2,1)S(1)}, u32[]{:S(2)}, u32[]{:S(2)}) %collective-permute-start.15) | collective-permute-done | bytes 524320 | tf_op jit(solution)/shard_map/ppermute | solution.py:11
  97.7 1.6 %collective-permute-done.14 = bf16[512,512]{1,0:T(8,128)(2,1)S(1)} collective-permute-done((bf16[512,512]{1,0:T(8,128)(2,1)S(1)}, bf16[512,512]{1,0:T(8,128)(2,1)S(1)}, u32[]{:S(2)}, u32[]{:S(2)}) %collective-permute-start.14) | collective-permute-done | bytes 524320 | tf_op jit(solution)/shard_map/ppermute | solution.py:11
  99.3 1.0 %maximum_dynamic-update-slice_fusion = bf16[4096,512]{1,0:T(8,128)(2,1)} fusion(bf16[4096,512]{1,0:T(8,128)(2,1)} %constant_dynamic-update-slice_fusion.3, s32[]{:T(128)S(6)} %select_n.58, bf16[512,512]{1,0:T(8,128)(2,1)S(1)} %collective-permute-done.15, bf16[512,512]{1,0:T(8,128)(2,1)S(1)} %collective-permute-done.14), kind=kLoop, calls=%fused_computation.10 | loop fusion | flops 2097152 | bytes 2097156 | tf_op jit(solution)/shard_map/dynamic_update_slice | solution.py:45
  (30 shorter events, 0.2 us)
Async XLA Ops:
  0.6 0.8 copy-start
  0.6 19.7 %copy-start.1 = (bf16[1,1024,512]{2,1,0:T(8,128)(2,1)S(1)}, bf16[1,1024,512]{2,1,0:T(8,128)(2,1)}, u32[]{:S(2)}) copy-start(bf16[1,1024,512]{2,1,0:T(8,128)(2,1)} %param.11) | copy-start | bytes 3145732
  0.7 19.7 %copy-start.2 = (bf16[1,1024,512]{2,1,0:T(8,128)(2,1)S(1)}, bf16[1,1024,512]{2,1,0:T(8,128)(2,1)}, u32[]{:S(2)}) copy-start(bf16[1,1024,512]{2,1,0:T(8,128)(2,1)} %param.10) | copy-start | bytes 3145732
  0.7 6.0 %copy-start.6 = (f32[1,2,512]{2,1,0:T(2,128)S(1)}, f32[1,2,512]{2,1,0:T(2,128)}, u32[]{:S(2)}) copy-start(f32[1,2,512]{2,1,0:T(2,128)} %param.17) | copy-start | bytes 12292
  0.7 19.1 %copy-start.7 = (f32[32,32]{1,0:T(8,128)S(1)}, f32[32,32]{1,0:T(8,128)}, u32[]{:S(2)}) copy-start(f32[32,32]{1,0:T(8,128)} %param.14) | copy-start | bytes 12292
  5.2 1.4 %collective-permute-start = (f32[32,512]{1,0:T(8,128)S(1)}, f32[32,512]{1,0:T(8,128)S(1)}, u32[]{:S(2)}, u32[]{:S(2)}) collective-permute-start(f32[32,512]{1,0:T(8,128)S(1)} %dynamic-slice_bitcast_fusion), channel_id=1, source_target_pairs={{0,4},{4,0},{1,5},{5,1},{2,6},{6,2},{3,7},{7,3},{8,12},{12,8},{9,1... | collective-permute-start | bytes 196616 | tf_op jit(solution)/shard_map/ppermute | solution.py:11
  6.7 10.4 %collective-permute-start.2 = (f32[34,512]{1,0:T(8,128)S(1)}, f32[34,512]{1,0:T(8,128)S(1)}, u32[]{:S(2)}, u32[]{:S(2)}) collective-permute-start(f32[34,512]{1,0:T(8,128)S(1)} %pad_maximum_fusion), channel_id=1, source_target_pairs={{0,16},{8,24},{16,0},{24,8},{1,17},{9,25},{17,1},{25,9},{2,18},{10... | collective-permute-start | bytes 208904 | tf_op jit(solution)/shard_map/ppermute | solution.py:11
  10.7 6.9 %collective-permute-start.3 = (f32[34,512]{1,0:T(8,128)S(1)}, f32[34,512]{1,0:T(8,128)S(1)}, u32[]{:S(2)}, u32[]{:S(2)}) collective-permute-start(f32[34,512]{1,0:T(8,128)S(1)} %pad_maximum_fusion), channel_id=1, source_target_pairs={{0,24},{8,16},{16,8},{24,0},{1,25},{9,17},{17,9},{25,1},{2,26},{10... | collective-permute-start | bytes 208904 | tf_op jit(solution)/shard_map/ppermute | solution.py:11
  12.1 6.3 %collective-permute-start.1 = (f32[34,512]{1,0:T(8,128)S(1)}, f32[34,512]{1,0:T(8,128)S(1)}, u32[]{:S(2)}, u32[]{:S(2)}) collective-permute-start(f32[34,512]{1,0:T(8,128)S(1)} %pad_maximum_fusion), channel_id=1, source_target_pairs={{0,8},{8,0},{16,24},{24,16},{1,9},{9,1},{17,25},{25,17},{2,10},{10... | collective-permute-start | bytes 208904 | tf_op jit(solution)/shard_map/ppermute | solution.py:11
  18.4 1.3 %collective-permute-start.4 = (f32[32,512]{1,0:T(8,128)S(1)}, f32[32,512]{1,0:T(8,128)S(1)}, u32[]{:S(2)}, u32[]{:S(2)}) collective-permute-start(f32[32,512]{1,0:T(8,128)S(1)} %slice.32), channel_id=1, source_target_pairs={{0,4},{4,0},{1,5},{5,1},{2,6},{6,2},{3,7},{7,3},{8,12},{12,8},{9,1... | collective-permute-start | bytes 196616 | tf_op jit(solution)/shard_map/ppermute | solution.py:11
  21.8 5.0 %collective-permute-start.6 = (f32[32,544]{1,0:T(8,128)S(1)}, f32[32,544]{1,0:T(8,128)S(1)}, u32[]{:S(2)}, u32[]{:S(2)}) collective-permute-start(f32[32,544]{1,0:T(8,128)S(1)} %pad_maximum_fusion.1), channel_id=1, source_target_pairs={{0,2},{1,3},{2,0},{3,1},{4,6},{5,7},{6,4},{7,5},{8,10},{9,11},{10,... | collective-permute-start | bytes 208904 | tf_op jit(solution)/shard_map/ppermute | solution.py:11
  23.5 6.1 %collective-permute-start.7 = (f32[32,544]{1,0:T(8,128)S(1)}, f32[32,544]{1,0:T(8,128)S(1)}, u32[]{:S(2)}, u32[]{:S(2)}) collective-permute-start(f32[32,544]{1,0:T(8,128)S(1)} %pad_maximum_fusion.1), channel_id=1, source_target_pairs={{0,3},{1,2},{2,1},{3,0},{4,7},{5,6},{6,5},{7,4},{8,11},{9,10},{10,... | collective-permute-start | bytes 208904 | tf_op jit(solution)/shard_map/ppermute | solution.py:11
  24.9 4.7 %collective-permute-start.5 = (f32[32,544]{1,0:T(8,128)S(1)}, f32[32,544]{1,0:T(8,128)S(1)}, u32[]{:S(2)}, u32[]{:S(2)}) collective-permute-start(f32[32,544]{1,0:T(8,128)S(1)} %pad_maximum_fusion.1), channel_id=1, source_target_pairs={{0,1},{1,0},{2,3},{3,2},{4,5},{5,4},{6,7},{7,6},{8,9},{9,8},{10,11... | collective-permute-start | bytes 208904 | tf_op jit(solution)/shard_map/ppermute | solution.py:11
  29.6 7.0 %collective-permute-start.10 = (f32[32,544]{1,0:T(8,128)S(1)}, f32[32,544]{1,0:T(8,128)S(1)}, u32[]{:S(2)}, u32[]{:S(2)}) collective-permute-start(f32[32,544]{1,0:T(8,128)S(1)} %add_add_fusion), channel_id=1, source_target_pairs={{0,24},{8,16},{16,8},{24,0},{1,25},{9,17},{17,9},{25,1},{2,26},{10... | collective-permute-start | bytes 208904 | tf_op jit(solution)/shard_map/ppermute | solution.py:11
  33.0 6.9 %collective-permute-start.9 = (f32[32,544]{1,0:T(8,128)S(1)}, f32[32,544]{1,0:T(8,128)S(1)}, u32[]{:S(2)}, u32[]{:S(2)}) collective-permute-start(f32[32,544]{1,0:T(8,128)S(1)} %add_add_fusion), channel_id=1, source_target_pairs={{0,16},{8,24},{16,0},{24,8},{1,17},{9,25},{17,1},{25,9},{2,18},{10... | collective-permute-start | bytes 208904 | tf_op jit(solution)/shard_map/ppermute | solution.py:11
  33.0 6.9 %collective-permute-start.8 = (f32[32,544]{1,0:T(8,128)S(1)}, f32[32,544]{1,0:T(8,128)S(1)}, u32[]{:S(2)}, u32[]{:S(2)}) collective-permute-start(f32[32,544]{1,0:T(8,128)S(1)} %add_add_fusion), channel_id=1, source_target_pairs={{0,8},{8,0},{16,24},{24,16},{1,9},{9,1},{17,25},{25,17},{2,10},{10... | collective-permute-start | bytes 208904 | tf_op jit(solution)/shard_map/ppermute | solution.py:11
  40.2 1.2 %collective-permute-start.11 = (f32[32,32]{1,0:T(8,128)S(1)}, f32[32,32]{1,0:T(8,128)S(1)}, u32[]{:S(2)}, u32[]{:S(2)}) collective-permute-start(f32[32,32]{1,0:T(8,128)S(1)} %fusion.12), channel_id=1, source_target_pairs={{0,4},{4,0},{1,5},{5,1},{2,6},{6,2},{3,7},{7,3},{8,12},{12,8},{9,1... | collective-permute-start | bytes 12296 | tf_op jit(solution)/shard_map/ppermute | solution.py:11
  42.7 2.4 %copy-start.4 = (f32[1024,512]{1,0:T(8,128)S(1)}, f32[1024,512]{1,0:T(8,128)}, u32[]{:S(2)}) copy-start(f32[1024,512]{1,0:T(8,128)} %param.12) | copy-start | bytes 6291460
  42.7 3.4 %copy-start.5 = (bf16[1024,512]{1,0:T(8,128)(2,1)S(1)}, bf16[1024,512]{1,0:T(8,128)(2,1)}, u32[]{:S(2)}) copy-start(bf16[1024,512]{1,0:T(8,128)(2,1)} %param.9) | copy-start | bytes 3145732
  46.1 7.4 %copy-start.8 = (f32[2,512]{1,0:T(2,128)S(1)}, f32[2,512]{1,0:T(2,128)}, u32[]{:S(2)}) copy-start(f32[2,512]{1,0:T(2,128)} %param.15) | copy-start | bytes 12292
  46.1 7.4 %copy-start.9 = (f32[2,512]{1,0:T(2,128)S(1)}, f32[2,512]{1,0:T(2,128)}, u32[]{:S(2)}) copy-start(f32[2,512]{1,0:T(2,128)} %param.16) | copy-start | bytes 12292
  51.1 32.6 %collective-permute-start.12 = (bf16[1024,512]{1,0:T(8,128)(2,1)}, bf16[1024,512]{1,0:T(8,128)(2,1)S(1)}, u32[]{:S(2)}, u32[]{:S(2)}) collective-permute-start(bf16[1024,512]{1,0:T(8,128)(2,1)} %get-tuple-element.9), channel_id=1, source_target_pairs={{0,1},{1,0},{2,3},{3,2},{4,5},{5,4},{6,7},{7,6},{8,9},{9,8},{10,11... | collective-permute-start | bytes 3145736 | tf_op jit(solution)/shard_map/ppermute | solution.py:11
  52.0 32.4 %collective-permute-start.13 = (bf16[1024,512]{1,0:T(8,128)(2,1)}, bf16[1024,512]{1,0:T(8,128)(2,1)}, u32[]{:S(2)}, u32[]{:S(2)}) collective-permute-start(bf16[1024,512]{1,0:T(8,128)(2,1)} %get-tuple-element.9), channel_id=1, source_target_pairs={{0,2},{1,3},{2,0},{3,1},{4,6},{5,7},{6,4},{7,5},{8,10},{9,11},{10,... | collective-permute-start | bytes 3145736 | tf_op jit(solution)/shard_map/ppermute | solution.py:11
  54.1 22.5 %collective-permute-start.16 = (f32[2,512]{1,0:T(2,128)S(1)}, f32[2,512]{1,0:T(2,128)S(1)}, u32[]{:S(2)}, u32[]{:S(2)}) collective-permute-start(f32[2,512]{1,0:T(2,128)S(1)} %get-tuple-element.6), channel_id=1, source_target_pairs={{0,1},{1,0},{2,3},{3,2},{4,5},{5,4},{6,7},{7,6},{8,9},{9,8},{10,11... | collective-permute-start | bytes 12296 | tf_op jit(solution)/shard_map/ppermute | solution.py:11
  55.2 22.9 %collective-permute-start.17 = (f32[2,512]{1,0:T(2,128)S(1)}, f32[2,512]{1,0:T(2,128)S(1)}, u32[]{:S(2)}, u32[]{:S(2)}) collective-permute-start(f32[2,512]{1,0:T(2,128)S(1)} %get-tuple-element.6), channel_id=1, source_target_pairs={{0,2},{1,3},{2,0},{3,1},{4,6},{5,7},{6,4},{7,5},{8,10},{9,11},{10,... | collective-permute-start | bytes 12296 | tf_op jit(solution)/shard_map/ppermute | solution.py:11
  76.6 3.6 %collective-permute-start.19 = (f32[1,512]{1,0:T(1,128)S(1)}, f32[1,512]{1,0:T(1,128)S(1)}, u32[]{:S(2)}, u32[]{:S(2)}) collective-permute-start(f32[1,512]{1,0:T(1,128)S(1)} %slice.39), channel_id=1, source_target_pairs={{0,2},{1,3},{2,0},{3,1},{4,6},{5,7},{6,4},{7,5},{8,10},{9,11},{10,... | collective-permute-start | bytes 6152 | tf_op jit(solution)/shard_map/ppermute | solution.py:11
  78.1 3.6 %collective-permute-start.18 = (f32[1,512]{1,0:T(1,128)S(1)}, f32[1,512]{1,0:T(1,128)S(1)}, u32[]{:S(2)}, u32[]{:S(2)}) collective-permute-start(f32[1,512]{1,0:T(1,128)S(1)} %slice.38), channel_id=1, source_target_pairs={{0,1},{1,0},{2,3},{3,2},{4,5},{5,4},{6,7},{7,6},{8,9},{9,8},{10,11... | collective-permute-start | bytes 6152 | tf_op jit(solution)/shard_map/ppermute | solution.py:11
  81.8 1.2 %collective-permute-start.20 = (f32[2,2048]{1,0:T(2,128)S(1)}, f32[2,2048]{1,0:T(2,128)S(1)}, u32[]{:S(2)}, u32[]{:S(2)}) collective-permute-start(f32[2,2048]{1,0:T(2,128)S(1)} %bitcast.26), channel_id=1, source_target_pairs={{0,4},{4,0},{1,5},{5,1},{2,6},{6,2},{3,7},{7,3},{8,12},{12,8},{9,1... | collective-permute-start | bytes 49160 | tf_op jit(solution)/shard_map/ppermute | solution.py:11
  81.9 4.8 %copy-start.3 = (f32[1024,512]{1,0:T(8,128)S(1)}, f32[1024,512]{1,0:T(8,128)}, u32[]{:S(2)}) copy-start(f32[1024,512]{1,0:T(8,128)} %get-tuple-element.13) | copy-start | bytes 6291460
  83.7 14.1 %collective-permute-start.15 = (bf16[512,512]{1,0:T(8,128)(2,1)S(1)}, bf16[512,512]{1,0:T(8,128)(2,1)S(1)}, u32[]{:S(2)}, u32[]{:S(2)}) collective-permute-start(bf16[512,512]{1,0:T(8,128)(2,1)S(1)} %slice.36), channel_id=1, source_target_pairs={{0,2},{1,3},{2,0},{3,1},{4,6},{5,7},{6,4},{7,5},{8,10},{9,11},{10,... | collective-permute-start | bytes 1572872 | tf_op jit(solution)/shard_map/ppermute | solution.py:11
  85.5 13.8 %collective-permute-start.14 = (bf16[512,512]{1,0:T(8,128)(2,1)S(1)}, bf16[512,512]{1,0:T(8,128)(2,1)S(1)}, u32[]{:S(2)}, u32[]{:S(2)}) collective-permute-start(bf16[512,512]{1,0:T(8,128)(2,1)S(1)} %slice.35), channel_id=1, source_target_pairs={{0,1},{1,0},{2,3},{3,2},{4,5},{5,4},{6,7},{7,6},{8,9},{9,8},{10,11... | collective-permute-start | bytes 1572872 | tf_op jit(solution)/shard_map/ppermute | solution.py:11

commit v2 on v0

v2 whole, which is shorter than its diff:
```python
import functools

import jax
import jax.numpy as jnp
from jax import lax
from jax.experimental import pallas as pl
from jax.experimental.pallas import tpu as pltpu
from jax.sharding import PartitionSpec as P

HIGHEST = lax.Precision.HIGHEST
F32 = jnp.float32
BF16 = jnp.bfloat16
KEEP = 0.05 * 0.9 * 0.9
MOVE = 0.05 * (1.0 + 0.9)
EARLY = 11
BLOCKS = 4
WHOLE = pl.BlockSpec(memory_space=pltpu.VMEM)
SCALAR = pl.BlockSpec(memory_space=pltpu.SMEM)
ANYWHERE = pl.BlockSpec(memory_space=pl.ANY)
IN_HBM = pl.BlockSpec(memory_space=pltpu.HBM)
PARAMS = pltpu.CompilerParams(vmem_limit_bytes=16 * 2**20)


def hbm(x):
    return pltpu.with_memory_space_constraint(x, pltpu.HBM)


def swap(x, axis, distance):
    count = lax.axis_size(axis)
    return lax.ppermute(x, axis, [(i, i ^ distance) for i in range(count)])


def partners(x, axis):
    count = lax.axis_size(axis)
    while count > 4:
        count //= 2
        x = x + swap(x, axis, count)
    return [x] + [swap(x, axis, distance) for distance in range(1, count)]


def added(parts):
    while len(parts) > 1:
        parts = [a + b for a, b in zip(parts[::2], parts[1::2])]
    return parts[0]


def packed(square):
    step = 8
    return jnp.concatenate([square[i : i + step] for i in range(0, square.shape[0], step)], axis=1)


def pieces(x):
    one = x.astype(BF16)
    rest = x - one.astype(F32)
    two = rest.astype(BF16)
    three = (rest - two.astype(F32)).astype(BF16)
    return one, two, three


def dot(a, b, dims):
    return lax.dot_general(a, b, ((dims[0], dims[1]), ((), ())), preferred_element_type=F32)


def folded(x):
    rank = x.shape[0] // 3
    return x[:rank] + x[rank : 2 * rank] + x[2 * rank :]


def loaded(grads_any, error_any, grads_ref, error_ref, sems):
    rows = grads_any.shape[0]
    block = rows // BLOCKS
    copies = []
    for part in range(BLOCKS):
        span = pl.ds(part * block, block)
        copies.append((grads_any.at[span], grads_ref.at[span]))
        copies.append((error_any.at[span], error_ref.at[span]))
    copies = fetch(copies, sems)

    def blocks():
        for part in range(BLOCKS):
            copies[2 * part].wait()
            copies[2 * part + 1].wait()
            span = pl.ds(part * block, block)
            yield part, grads_ref[span, :], error_ref[span, :]

    return blocks


def left_kernel(basis_ref, grads_any, error_any, gains_ref, kept_ref, given_ref, grads_ref, error_ref, sems):
    blocks = loaded(grads_any, error_any, grads_ref, error_ref, sems)
    stack = jnp.concatenate(pieces(basis_ref[...]), axis=0)
    rank = basis_ref.shape[0]
    half = grads_ref.shape[0] // 2
    kept_ref[rank:, :] = jnp.concatenate([gains_ref[...], jnp.zeros((6, half), F32)], axis=0)
    terms = []
    for _, grads, error in blocks():
        terms.append(folded(dot(stack, grads, ((1,), (1,))) + dot(stack, error, ((1,), (1,)))))
    middle = BLOCKS // 2
    front = jnp.concatenate(terms[:middle], axis=1)
    back = jnp.concatenate(terms[middle:], axis=1)
    first = lax.axis_index("tensor") == 0
    kept_ref[:rank, :] = jnp.where(first, front, back)
    given_ref[...] = jnp.where(first, back, front)


def pair_kernel(kept_ref, other_ref, out_ref):
    rank = other_ref.shape[0]
    out_ref[:rank, :] = kept_ref[:rank, :] + other_ref[...]
    out_ref[rank:, :] = kept_ref[rank:, :]


def sum_kernel(replicas, *refs):
    *parts, gain_ref, gain_momentum_ref, mine_ref, new_gain_momentum_ref, tail_ref = refs
    mean = added([part[...] for part in parts]) / replicas
    rank = mine_ref.shape[0]
    mine_ref[...] = mean[:rank]
    gain_mean = mean[rank : rank + 2]
    new_gain_momentum = 0.9 * gain_momentum_ref[...] + gain_mean
    new_gain_momentum_ref[...] = new_gain_momentum
    new_gain = gain_ref[...] - 0.02 * (gain_mean + 0.9 * new_gain_momentum)
    tail_ref[...] = jnp.concatenate([new_gain[:, i * 128 : (i + 1) * 128] for i in range(4)], axis=0)


def right_kernel(mine_ref, other_ref, root_ref, grads_ref, error_ref, term_ref, gram_ref, ortho_ref):
    rank, half = mine_ref.shape
    first = lax.axis_index("tensor") == 0
    mine = mine_ref[...]
    other = other_ref[...]
    lowp = (jnp.where(first, mine, other), jnp.where(first, other, mine))
    orthos = [
        lax.dot_general(root_ref[...], x, (((0,), (0,)), ((), ())), precision=HIGHEST, preferred_element_type=F32)
        for x in lowp
    ]
    stacks = [jnp.concatenate(pieces(x), axis=0) for x in orthos]
    for part in range(2):
        ortho_ref[pl.ds(part * rank, rank), :] = orthos[part]
    gram = sum(
        lax.dot_general(x, x, (((1,), (1,)), ((), ())), precision=HIGHEST, preferred_element_type=F32) for x in orthos
    )
    gram_ref[...] = packed(gram)
    term = jnp.zeros((3 * rank, grads_ref.shape[1]), F32)
    for part, stack in enumerate(stacks):
        span = pl.ds(part * half, half)
        term += dot(stack, grads_ref[span, :], ((1,), (0,))) + dot(stack, error_ref[span, :], ((1,), (0,)))
    term_ref[...] = folded(term)


def middle_kernel(count, *refs):
    parts, (gram_ref, tail_ref, _, _, out_ref) = refs[:count], refs[count:]
    term = added([part[...] for part in parts])
    rank, cols = term.shape
    out_ref[:rank, :] = term
    out_ref[rank:, :128] = gram_ref[...]
    out_ref[rank:, 128:256] = tail_ref[...]
    out_ref[rank:, 256:] = jnp.zeros((8, cols - 256), F32)


def factor_kernel(replicas, *refs):
    *parts, newbasis_ref, gram_ref, right_ref, wide_ref = refs
    rank, cols = newbasis_ref.shape
    values = [part[...] for part in parts]
    mean = added(values)
    newbasis = mean[:rank] / replicas
    newbasis_ref[...] = newbasis
    right = lax.dot_general(newbasis, newbasis, (((1,), (1,)), ((), ())), precision=HIGHEST, preferred_element_type=F32)
    gram_ref[...] = mean[rank:, :128]
    right_ref[...] = packed(right)
    section = lax.axis_index("section")
    for distance, value in enumerate(values):
        gain = jnp.concatenate([value[rank + 2 * i : rank + 2 * i + 2, 128:256] for i in range(4)], axis=1)
        for place in range(len(values)):

            @pl.when(section == place ^ distance)
            def _(place=place, gain=gain):
                wide_ref[:, place * cols : (place + 1) * cols] = gain


def base_of(weight, momentum):
    return weight.astype(F32) - KEEP * momentum


def fetch(copies, sems):
    started = []
    for index, (source, target) in enumerate(copies):
        copy = pltpu.make_async_copy(source, target, sems.at[index])
        copy.start()
        started.append(copy)
    return started


def start_kernel(weight_any, momentum_any, x_early_any, y_early_any, late_any, weight_ref, momentum_ref, base_ref, sems):
    rows = weight_any.shape[0]
    early = x_early_any.shape[0]
    late = rows - early
    block = rows // BLOCKS
    copies = []
    for part in range(BLOCKS):
        span = pl.ds(part * block, block)
        copies.append((weight_any.at[span], weight_ref.at[span]))
        copies.append((momentum_any.at[span], momentum_ref.at[span]))
    copies = fetch(copies, sems)
    sent = []
    for part in range(BLOCKS):
        copies[2 * part].wait()
        copies[2 * part + 1].wait()
        start, stop = part * block, (part + 1) * block
        span = pl.ds(start, block)
        base_ref[span, :] = base_of(weight_ref[span, :], momentum_ref[span, :])
        for low, high, ref, shift in (
            (0, early, y_early_any, 0),
            (late, rows, x_early_any, late),
            (0, late, late_any, 0),
            (early, rows, late_any, early - late),
        ):
            low, high = max(low, start), min(high, stop)
            if low < high:
                source = base_ref.at[pl.ds(low, high - low)]
                target = ref.at[pl.ds(low - shift, high - low)]
                sent.append(pltpu.make_async_copy(source, target, sems.at[2 * BLOCKS + len(sent)]))
                sent[-1].start()
    for copy in sent:
        copy.wait()


def left_stack(ortho):
    one, two, three = pieces(ortho)
    return jnp.concatenate([one, one, two, one, two, three], axis=0)


def right_stack(newbasis):
    one, two, three = pieces(newbasis)
    return jnp.concatenate([one, two, one, three, two, one], axis=0)


def product(ortho, right):
    return dot(left_stack(ortho), right, ((0,), (0,)))


def moved(base, scale, approx):
    return (base - (MOVE * scale) * approx).astype(BF16)


def after_kernel(entries, newbasis_ref, gram_ref, mine_ref, other_ref, own_ref, x_left_ref, y_left_ref, late_any, x_early_ref, y_early_ref, to_x_ref, to_y_ref, scale_ref, section_ref, late_ref, sems):
    (copy,) = fetch([(late_any, late_ref)], sems)
    rank = newbasis_ref.shape[0]
    early = x_early_ref.shape[0]
    late = late_ref.shape[0] // 2
    half = (early + late) // 2
    skip = half - late
    squares = (gram_ref[...] / entries) * (mine_ref[...] + other_ref[...])
    mean = jnp.sum(jnp.sum(squares, axis=1, keepdims=True), axis=0, keepdims=True)
    scale = lax.rsqrt(mean + 1e-06)
    scale_ref[...] = jnp.broadcast_to(scale, scale_ref.shape)
    section_ref[0] = lax.axis_index("section")
    right = right_stack(newbasis_ref[...])
    to_x_ref[:half, :] = moved(y_early_ref[:half, :], scale, product(y_left_ref[:rank, :], right))
    to_y_ref[:half, :] = moved(x_early_ref[early - half :, :], scale, product(x_left_ref[rank:, :], right))
    copy.wait()
    to_x_ref[half:, :] = moved(late_ref[:late, :], scale, product(own_ref[:rank, :late], right))
    to_y_ref[half:, :] = moved(late_ref[late:, :], scale, product(own_ref[rank:, skip:], right))


def own_kernel(place_ref, scale_ref, newbasis_ref, own_ref, weight_ref, momentum_ref, grads_ref, error_ref, new_error_ref, new_momentum_ref, out_ref):
    del place_ref
    rank, cols = newbasis_ref.shape
    block = weight_ref.shape[0]
    step = pl.program_id(0)
    per = cols // block
    start = (step // per) * rank
    columns = pl.ds(pl.multiple_of((step % per) * block, block), block)
    scale = scale_ref[0:1, 0:1]
    ortho = own_ref[pl.ds(pl.multiple_of(start, rank), rank), columns]
    approx = product(ortho, right_stack(newbasis_ref[...]))
    merged = grads_ref[...].astype(F32) + error_ref[...].astype(F32)
    new_error_ref[...] = (merged - approx).astype(BF16)
    momentum = momentum_ref[...]
    new_momentum_ref[...] = 0.9 * momentum + scale * approx
    out_ref[...] = moved(base_of(weight_ref[...], momentum), scale, approx)


def near_kernel(scale_ref, newbasis_ref, x_left_ref, y_left_ref, x_early_ref, y_early_ref, held_ref, out_ref, done_ref, sems):
    del held_ref
    rank = newbasis_ref.shape[0]
    early = x_early_ref.shape[0]
    half = x_left_ref.shape[1]
    extra = early - half
    rows = 2 * half
    scale = scale_ref[0:1, 0:1]
    right = right_stack(newbasis_ref[...])
    section = lax.axis_index("section")
    x_side = (section ^ 1) * rows
    y_side = (section ^ 2) * rows
    work = (
        (x_early_ref, 0, x_left_ref[:rank, half - extra :], extra, x_side + half - extra),
        (x_early_ref, extra, x_left_ref[rank:, :], half, x_side + half),
        (y_early_ref, 0, y_left_ref[:rank, :], half, y_side),
        (y_early_ref, half, y_left_ref[rank:, :extra], extra, y_side + half),
    )
    sent = []
    start = 0
    for index, (ref, begin, ortho, size, to) in enumerate(work):
        span = pl.ds(start, size)
        done_ref[span, :] = moved(ref[begin : begin + size, :], scale, product(ortho, right))
        to = pl.multiple_of(to, 64)
        copy = pltpu.make_async_copy(done_ref.at[span], out_ref.at[pl.ds(to, size)], sems.at[index])
        copy.start()
        sent.append(copy)
        start += size
    for copy in sent:
        copy.wait()


def settle_kernel(x_ref, y_ref, held_ref, out_ref, sems):
    del held_ref
    rows = out_ref.shape[0] // lax.axis_size("section")
    half = rows // 2
    late = x_ref.shape[0] - half
    section = lax.axis_index("section")
    x_side = (section ^ 1) * rows
    y_side = (section ^ 2) * rows
    across = (section ^ 3) * rows
    copies = []
    for ref, start, size, to in (
        (x_ref, 0, half, across),
        (x_ref, half, late, x_side),
        (y_ref, 0, half, across + half),
        (y_ref, half, late, y_side + rows - late),
    ):
        to = pl.multiple_of(to, 64)
        copies.append((ref.at[pl.ds(start, size), :], out_ref.at[pl.ds(to, size), :]))
    for copy in fetch(copies, sems):
        copy.wait()


def gain_kernel(wide_ref, other_ref, out_ref):
    cols = wide_ref.shape[1]
    first = lax.axis_index("tensor") == 0
    wide = wide_ref[...]
    other = other_ref[...]
    out_ref[:, :cols] = jnp.where(first, wide, other)
    out_ref[:, cols:] = jnp.where(first, other, wide)


def shape(dims, kind):
    return jax.ShapeDtypeStruct(dims, kind)


def cost(flops, size):
    return pl.CostEstimate(flops=flops, bytes_accessed=size, transcendentals=0)


def call(kernel, name, out_shape, in_specs, size, **more):
    out_specs = more.pop("out_specs", [WHOLE] * len(out_shape))
    return pl.pallas_call(
        kernel,
        out_shape=out_shape,
        in_specs=in_specs,
        out_specs=out_specs,
        compiler_params=PARAMS,
        name=name,
        cost_estimate=cost(0, size),
        **more,
    )


def on_device(weight, grads, error, momentum, basis, gram_root, gain, gain_momentum, gain_grads):
    replicas = lax.axis_size("replica")
    tensors = lax.axis_size("tensor")
    sections = lax.axis_size("section")
    rows, cols = weight.shape
    rank = basis.shape[1]
    half = rows // 2
    early = rows * EARLY // 16
    late = rows - early
    grads = hbm(grads[0])
    error = hbm(error[0])
    weight = hbm(weight)
    momentum = hbm(momentum)

    x_early, y_early, late_rows = call(
        start_kernel,
        "start",
        [pltpu.HBM((early, cols), F32)] * 2 + [pltpu.HBM((2 * late, cols), F32)],
        [IN_HBM] * 2,
        0,
        out_specs=[IN_HBM] * 3,
        scratch_shapes=[
            pltpu.VMEM((rows, cols), BF16),
            pltpu.VMEM((rows, cols), F32),
            pltpu.VMEM((rows, cols), F32),
            pltpu.SemaphoreType.DMA((6 * BLOCKS,)),
        ],
    )(weight, momentum)
    from_x = swap(x_early, "section", 1)
    from_y = swap(y_early, "section", 2)

    kept, given, held_grads, held_error = call(
        left_kernel,
        "left",
        [shape((rank + 8, half), F32), shape((rank, half), F32)] + [pltpu.VMEM((rows, cols), BF16)] * 2,
        [WHOLE, IN_HBM, IN_HBM, WHOLE],
        0,
        scratch_shapes=[pltpu.SemaphoreType.DMA((2 * BLOCKS,))],
    )(basis.T, grads, error, gain_grads[0])
    (pair,) = call(pair_kernel, "pair", [shape(kept.shape, F32)], [WHOLE] * 2, 0)(kept, swap(given, "tensor", 1))
    parts = partners(pair, "replica")
    mine, new_gain_momentum, tail = call(
        functools.partial(sum_kernel, replicas),
        "sum",
        [shape((rank, half), F32), shape((2, cols), F32), shape((8, 128), F32)],
        [WHOLE] * (len(parts) + 2),
        0,
    )(*parts, gain, gain_momentum)

    term, gram, ortho = call(
        right_kernel,
        "right",
        [shape((rank, cols), F32), shape((8, 128), F32), shape((2 * rank, half), F32)],
        [WHOLE] * 5,
        0,
    )(mine, swap(mine, "tensor", 1), gram_root, held_grads, held_error)
    parts = partners(term, "replica")
    (joined,) = call(
        functools.partial(middle_kernel, len(parts)),
        "middle",
        [shape((rank + 8, cols), F32)],
        [WHOLE] * (len(parts) + 2) + [ANYWHERE] * 2,
        0,
    )(*parts, gram, tail, from_x, from_y)
    parts = partners(joined, "section")
    x_left = swap(ortho, "section", 1)
    y_left = swap(ortho, "section", 2)
    newbasis, grams, right, wide = call(
        functools.partial(factor_kernel, replicas),
        "factor",
        [shape((rank, cols), F32), shape((8, 128), F32), shape((8, 128), F32), shape((2, sections * cols), F32)],
        [WHOLE] * len(parts),
        0,
    )(*parts)

    entries = rows * cols * tensors * sections
    to_x, to_y, scale, where = call(
        functools.partial(after_kernel, entries),
        "after",
        [shape((half + late, cols), BF16)] * 2 + [shape((8, 128), F32), shape((1,), jnp.int32)],
        [WHOLE] * 7 + [IN_HBM] + [WHOLE] * 2,
        0,
        out_specs=[WHOLE] * 3 + [SCALAR],
        scratch_shapes=[pltpu.VMEM((2 * late, cols), F32), pltpu.SemaphoreType.DMA((1,))],
    )(newbasis, grams, right, swap(right, "tensor", 1), ortho, x_left, y_left, hbm(late_rows), from_x, from_y)
    late_x = swap(to_x, "section", 1)
    late_y = swap(to_y, "section", 2)

    blocks = 4
    block = rows // blocks
    fixed = pl.BlockSpec((rank, cols), lambda i, place: (0, 0))
    step = pl.BlockSpec((block, cols), lambda i, place: (i, 0))
    new_error, new_momentum, out = pl.pallas_call(
        own_kernel,
        out_shape=[pltpu.HBM((rows, cols), BF16), pltpu.HBM((rows, cols), F32), pltpu.HBM((sections * rows, cols), BF16)],
        grid_spec=pltpu.PrefetchScalarGridSpec(
            num_scalar_prefetch=1,
            grid=(blocks,),
            in_specs=[
                pl.BlockSpec((8, 128), lambda i, place: (0, 0)),
                fixed,
                pl.BlockSpec(ortho.shape, lambda i, place: (0, 0)),
                step,
                step,
                step,
                step,
            ],
            out_specs=[step, step, pl.BlockSpec((block, cols), lambda i, place: (place[0] * blocks + i, 0))],
        ),
        compiler_params=PARAMS,
        name="own",
        cost_estimate=cost(12 * rows * cols * rank, 16 * rows * cols),
    )(where, scale, newbasis, ortho, weight, momentum, grads, error)

    (out,) = call(
        near_kernel,
        "near",
        [pltpu.HBM(out.shape, BF16)],
        [WHOLE] * 6 + [IN_HBM],
        12 * early * cols,
        out_specs=[IN_HBM],
        scratch_shapes=[pltpu.VMEM((2 * early, cols), BF16), pltpu.SemaphoreType.DMA((4,))],
        input_output_aliases={6: 0},
    )(scale, newbasis, x_left, y_left, from_x, from_y, hbm(out))
    (new_weight,) = call(
        settle_kernel,
        "settle",
        [pltpu.HBM(out.shape, BF16)],
        [WHOLE] * 2 + [IN_HBM],
        0,
        out_specs=[IN_HBM],
        scratch_shapes=[pltpu.SemaphoreType.DMA((4,))],
        input_output_aliases={2: 0},
    )(late_x, late_y, hbm(out))
    (new_gain,) = call(gain_kernel, "gain", [shape((2, 2 * sections * cols), F32)], [WHOLE] * 2, 0)(
        wide, swap(wide, "tensor", 1)
    )
    return (new_weight, new_error[None], new_momentum, new_gain, new_gain_momentum)


def solution(mesh):
    placed = (
        P("section", "tensor"),
        P("replica", "section", "tensor"),
        P("replica", "section", "tensor"),
        P("section", "tensor"),
        P("tensor", None),
        P(),
        P(None, ("tensor", "section")),
        P(None, ("tensor", "section")),
        P("replica", None, ("tensor", "section")),
    )
    return jax.shard_map(
        on_device,
        mesh=mesh,
        in_specs=placed,
        out_specs=(
            P(None, "tensor"),
            P("replica", "section", "tensor"),
            P("section", "tensor"),
            P(),
            P(None, ("tensor", "section")),
        ),
        check_vma=False,
    )
```

time: 274 us -> 76.8 us (0.28)
  waiting for transfers between devices: 183 us -> 35.8 us
  blocking collectives: 49.7 us -> 0 us
  starting transfers between devices: 0.12 us -> 20.2 us
  Pallas kernels: 0 us -> 19.6 us
  matrix products: 14.8 us -> 0 us
  between operations: 14.5 us -> 0.78 us
  local copies, waits for them, and re-layouts: 5.88 us -> 0.02 us
  other arithmetic: 5.48 us -> 0 us
    psum x2 -> x0, waiting for transfers between devices: 165 us -> none  [the longest x1 106 us: on_device(): newbasis = lax.psum(basis_term, ('replica', 'section')) / replicas]
    ppermute x0 -> x19, waiting for transfers between devices: none -> 35.8 us  [swap(): return lax.ppermute(x, axis, [(i, i ^ distance) for i in range(count)])]
    psum x2 -> x0, blocking collectives: 25.5 us -> none  [the longest x1 14.8 us: on_device(): square_sum = lax.psum(jnp.sum(approx * approx), ('tensor', 'section'))]
    all_gather x1 -> x0, blocking collectives: 24.1 us -> none  [on_device(): lax.all_gather(local_gain, ('tensor', 'section'), axis=1, tiled=True)]
    ppermute x0 -> x19, starting transfers between devices: none -> 20.2 us  [swap(): return lax.ppermute(x, axis, [(i, i ^ distance) for i in range(count)])]
    pallas_call x0 -> x12, Pallas kernels: none -> 19.6 us  [the longest x1 6.1 us: on_device(): pl.pallas_call(own_kernel, out_shape=[pltpu.HBM((rows, cols), BF16), pltp...]
    all_gather x1 -> x0, waiting for transfers between devices: 17.5 us -> none  [on_device(): new_weight = lax.all_gather(local_weight, 'section', axis=0, tiled=True)]
    dot_general x4 -> x0, matrix products: 14.8 us -> none  [the longest x1 4.81 us: on_device(): approx = jnp.dot(ortho, newbasis.T, precision=highest)]
  transfers between devices with their start and end apart: 3 -> 19, of which waited for: 3 -> 13; matrix products, arithmetic and copies ran while one was open for 0% -> 0% of each run, Pallas kernels for 0% -> 17%
where the time goes in v2:
time: 76.8 us; the launch traced here: 76.5 us
  waiting for transfers between devices  35.8 us (47%)
  starting transfers between devices  20.2 us (26%)
  Pallas kernels  19.6 us (26%)
  between operations  0.78 us (1%)
    ppermute x19, waiting for transfers between devices, swap(): return lax.ppermute(x, axis, [(i, i ^ distance) for i in range(count)])  35.8 us
    ppermute x19, starting transfers between devices, swap(): return lax.ppermute(x, axis, [(i, i ^ distance) for i in range(count)])  20.2 us
    pallas_call x1, Pallas kernels, on_device(): pl.pallas_call(own_kernel, out_shape=[pltpu.HBM((rows, cols), BF16), pltp...  6.1 us
    pallas_call x1, Pallas kernels, on_device(): call(start_kernel, 'start', [pltpu.HBM((early, cols), F32)] * 2 + [pltpu....  3.46 us
    pallas_call x1, Pallas kernels, on_device(): call(left_kernel, 'left', [shape((rank + 8, half), F32), shape((rank, hal...  2.82 us
    pallas_call x1, Pallas kernels, on_device(): call(functools.partial(after_kernel, entries), 'after', [shape((half + la...  2.1 us
  transfers between devices with their start and end apart: 19, of which 13 were waited for; matrix products, arithmetic and copies ran while one was open for 0% of the time, Pallas kernels for 17%

profile of v2, /device:TPU:0, one launch (start us, length us, event | category | flops | bytes accessed | tf_op | source)
XLA Modules:
  0.0 76.5 jit_solution(13715477465603560422)
XLA Ops:
  0.6 0.0 copy-start
  0.6 0.0 copy-start.2
  0.7 0.0 copy-start.3
  0.7 0.0 copy-start.4
  0.7 3.5 %start.1 = (f32[704,512]{1,0:T(8,128)}, f32[704,512]{1,0:T(8,128)}, f32[640,512]{1,0:T(8,128)}) custom-call(bf16[1024,512]{1,0:T(8,128)(2,1)} %weight_ref.1, f32[1024,512]{1,0:T(8,128)} %momentum_ref.1), custom_call_target="tpu_custom_call" | custom-call | tf_op jit(solution)/shard_map/start/pallas_call | solution.py:380
  4.1 0.0 copy-start.1
  4.2 3.0 %collective-permute-start.8 = (f32[704,512]{1,0:T(8,128)}, f32[704,512]{1,0:T(8,128)S(1)}, u32[]{:S(2)}, u32[]{:S(2)}) collective-permute-start(f32[704,512]{1,0:T(8,128)} %get-tuple-element.37), channel_id=1, source_target_pairs={{0,1},{1,0},{2,3},{3,2},{4,5},{5,4},{6,7},{7,6},{8,9},{9,8},{10,11... | collective-permute-start | bytes 4325384 | tf_op jit(solution)/shard_map/ppermute | solution.py:30
  7.2 1.5 %collective-permute-start.9 = (f32[704,512]{1,0:T(8,128)}, f32[704,512]{1,0:T(8,128)S(1)}, u32[]{:S(2)}, u32[]{:S(2)}) collective-permute-start(f32[704,512]{1,0:T(8,128)} %get-tuple-element.38), channel_id=1, source_target_pairs={{0,2},{1,3},{2,0},{3,1},{4,6},{5,7},{6,4},{7,5},{8,10},{9,11},{10,... | collective-permute-start | bytes 4325384 | tf_op jit(solution)/shard_map/ppermute | solution.py:30
  8.7 0.0 copy-done
  8.7 0.0 copy-done.2
  8.7 2.8 %left.1 = (f32[40,512]{1,0:T(8,128)S(1)}, f32[32,512]{1,0:T(8,128)S(1)}, bf16[1024,512]{1,0:T(8,128)(2,1)S(1)}, bf16[1024,512]{1,0:T(8,128)(2,1)S(1)}) custom-call(f32[32,512]{1,0:T(8,128)S(1)} %bitcast.5, bf16[1024,512]{1,0:T(8,128)(2,1)} %bitcast.7, bf16[1024,512]{1,0:T(8,128)(2,1)} %bitcast.9, f32[2,512]{1,0:T(2,128)S(1)} %bitcast.6), custom_call_target="tpu_custom_call" | custom-call | tf_op jit(solution)/shard_map/left/pallas_call | solution.py:397
  11.5 0.1 collective-permute-start
  11.6 1.2 %collective-permute-done.other_ref = f32[32,512]{1,0:T(8,128)S(1)} collective-permute-done((f32[32,512]{1,0:T(8,128)S(1)}, f32[32,512]{1,0:T(8,128)S(1)}, u32[]{:S(2)}, u32[]{:S(2)}) %collective-permute-start) | collective-permute-done | bytes 65568 | tf_op jit(solution)/shard_map/ppermute | solution.py:30
  12.8 1.6 %collective-permute-start.1 = (f32[40,512]{1,0:T(8,128)S(1)}, f32[40,512]{1,0:T(8,128)S(1)}, u32[]{:S(2)}, u32[]{:S(2)}) collective-permute-start(f32[40,512]{1,0:T(8,128)S(1)} %pair.1.refs_0_), channel_id=1, source_target_pairs={{0,8},{8,0},{16,24},{24,16},{1,9},{9,1},{17,25},{25,17},{2,10},{10... | collective-permute-start | bytes 245768 | tf_op jit(solution)/shard_map/ppermute | solution.py:30
  14.5 2.6 %collective-permute-start.2 = (f32[40,512]{1,0:T(8,128)S(1)}, f32[40,512]{1,0:T(8,128)S(1)}, u32[]{:S(2)}, u32[]{:S(2)}) collective-permute-start(f32[40,512]{1,0:T(8,128)S(1)} %pair.1.refs_0_), channel_id=1, source_target_pairs={{0,16},{8,24},{16,0},{24,8},{1,17},{9,25},{17,1},{25,9},{2,18},{10... | collective-permute-start | bytes 245768 | tf_op jit(solution)/shard_map/ppermute | solution.py:30
  17.1 0.2 collective-permute-start.3
  17.3 0.1 collective-permute-done.1.refs_1_
  17.4 6.5 %collective-permute-done.2.refs_2_ = f32[40,512]{1,0:T(8,128)S(1)} collective-permute-done((f32[40,512]{1,0:T(8,128)S(1)}, f32[40,512]{1,0:T(8,128)S(1)}, u32[]{:S(2)}, u32[]{:S(2)}) %collective-permute-start.2) | collective-permute-done | bytes 81952 | tf_op jit(solution)/shard_map/ppermute | solution.py:30
  24.0 0.0 collective-permute-done.3.refs_3_
  24.0 0.0 copy-done.3
  24.0 0.0 copy-done.4
  24.0 0.6 sum.1
  24.6 0.0 collective-permute-start.4
  24.6 1.3 %collective-permute-done.4.other_ref = f32[32,512]{1,0:T(8,128)S(1)} collective-permute-done((f32[32,512]{1,0:T(8,128)S(1)}, f32[32,512]{1,0:T(8,128)S(1)}, u32[]{:S(2)}, u32[]{:S(2)}) %collective-permute-start.4) | collective-permute-done | bytes 65568 | tf_op jit(solution)/shard_map/ppermute | solution.py:30
  25.8 0.0 copy-done.1
  25.8 0.8 %right.1 = (f32[32,512]{1,0:T(8,128)S(1)}, f32[8,128]{1,0:T(8,128)S(1)}, f32[64,512]{1,0:T(8,128)S(1)}) custom-call(f32[32,512]{1,0:T(8,128)S(1)} %get-tuple-element.31.mine_ref, f32[32,512]{1,0:T(8,128)S(1)} %collective-permute-done.4.other_ref, f32[32,32]{1,0:T(8,128)S(1)} %copy-done.1, bf16[1024,512]{1,0:T(8,128)(2,1)S(1)} %get-tuple-element.32.grads_ref, ...), custom_call_target="tpu_custom_call" | custom-call | tf_op jit(solution)/shard_map/right/pallas_call | solution.py:415
  26.7 1.6 %collective-permute-start.5 = (f32[32,512]{1,0:T(8,128)S(1)}, f32[32,512]{1,0:T(8,128)S(1)}, u32[]{:S(2)}, u32[]{:S(2)}) collective-permute-start(f32[32,512]{1,0:T(8,128)S(1)} %get-tuple-element.34.refs_0_), channel_id=1, source_target_pairs={{0,8},{8,0},{16,24},{24,16},{1,9},{9,1},{17,25},{25,17},{2,10},{10... | collective-permute-start | bytes 196616 | tf_op jit(solution)/shard_map/ppermute | solution.py:30
  28.3 1.5 %collective-permute-start.6 = (f32[32,512]{1,0:T(8,128)S(1)}, f32[32,512]{1,0:T(8,128)S(1)}, u32[]{:S(2)}, u32[]{:S(2)}) collective-permute-start(f32[32,512]{1,0:T(8,128)S(1)} %get-tuple-element.34.refs_0_), channel_id=1, source_target_pairs={{0,16},{8,24},{16,0},{24,8},{1,17},{9,25},{17,1},{25,9},{2,18},{10... | collective-permute-start | bytes 196616 | tf_op jit(solution)/shard_map/ppermute | solution.py:30
  29.8 1.3 %collective-permute-start.7 = (f32[32,512]{1,0:T(8,128)S(1)}, f32[32,512]{1,0:T(8,128)S(1)}, u32[]{:S(2)}, u32[]{:S(2)}) collective-permute-start(f32[32,512]{1,0:T(8,128)S(1)} %get-tuple-element.34.refs_0_), channel_id=1, source_target_pairs={{0,24},{8,16},{16,8},{24,0},{1,25},{9,17},{17,9},{25,1},{2,26},{10... | collective-permute-start | bytes 196616 | tf_op jit(solution)/shard_map/ppermute | solution.py:30
  31.1 0.0 collective-permute-done.5.refs_1_
  31.1 0.5 collective-permute-start.14
  31.7 4.9 %collective-permute-done.6.refs_2_ = f32[32,512]{1,0:T(8,128)S(1)} collective-permute-done((f32[32,512]{1,0:T(8,128)S(1)}, f32[32,512]{1,0:T(8,128)S(1)}, u32[]{:S(2)}, u32[]{:S(2)}) %collective-permute-start.6) | collective-permute-done | bytes 65568 | tf_op jit(solution)/shard_map/ppermute | solution.py:30
  36.5 0.5 collective-permute-start.15
  37.0 0.0 collective-permute-done.7.refs_3_
  37.0 2.8 %collective-permute-done.8.refs_6_.x_early_ref = f32[704,512]{1,0:T(8,128)S(1)} collective-permute-done((f32[704,512]{1,0:T(8,128)}, f32[704,512]{1,0:T(8,128)S(1)}, u32[]{:S(2)}, u32[]{:S(2)}) %collective-permute-start.8) | collective-permute-done | bytes 1441824 | tf_op jit(solution)/shard_map/ppermute | solution.py:30
  39.8 2.0 %collective-permute-done.9.refs_7_.y_early_ref = f32[704,512]{1,0:T(8,128)S(1)} collective-permute-done((f32[704,512]{1,0:T(8,128)}, f32[704,512]{1,0:T(8,128)S(1)}, u32[]{:S(2)}, u32[]{:S(2)}) %collective-permute-start.9) | collective-permute-done | bytes 1441824 | tf_op jit(solution)/shard_map/ppermute | solution.py:30
  41.8 0.2 collective-permute-start.10
  42.0 2.0 %collective-permute-start.11 = (f32[40,512]{1,0:T(8,128)S(1)}, f32[40,512]{1,0:T(8,128)S(1)}, u32[]{:S(2)}, u32[]{:S(2)}) collective-permute-start(f32[40,512]{1,0:T(8,128)S(1)} %middle.1.refs_0_), channel_id=1, source_target_pairs={{0,2},{1,3},{2,0},{3,1},{4,6},{5,7},{6,4},{7,5},{8,10},{9,11},{10,... | collective-permute-start | bytes 245768 | tf_op jit(solution)/shard_map/ppermute | solution.py:30
  44.0 1.4 %collective-permute-start.12 = (f32[40,512]{1,0:T(8,128)S(1)}, f32[40,512]{1,0:T(8,128)S(1)}, u32[]{:S(2)}, u32[]{:S(2)}) collective-permute-start(f32[40,512]{1,0:T(8,128)S(1)} %middle.1.refs_0_), channel_id=1, source_target_pairs={{0,3},{1,2},{2,1},{3,0},{4,7},{5,6},{6,5},{7,4},{8,11},{9,10},{10,... | collective-permute-start | bytes 245768 | tf_op jit(solution)/shard_map/ppermute | solution.py:30
  45.4 1.0 %collective-permute-done.10.refs_1_ = f32[40,512]{1,0:T(8,128)S(1)} collective-permute-done((f32[40,512]{1,0:T(8,128)S(1)}, f32[40,512]{1,0:T(8,128)S(1)}, u32[]{:S(2)}, u32[]{:S(2)}) %collective-permute-start.10) | collective-permute-done | bytes 81952 | tf_op jit(solution)/shard_map/ppermute | solution.py:30
  46.3 0.1 collective-permute-done.11.refs_2_
  46.4 2.9 %collective-permute-done.12.refs_3_ = f32[40,512]{1,0:T(8,128)S(1)} collective-permute-done((f32[40,512]{1,0:T(8,128)S(1)}, f32[40,512]{1,0:T(8,128)S(1)}, u32[]{:S(2)}, u32[]{:S(2)}) %collective-permute-start.12) | collective-permute-done | bytes 81952 | tf_op jit(solution)/shard_map/ppermute | solution.py:30
  49.3 0.3 factor.1
  49.6 0.1 collective-permute-start.13
  49.7 0.0 collective-permute-done.14.x_left_ref
  49.7 0.0 collective-permute-done.15.y_left_ref
  49.7 1.1 %collective-permute-done.13.other_ref = f32[8,128]{1,0:T(8,128)S(1)} collective-permute-done((f32[8,128]{1,0:T(8,128)S(1)}, f32[8,128]{1,0:T(8,128)S(1)}, u32[]{:S(2)}, u32[]{:S(2)}) %collective-permute-start.13) | collective-permute-done | bytes 4128 | tf_op jit(solution)/shard_map/ppermute | solution.py:30
  50.8 2.1 %after.1 = (bf16[832,512]{1,0:T(8,128)(2,1)S(1)}, bf16[832,512]{1,0:T(8,128)(2,1)S(1)}, f32[8,128]{1,0:T(8,128)S(1)}, s32[1]{0:T(128)}) custom-call(f32[32,512]{1,0:T(8,128)S(1)} %get-tuple-element.39.newbasis_ref, f32[8,128]{1,0:T(8,128)S(1)} %get-tuple-element.40.gram_ref, f32[8,128]{1,0:T(8,128)S(1)} %get-tuple-element.41.mine_ref, ...), custom_call_target="tpu_custom_call" | custom-call | tf_op jit(solution)/shard_map/after/pallas_call | solution.py:442
  53.0 1.6 %collective-permute-start.16 = (bf16[832,512]{1,0:T(8,128)(2,1)S(1)}, bf16[832,512]{1,0:T(8,128)(2,1)S(1)}, u32[]{:S(2)}, u32[]{:S(2)}) collective-permute-start(bf16[832,512]{1,0:T(8,128)(2,1)S(1)} %get-tuple-element.44), channel_id=1, source_target_pairs={{0,1},{1,0},{2,3},{3,2},{4,5},{5,4},{6,7},{7,6},{8,9},{9,8},{10,11... | collective-permute-start | bytes 2555912 | tf_op jit(solution)/shard_map/ppermute | solution.py:30
  54.5 0.5 collective-permute-start.17
  55.0 0.0 collective-permute-start.18
  55.0 6.1 %own.1 = (bf16[1024,512]{1,0:T(8,128)(2,1)}, f32[1024,512]{1,0:T(8,128)}, bf16[4096,512]{1,0:T(8,128)(2,1)}) custom-call(s32[1]{0:T(128)} %get-tuple-element.47.place_ref, f32[8,128]{1,0:T(8,128)S(1)} %get-tuple-element.46.scale_ref, f32[32,512]{1,0:T(8,128)S(1)} %get-tuple-element.39.newbasis_ref, f32[64,512]{1,0:T(8,128)S(1)} %get-tuple-element.42.own_ref, ...), custom_call_target="tpu_custom_call" | custom-call | flops 201326592 | bytes 8388608 | tf_op jit(solution)/shard_map/own/pallas_call | solution.py:458
  61.1 1.5 %near.1.held_ref = bf16[4096,512]{1,0:T(8,128)(2,1)} custom-call(f32[8,128]{1,0:T(8,128)S(1)} %get-tuple-element.46.scale_ref, f32[32,512]{1,0:T(8,128)S(1)} %get-tuple-element.39.newbasis_ref, f32[64,512]{1,0:T(8,128)S(1)} %collective-permute-done.14.x_left_ref, f32[64,512]{1,0:T(8,128)S(1)} %collective-permute-done.15.y_left_ref, ...), custom_call_target="tpu_custom_call", output_to_operand_aliasing={{}: (6, {})} | custom-call | bytes 4325376 | tf_op jit(solution)/shard_map/near/pallas_call | solution.py:480
  62.7 0.0 collective-permute-done.18.other_ref
  62.7 0.6 gain.1
  63.3 10.7 %collective-permute-done.16.x_ref = bf16[832,512]{1,0:T(8,128)(2,1)S(1)} collective-permute-done((bf16[832,512]{1,0:T(8,128)(2,1)S(1)}, bf16[832,512]{1,0:T(8,128)(2,1)S(1)}, u32[]{:S(2)}, u32[]{:S(2)}) %collective-permute-start.16) | collective-permute-done | bytes 852000 | tf_op jit(solution)/shard_map/ppermute | solution.py:30
  74.0 1.2 %collective-permute-done.17.y_ref = bf16[832,512]{1,0:T(8,128)(2,1)S(1)} collective-permute-done((bf16[832,512]{1,0:T(8,128)(2,1)S(1)}, bf16[832,512]{1,0:T(8,128)(2,1)S(1)}, u32[]{:S(2)}, u32[]{:S(2)}) %collective-permute-start.17) | collective-permute-done | bytes 852000 | tf_op jit(solution)/shard_map/ppermute | solution.py:30
  75.3 1.2 %settle.1 = bf16[4096,512]{1,0:T(8,128)(2,1)} custom-call(bf16[832,512]{1,0:T(8,128)(2,1)S(1)} %collective-permute-done.16.x_ref, bf16[832,512]{1,0:T(8,128)(2,1)S(1)} %collective-permute-done.17.y_ref, bf16[4096,512]{1,0:T(8,128)(2,1)} %near.1.held_ref), custom_call_target="tpu_custom_call", output_to_operand_aliasing={{}: (2, {})} | custom-call | tf_op jit(solution)/shard_map/settle/pallas_call | solution.py:490
  (2 shorter events, 0.0 us)
Async XLA Ops:
  0.6 8.0 %copy-start = (f32[512,32]{0,1:T(8,128)S(1)}, f32[512,32]{0,1:T(8,128)}, u32[]{:S(2)}) copy-start(f32[512,32]{0,1:T(8,128)} %param.13) | copy-start | bytes 196612
  0.6 8.0 %copy-start.2 = (f32[1,2,512]{2,1,0:T(2,128)S(1)}, f32[1,2,512]{2,1,0:T(2,128)}, u32[]{:S(2)}) copy-start(f32[1,2,512]{2,1,0:T(2,128)} %param.17) | copy-start | bytes 12292
  0.7 23.3 %copy-start.3 = (f32[2,512]{1,0:T(2,128)S(1)}, f32[2,512]{1,0:T(2,128)}, u32[]{:S(2)}) copy-start(f32[2,512]{1,0:T(2,128)} %refs_4_.1) | copy-start | bytes 12292
  0.7 23.3 %copy-start.4 = (f32[2,512]{1,0:T(2,128)S(1)}, f32[2,512]{1,0:T(2,128)}, u32[]{:S(2)}) copy-start(f32[2,512]{1,0:T(2,128)} %refs_5_.1) | copy-start | bytes 12292
  4.1 21.7 %copy-start.1 = (f32[32,32]{1,0:T(8,128)S(1)}, f32[32,32]{1,0:T(8,128)}, u32[]{:S(2)}) copy-start(f32[32,32]{1,0:T(8,128)} %root_ref.1) | copy-start | bytes 12292
  4.2 35.6 %collective-permute-start.8 = (f32[704,512]{1,0:T(8,128)}, f32[704,512]{1,0:T(8,128)S(1)}, u32[]{:S(2)}, u32[]{:S(2)}) collective-permute-start(f32[704,512]{1,0:T(8,128)} %get-tuple-element.37), channel_id=1, source_target_pairs={{0,1},{1,0},{2,3},{3,2},{4,5},{5,4},{6,7},{7,6},{8,9},{9,8},{10,11... | collective-permute-start | bytes 4325384 | tf_op jit(solution)/shard_map/ppermute | solution.py:30
  7.2 34.7 %collective-permute-start.9 = (f32[704,512]{1,0:T(8,128)}, f32[704,512]{1,0:T(8,128)S(1)}, u32[]{:S(2)}, u32[]{:S(2)}) collective-permute-start(f32[704,512]{1,0:T(8,128)} %get-tuple-element.38), channel_id=1, source_target_pairs={{0,2},{1,3},{2,0},{3,1},{4,6},{5,7},{6,4},{7,5},{8,10},{9,11},{10,... | collective-permute-start | bytes 4325384 | tf_op jit(solution)/shard_map/ppermute | solution.py:30
  11.5 1.3 %collective-permute-start = (f32[32,512]{1,0:T(8,128)S(1)}, f32[32,512]{1,0:T(8,128)S(1)}, u32[]{:S(2)}, u32[]{:S(2)}) collective-permute-start(f32[32,512]{1,0:T(8,128)S(1)} %get-tuple-element.30), channel_id=1, source_target_pairs={{0,4},{4,0},{1,5},{5,1},{2,6},{6,2},{3,7},{7,3},{8,12},{12,8},{9,1... | collective-permute-start | bytes 196616 | tf_op jit(solution)/shard_map/ppermute | solution.py:30
  12.8 4.6 %collective-permute-start.1 = (f32[40,512]{1,0:T(8,128)S(1)}, f32[40,512]{1,0:T(8,128)S(1)}, u32[]{:S(2)}, u32[]{:S(2)}) collective-permute-start(f32[40,512]{1,0:T(8,128)S(1)} %pair.1.refs_0_), channel_id=1, source_target_pairs={{0,8},{8,0},{16,24},{24,16},{1,9},{9,1},{17,25},{25,17},{2,10},{10... | collective-permute-start | bytes 245768 | tf_op jit(solution)/shard_map/ppermute | solution.py:30
  14.5 9.5 %collective-permute-start.2 = (f32[40,512]{1,0:T(8,128)S(1)}, f32[40,512]{1,0:T(8,128)S(1)}, u32[]{:S(2)}, u32[]{:S(2)}) collective-permute-start(f32[40,512]{1,0:T(8,128)S(1)} %pair.1.refs_0_), channel_id=1, source_target_pairs={{0,16},{8,24},{16,0},{24,8},{1,17},{9,25},{17,1},{25,9},{2,18},{10... | collective-permute-start | bytes 245768 | tf_op jit(solution)/shard_map/ppermute | solution.py:30
  17.1 6.9 %collective-permute-start.3 = (f32[40,512]{1,0:T(8,128)S(1)}, f32[40,512]{1,0:T(8,128)S(1)}, u32[]{:S(2)}, u32[]{:S(2)}) collective-permute-start(f32[40,512]{1,0:T(8,128)S(1)} %pair.1.refs_0_), channel_id=1, source_target_pairs={{0,24},{8,16},{16,8},{24,0},{1,25},{9,17},{17,9},{25,1},{2,26},{10... | collective-permute-start | bytes 245768 | tf_op jit(solution)/shard_map/ppermute | solution.py:30
  24.6 1.3 %collective-permute-start.4 = (f32[32,512]{1,0:T(8,128)S(1)}, f32[32,512]{1,0:T(8,128)S(1)}, u32[]{:S(2)}, u32[]{:S(2)}) collective-permute-start(f32[32,512]{1,0:T(8,128)S(1)} %get-tuple-element.31.mine_ref), channel_id=1, source_target_pairs={{0,4},{4,0},{1,5},{5,1},{2,6},{6,2},{3,7},{7,3},{8,12},{12,8},{9,1... | collective-permute-start | bytes 196616 | tf_op jit(solution)/shard_map/ppermute | solution.py:30
  26.7 4.5 %collective-permute-start.5 = (f32[32,512]{1,0:T(8,128)S(1)}, f32[32,512]{1,0:T(8,128)S(1)}, u32[]{:S(2)}, u32[]{:S(2)}) collective-permute-start(f32[32,512]{1,0:T(8,128)S(1)} %get-tuple-element.34.refs_0_), channel_id=1, source_target_pairs={{0,8},{8,0},{16,24},{24,16},{1,9},{9,1},{17,25},{25,17},{2,10},{10... | collective-permute-start | bytes 196616 | tf_op jit(solution)/shard_map/ppermute | solution.py:30
  28.3 8.2 %collective-permute-start.6 = (f32[32,512]{1,0:T(8,128)S(1)}, f32[32,512]{1,0:T(8,128)S(1)}, u32[]{:S(2)}, u32[]{:S(2)}) collective-permute-start(f32[32,512]{1,0:T(8,128)S(1)} %get-tuple-element.34.refs_0_), channel_id=1, source_target_pairs={{0,16},{8,24},{16,0},{24,8},{1,17},{9,25},{17,1},{25,9},{2,18},{10... | collective-permute-start | bytes 196616 | tf_op jit(solution)/shard_map/ppermute | solution.py:30
  29.8 7.2 %collective-permute-start.7 = (f32[32,512]{1,0:T(8,128)S(1)}, f32[32,512]{1,0:T(8,128)S(1)}, u32[]{:S(2)}, u32[]{:S(2)}) collective-permute-start(f32[32,512]{1,0:T(8,128)S(1)} %get-tuple-element.34.refs_0_), channel_id=1, source_target_pairs={{0,24},{8,16},{16,8},{24,0},{1,25},{9,17},{17,9},{25,1},{2,26},{10... | collective-permute-start | bytes 196616 | tf_op jit(solution)/shard_map/ppermute | solution.py:30
  31.1 18.6 %collective-permute-start.14 = (f32[64,512]{1,0:T(8,128)S(1)}, f32[64,512]{1,0:T(8,128)S(1)}, u32[]{:S(2)}, u32[]{:S(2)}) collective-permute-start(f32[64,512]{1,0:T(8,128)S(1)} %get-tuple-element.42.own_ref), channel_id=1, source_target_pairs={{0,1},{1,0},{2,3},{3,2},{4,5},{5,4},{6,7},{7,6},{8,9},{9,8},{10,11... | collective-permute-start | bytes 393224 | tf_op jit(solution)/shard_map/ppermute | solution.py:30
  36.5 13.2 %collective-permute-start.15 = (f32[64,512]{1,0:T(8,128)S(1)}, f32[64,512]{1,0:T(8,128)S(1)}, u32[]{:S(2)}, u32[]{:S(2)}) collective-permute-start(f32[64,512]{1,0:T(8,128)S(1)} %get-tuple-element.42.own_ref), channel_id=1, source_target_pairs={{0,2},{1,3},{2,0},{3,1},{4,6},{5,7},{6,4},{7,5},{8,10},{9,11},{10,... | collective-permute-start | bytes 393224 | tf_op jit(solution)/shard_map/ppermute | solution.py:30
  41.8 4.5 %collective-permute-start.10 = (f32[40,512]{1,0:T(8,128)S(1)}, f32[40,512]{1,0:T(8,128)S(1)}, u32[]{:S(2)}, u32[]{:S(2)}) collective-permute-start(f32[40,512]{1,0:T(8,128)S(1)} %middle.1.refs_0_), channel_id=1, source_target_pairs={{0,1},{1,0},{2,3},{3,2},{4,5},{5,4},{6,7},{7,6},{8,9},{9,8},{10,11... | collective-permute-start | bytes 245768 | tf_op jit(solution)/shard_map/ppermute | solution.py:30
  42.0 4.4 %collective-permute-start.11 = (f32[40,512]{1,0:T(8,128)S(1)}, f32[40,512]{1,0:T(8,128)S(1)}, u32[]{:S(2)}, u32[]{:S(2)}) collective-permute-start(f32[40,512]{1,0:T(8,128)S(1)} %middle.1.refs_0_), channel_id=1, source_target_pairs={{0,2},{1,3},{2,0},{3,1},{4,6},{5,7},{6,4},{7,5},{8,10},{9,11},{10,... | collective-permute-start | bytes 245768 | tf_op jit(solution)/shard_map/ppermute | solution.py:30
  44.0 5.3 %collective-permute-start.12 = (f32[40,512]{1,0:T(8,128)S(1)}, f32[40,512]{1,0:T(8,128)S(1)}, u32[]{:S(2)}, u32[]{:S(2)}) collective-permute-start(f32[40,512]{1,0:T(8,128)S(1)} %middle.1.refs_0_), channel_id=1, source_target_pairs={{0,3},{1,2},{2,1},{3,0},{4,7},{5,6},{6,5},{7,4},{8,11},{9,10},{10,... | collective-permute-start | bytes 245768 | tf_op jit(solution)/shard_map/ppermute | solution.py:30
  49.6 1.2 %collective-permute-start.13 = (f32[8,128]{1,0:T(8,128)S(1)}, f32[8,128]{1,0:T(8,128)S(1)}, u32[]{:S(2)}, u32[]{:S(2)}) collective-permute-start(f32[8,128]{1,0:T(8,128)S(1)} %get-tuple-element.41.mine_ref), channel_id=1, source_target_pairs={{0,4},{4,0},{1,5},{5,1},{2,6},{6,2},{3,7},{7,3},{8,12},{12,8},{9,1... | collective-permute-start | bytes 12296 | tf_op jit(solution)/shard_map/ppermute | solution.py:30
  53.0 21.1 %collective-permute-start.16 = (bf16[832,512]{1,0:T(8,128)(2,1)S(1)}, bf16[832,512]{1,0:T(8,128)(2,1)S(1)}, u32[]{:S(2)}, u32[]{:S(2)}) collective-permute-start(bf16[832,512]{1,0:T(8,128)(2,1)S(1)} %get-tuple-element.44), channel_id=1, source_target_pairs={{0,1},{1,0},{2,3},{3,2},{4,5},{5,4},{6,7},{7,6},{8,9},{9,8},{10,11... | collective-permute-start | bytes 2555912 | tf_op jit(solution)/shard_map/ppermute | solution.py:30
  54.5 20.7 %collective-permute-start.17 = (bf16[832,512]{1,0:T(8,128)(2,1)S(1)}, bf16[832,512]{1,0:T(8,128)(2,1)S(1)}, u32[]{:S(2)}, u32[]{:S(2)}) collective-permute-start(bf16[832,512]{1,0:T(8,128)(2,1)S(1)} %get-tuple-element.45), channel_id=1, source_target_pairs={{0,2},{1,3},{2,0},{3,1},{4,6},{5,7},{6,4},{7,5},{8,10},{9,11},{10,... | collective-permute-start | bytes 2555912 | tf_op jit(solution)/shard_map/ppermute | solution.py:30
  55.0 7.6 %collective-permute-start.18 = (f32[2,2048]{1,0:T(2,128)S(1)}, f32[2,2048]{1,0:T(2,128)S(1)}, u32[]{:S(2)}, u32[]{:S(2)}) collective-permute-start(f32[2,2048]{1,0:T(2,128)S(1)} %get-tuple-element.51.wide_ref), channel_id=1, source_target_pairs={{0,4},{4,0},{1,5},{5,1},{2,6},{6,2},{3,7},{7,3},{8,12},{12,8},{9,1... | collective-permute-start | bytes 49160 | tf_op jit(solution)/shard_map/ppermute | solution.py:30

commit v3 on v0

v3 whole, which is shorter than its diff:
```python
import functools

import jax
import jax.numpy as jnp
from jax import lax
from jax.experimental import pallas as pl
from jax.experimental.pallas import tpu as pltpu
from jax.sharding import PartitionSpec as P

HIGHEST = lax.Precision.HIGHEST
F32 = jnp.float32
BF16 = jnp.bfloat16
KEEP = 0.05 * 0.9 * 0.9
MOVE = 0.05 * (1.0 + 0.9)
CROSS = 20
BLOCKS = 2
LANES = 128
WHOLE = pl.BlockSpec(memory_space=pltpu.VMEM)
ANYWHERE = pl.BlockSpec(memory_space=pl.ANY)
SCALAR = pl.BlockSpec(memory_space=pltpu.SMEM)
IN_HBM = pl.BlockSpec(memory_space=pltpu.HBM)
PARAMS = pltpu.CompilerParams(vmem_limit_bytes=16 * 2**20)


def hbm(x):
    return pltpu.with_memory_space_constraint(x, pltpu.HBM)


def swap(x, axis, distance):
    count = lax.axis_size(axis)
    return lax.ppermute(x, axis, [(i, i ^ distance) for i in range(count)])


BACK = (1, 2)
FRONT = (2, 1)


def beside(x, sides):
    sections = lax.axis_size("section")
    layers = lax.axis_size("replica")
    pairs = [
        (layer * sections + i, layer * sections + (i ^ sides[layer % 2]))
        for layer in range(layers)
        for i in range(sections)
    ]
    return lax.ppermute(x, ("replica", "section"), pairs)


def beside_index(sides):
    odd = (lax.axis_index("replica") & 1) == 1
    return lax.axis_index("section") ^ jnp.where(odd, sides[1], sides[0])


def partners(x, axis):
    count = lax.axis_size(axis)
    while count > 4:
        count //= 2
        x = x + swap(x, axis, count)
    return [x] + [swap(x, axis, distance) for distance in range(1, count)]


def added(parts):
    while len(parts) > 1:
        parts = [a + b for a, b in zip(parts[::2], parts[1::2])]
    return parts[0]


def pieces(x):
    one = x.astype(BF16)
    rest = x - one.astype(F32)
    two = rest.astype(BF16)
    three = (rest - two.astype(F32)).astype(BF16)
    return one, two, three


def dot(a, b, dims):
    return lax.dot_general(a, b, ((dims[0], dims[1]), ((), ())), preferred_element_type=F32)


def dot_full(a, b, dims):
    return lax.dot_general(a, b, ((dims[0], dims[1]), ((), ())), precision=HIGHEST, preferred_element_type=F32)


def folded(x):
    rank = x.shape[0] // 3
    return x[:rank] + x[rank : 2 * rank] + x[2 * rank :]


def tall(x):
    return jnp.concatenate([x[:, i : i + LANES] for i in range(0, x.shape[1], LANES)], axis=0)


def wide(x, count):
    return jnp.concatenate([x[i : i + count] for i in range(0, x.shape[0], count)], axis=1)


def fetch(copies, sems):
    started = []
    for index, (source, target) in enumerate(copies):
        copy = pltpu.make_async_copy(source, target, sems.at[index])
        copy.start()
        started.append(copy)
    return started


def base_of(weight, momentum):
    return weight.astype(F32) - KEEP * momentum


def left_stack(ortho):
    one, two, three = pieces(ortho)
    return jnp.concatenate([one, one, two, one, two, three], axis=0)


def right_stack(newbasis):
    one, two, three = pieces(newbasis)
    return jnp.concatenate([one, two, one, three, two, one], axis=0)


def product(ortho, right):
    return dot(left_stack(ortho), right, ((0,), (0,)))


def moved(base, scale, approx):
    return (base - (MOVE * scale) * approx).astype(BF16)


def start_kernel(weight_any, momentum_any, grads_any, error_any, basis_any, gains_any, back_ref, front_ref, late_ref, kept_ref, given_ref, grads_ref, error_ref, weight_ref, momentum_ref, basis_ref, gains_ref, sems):
    rows = weight_any.shape[0]
    early = back_ref.shape[0]
    late = late_ref.shape[0] // 2
    block = rows // BLOCKS
    copies = [(basis_any, basis_ref), (gains_any, gains_ref)]
    for pair in ((weight_any, weight_ref, momentum_any, momentum_ref), (grads_any, grads_ref, error_any, error_ref)):
        for part in range(BLOCKS):
            span = pl.ds(part * block, block)
            copies.append((pair[0].at[span], pair[1].at[span]))
            copies.append((pair[2].at[span], pair[3].at[span]))
    copies = fetch(copies, sems)
    rank = basis_ref.shape[0]
    half = rows // 2
    copies[0].wait()
    copies[1].wait()
    stack = jnp.concatenate(pieces(basis_ref[...]), axis=0)
    summed = rank * half // LANES
    kept_ref[summed:, :] = tall(gains_ref[...])
    for part in range(BLOCKS):
        copies[2 + 2 * part].wait()
        copies[3 + 2 * part].wait()
        start, stop = part * block, (part + 1) * block
        base = base_of(weight_ref[start:stop, :], momentum_ref[start:stop, :])
        for low, high, ref, shift in (
            (0, early, front_ref, 0),
            (rows - early, rows, back_ref, rows - early),
            (0, late, late_ref, 0),
            (rows - late, rows, late_ref, rows - 2 * late),
        ):
            low, high = max(low, start), min(high, stop)
            if low < high:
                ref[low - shift : high - shift, :] = base[low - start : high - start, :]
    terms = []
    for part in range(BLOCKS):
        copies[2 + 2 * (BLOCKS + part)].wait()
        copies[3 + 2 * (BLOCKS + part)].wait()
        span = pl.ds(part * block, block)
        term = dot(stack, grads_ref[span, :], ((1,), (1,))) + dot(stack, error_ref[span, :], ((1,), (1,)))
        terms.append(folded(term))
    middle = BLOCKS // 2
    front = jnp.concatenate(terms[:middle], axis=1)
    back = jnp.concatenate(terms[middle:], axis=1)
    first = lax.axis_index("tensor") == 0
    kept_ref[:summed, :] = tall(jnp.where(first, front, back))
    given_ref[...] = tall(jnp.where(first, back, front))


def pair_kernel(kept_ref, other_ref, out_ref):
    summed = other_ref.shape[0]
    out_ref[:summed, :] = kept_ref[:summed, :] + other_ref[...]
    out_ref[summed:, :] = kept_ref[summed:, :]


def sum_kernel(replicas, *refs):
    *parts, gain_ref, gain_momentum_ref, mine_ref, new_gain_momentum_ref, tail_ref = refs
    mean = added([part[...] for part in parts]) / replicas
    summed = mine_ref.shape[0]
    mine_ref[...] = mean[:summed]
    gain_mean = wide(mean[summed:], 2)
    new_gain_momentum = 0.9 * gain_momentum_ref[...] + gain_mean
    new_gain_momentum_ref[...] = new_gain_momentum
    tail_ref[...] = tall(gain_ref[...] - 0.02 * (gain_mean + 0.9 * new_gain_momentum))


def right_kernel(mine_ref, other_ref, root_ref, grads_ref, error_ref, term_ref, gram_ref, ortho_ref):
    rank = root_ref.shape[0]
    half = grads_ref.shape[0] // 2
    first = lax.axis_index("tensor") == 0
    mine = wide(mine_ref[...], rank)
    other = wide(other_ref[...], rank)
    lowp = (jnp.where(first, mine, other), jnp.where(first, other, mine))
    orthos = [dot_full(root_ref[...], x, ((0,), (0,))) for x in lowp]
    stacks = [jnp.concatenate(pieces(x), axis=0) for x in orthos]
    term = jnp.zeros((3 * rank, grads_ref.shape[1]), F32)
    for part, stack in enumerate(stacks):
        span = pl.ds(part * half, half)
        term += dot(stack, grads_ref[span, :], ((1,), (0,))) + dot(stack, error_ref[span, :], ((1,), (0,)))
    term_ref[...] = tall(folded(term))
    gram_ref[...] = wide(sum(dot_full(x, x, ((1,), (1,))) for x in orthos), rank // 4)
    for part in range(2):
        ortho_ref[pl.ds(part * rank, rank), :] = orthos[part]


def middle_kernel(count, *refs):
    parts, (gram_ref, tail_ref, _, _, out_ref) = refs[:count], refs[count:]
    out_ref[...] = jnp.concatenate([added([part[...] for part in parts]), gram_ref[...], tail_ref[...]], axis=0)


def factor_kernel(replicas, *refs):
    *parts, newbasis_ref, gram_ref, right_ref, wide_ref = refs
    rank, cols = newbasis_ref.shape
    summed = rank * cols // LANES
    values = [part[...] for part in parts]
    mean = added(values)
    newbasis = wide(mean[:summed], rank) / replicas
    newbasis_ref[...] = newbasis
    right = dot_full(newbasis, newbasis, ((1,), (1,)))
    gram_ref[...] = mean[summed : summed + 8]
    right_ref[...] = wide(right, rank // 4)
    section = lax.axis_index("section")
    for distance, value in enumerate(values):
        gain = wide(value[summed + 8 :], 2)
        for place in range(len(values)):

            @pl.when(section == place ^ distance)
            def _(place=place, gain=gain):
                wide_ref[:, place * cols : (place + 1) * cols] = gain


def after_kernel(entries, newbasis_ref, gram_ref, mine_ref, other_ref, own_ref, back_left_ref, front_left_ref, late_ref, back_ref, front_ref, to_back_ref, to_front_ref, scale_ref, section_ref):
    rank = newbasis_ref.shape[0]
    late = late_ref.shape[0] // 2
    half = own_ref.shape[1]
    squares = (gram_ref[...] / entries) * (mine_ref[...] + other_ref[...])
    mean = jnp.sum(jnp.sum(squares, axis=1, keepdims=True), axis=0, keepdims=True)
    scale = lax.rsqrt(mean + 1e-06)
    scale_ref[...] = jnp.broadcast_to(scale, scale_ref.shape)
    section_ref[0] = lax.axis_index("section")
    right = right_stack(newbasis_ref[...])
    to_back_ref[:half, :] = moved(front_ref[...], scale, product(front_left_ref[:rank, :], right))
    to_back_ref[half:, :] = moved(late_ref[:late, :], scale, product(own_ref[:rank, :late], right))
    to_front_ref[:half, :] = moved(back_ref[...], scale, product(back_left_ref[rank:, :], right))
    to_front_ref[half:, :] = moved(late_ref[late:, :], scale, product(own_ref[rank:, half - late :], right))


def cross_kernel(scale_ref, newbasis_ref, back_left_ref, front_left_ref, back_ref, front_ref, out_ref):
    rank = newbasis_ref.shape[0]
    half = back_left_ref.shape[1]
    count = out_ref.shape[0] // 2
    late = half - count
    scale = scale_ref[0:1, 0:1]
    right = right_stack(newbasis_ref[...])
    out_ref[:count, :] = moved(back_ref[:count, :], scale, product(back_left_ref[rank:, :count], right))
    out_ref[count:, :] = moved(front_ref[late:, :], scale, product(front_left_ref[:rank, late:], right))


def own_kernel(place_ref, scale_ref, newbasis_ref, own_ref, weight_ref, momentum_ref, grads_ref, error_ref, new_error_ref, new_momentum_ref, out_ref):
    del place_ref
    rank, cols = newbasis_ref.shape
    block = weight_ref.shape[0]
    step = pl.program_id(0)
    per = cols // block
    start = (step // per) * rank
    columns = pl.ds(pl.multiple_of((step % per) * block, block), block)
    scale = scale_ref[0:1, 0:1]
    ortho = own_ref[pl.ds(pl.multiple_of(start, rank), rank), columns]
    approx = product(ortho, right_stack(newbasis_ref[...]))
    merged = grads_ref[...].astype(F32) + error_ref[...].astype(F32)
    new_error_ref[...] = (merged - approx).astype(BF16)
    momentum = momentum_ref[...]
    new_momentum_ref[...] = 0.9 * momentum + scale * approx
    out_ref[...] = moved(base_of(weight_ref[...], momentum), scale, approx)


def near_kernel(scale_ref, newbasis_ref, back_left_ref, front_left_ref, back_ref, front_ref, held_ref, out_ref, done_ref, sems):
    del held_ref
    rank = newbasis_ref.shape[0]
    half = back_left_ref.shape[1]
    rows = 2 * half
    scale = scale_ref[0:1, 0:1]
    right = right_stack(newbasis_ref[...])
    back_side = beside_index(BACK) * rows
    front_side = beside_index(FRONT) * rows
    copies = []
    for index, (ref, ortho, to) in enumerate(
        ((back_ref, back_left_ref[rank:, :], back_side + half), (front_ref, front_left_ref[:rank, :], front_side))
    ):
        span = pl.ds(index * half, half)
        done_ref[span, :] = moved(ref[...], scale, product(ortho, right))
        to = pl.multiple_of(to, 16)
        copy = pltpu.make_async_copy(done_ref.at[span], out_ref.at[pl.ds(to, half)], sems.at[index])
        copy.start()
        copies.append(copy)
    for copy in copies:
        copy.wait()


def settle_kernel(sources, cross, late, *refs):
    *came_refs, _, out_ref, sems = refs
    rows = out_ref.shape[0] // lax.axis_size("section")
    half = rows // 2
    back_side = beside_index(BACK) * rows
    front_side = beside_index(FRONT) * rows
    across = (lax.axis_index("section") ^ 3) * rows
    last = rows - late
    places = {
        "back": ((half, across), (late, back_side)),
        "front": ((half, across + half), (late, front_side + last)),
        "cross": ((cross, front_side + last - cross), (cross, back_side + late)),
    }
    copies = []
    for source, came_ref in zip(sources, came_refs):
        start = 0
        for size, to in places[source]:
            to = pl.multiple_of(to, 16)
            copies.append((came_ref.at[pl.ds(start, size), :], out_ref.at[pl.ds(to, size), :]))
            start += size
    for copy in fetch(copies, sems):
        copy.wait()


def gain_kernel(wide_ref, other_ref, out_ref):
    cols = wide_ref.shape[1]
    first = lax.axis_index("tensor") == 0
    mine = wide_ref[...]
    other = other_ref[...]
    out_ref[:, :cols] = jnp.where(first, mine, other)
    out_ref[:, cols:] = jnp.where(first, other, mine)


def shape(dims, kind=F32):
    return jax.ShapeDtypeStruct(dims, kind)


def call(kernel, name, out_shape, in_specs, **more):
    out_specs = more.pop("out_specs", [WHOLE] * len(out_shape))
    return pl.pallas_call(
        kernel,
        out_shape=out_shape,
        in_specs=in_specs,
        out_specs=out_specs,
        compiler_params=PARAMS,
        name=name,
        cost_estimate=pl.CostEstimate(flops=0, bytes_accessed=0, transcendentals=0),
        **more,
    )


def on_device(weight, grads, error, momentum, basis, gram_root, gain, gain_momentum, gain_grads):
    replicas = lax.axis_size("replica")
    tensors = lax.axis_size("tensor")
    sections = lax.axis_size("section")
    rows, cols = weight.shape
    rank = basis.shape[1]
    half = rows // 2
    cross = rows * CROSS // 64
    late = half - cross
    summed = rank * half // LANES
    weight, momentum, grads, error = (hbm(x) for x in (weight, momentum, grads[0], error[0]))

    back, front, late_rows, kept, given, held_grads, held_error = call(
        start_kernel,
        "start",
        [pltpu.VMEM((half, cols), F32)] * 2
        + [shape((2 * late, cols)), shape((summed + 8, LANES)), shape((summed, LANES))]
        + [pltpu.VMEM((rows, cols), BF16)] * 2,
        [IN_HBM] * 6,
        scratch_shapes=[
            pltpu.VMEM((rows, cols), BF16),
            pltpu.VMEM((rows, cols), F32),
            pltpu.VMEM((rank, cols), F32),
            pltpu.VMEM((2, cols), F32),
            pltpu.SemaphoreType.DMA((4 * BLOCKS + 2,)),
        ],
    )(weight, momentum, grads, error, hbm(basis.T), hbm(gain_grads[0]))
    back = beside(back, BACK)
    front = beside(front, FRONT)
    (pair,) = call(pair_kernel, "pair", [shape(kept.shape)], [WHOLE] * 2)(kept, swap(given, "tensor", 1))
    parts = partners(pair, "replica")
    mine, new_gain_momentum, tail = call(
        functools.partial(sum_kernel, replicas),
        "sum",
        [shape((summed, LANES)), shape((2, cols)), shape((8, LANES))],
        [WHOLE] * (len(parts) + 2),
    )(*parts, gain, gain_momentum)

    term, gram, ortho = call(
        right_kernel,
        "right",
        [shape((summed, LANES)), shape((8, LANES)), shape((2 * rank, half))],
        [WHOLE] * 5,
    )(mine, swap(mine, "tensor", 1), gram_root, held_grads, held_error)
    parts = partners(term, "replica")
    (joined,) = call(
        functools.partial(middle_kernel, len(parts)),
        "middle",
        [shape((summed + 16, LANES))],
        [WHOLE] * (len(parts) + 2) + [ANYWHERE] * 2,
    )(*parts, gram, tail, back, front)
    parts = partners(joined, "section")
    back_left = beside(ortho, BACK)
    front_left = beside(ortho, FRONT)
    newbasis, gram, right, gains = call(
        functools.partial(factor_kernel, replicas),
        "factor",
        [shape((rank, cols)), shape((8, LANES)), shape((8, LANES)), shape((2, sections * cols))],
        [WHOLE] * len(parts),
    )(*parts)

    entries = rows * cols * tensors * sections
    to_back, to_front, scale, where = call(
        functools.partial(after_kernel, entries),
        "after",
        [shape((half + late, cols), BF16)] * 2 + [shape((8, LANES)), shape((1,), jnp.int32)],
        [WHOLE] * 10,
        out_specs=[WHOLE] * 3 + [SCALAR],
    )(newbasis, gram, right, swap(right, "tensor", 1), ortho, back_left, front_left, late_rows, back, front)
    late_back = beside(to_back, BACK)
    late_front = beside(to_front, FRONT)
    (to_cross,) = call(cross_kernel, "cross", [shape((2 * cross, cols), BF16)], [WHOLE] * 6)(
        scale, newbasis, back_left, front_left, back, front
    )
    late_cross = swap(to_cross, "replica", 1)

    blocks = 4
    block = rows // blocks
    step = pl.BlockSpec((block, cols), lambda i, place: (i, 0))
    fixed = [pl.BlockSpec(x.shape, lambda i, place: (0, 0)) for x in (scale, newbasis, ortho)]
    new_error, new_momentum, out = pl.pallas_call(
        own_kernel,
        out_shape=[
            pltpu.HBM((rows, cols), BF16),
            pltpu.HBM((rows, cols), F32),
            pltpu.HBM((sections * rows, cols), BF16),
        ],
        grid_spec=pltpu.PrefetchScalarGridSpec(
            num_scalar_prefetch=1,
            grid=(blocks,),
            in_specs=fixed + [step] * 4,
            out_specs=[step, step, pl.BlockSpec((block, cols), lambda i, place: (place[0] * blocks + i, 0))],
        ),
        compiler_params=PARAMS,
        name="own",
        cost_estimate=pl.CostEstimate(flops=0, bytes_accessed=0, transcendentals=0),
    )(where, scale, newbasis, ortho, weight, momentum, grads, error)
    (out,) = call(
        near_kernel,
        "near",
        [pltpu.HBM(out.shape, BF16)],
        [WHOLE] * 6 + [IN_HBM],
        out_specs=[IN_HBM],
        scratch_shapes=[pltpu.VMEM((2 * half, cols), BF16), pltpu.SemaphoreType.DMA((2,))],
        input_output_aliases={6: 0},
    )(scale, newbasis, back_left, front_left, back, front, hbm(out))
    for sources, came in ((("back",), [late_back]), (("front", "cross"), [late_front, late_cross])):
        (out,) = call(
            functools.partial(settle_kernel, sources, cross, late),
            "settle",
            [pltpu.HBM(out.shape, BF16)],
            [WHOLE] * len(came) + [IN_HBM],
            out_specs=[IN_HBM],
            scratch_shapes=[pltpu.SemaphoreType.DMA((2 * len(came),))],
            input_output_aliases={len(came): 0},
        )(*came, hbm(out))
    (new_gain,) = call(gain_kernel, "gain", [shape((2, tensors * sections * cols))], [WHOLE] * 2)(
        gains, swap(gains, "tensor", 1)
    )
    return (out, new_error[None], new_momentum, new_gain, new_gain_momentum)


def solution(mesh):
    placed = (
        P("section", "tensor"),
        P("replica", "section", "tensor"),
        P("replica", "section", "tensor"),
        P("section", "tensor"),
        P("tensor", None),
        P(),
        P(None, ("tensor", "section")),
        P(None, ("tensor", "section")),
        P("replica", None, ("tensor", "section")),
    )
    return jax.shard_map(
        on_device,
        mesh=mesh,
        in_specs=placed,
        out_specs=(
            P(None, "tensor"),
            P("replica", "section", "tensor"),
            P("section", "tensor"),
            P(),
            P(None, ("tensor", "section")),
        ),
        check_vma=False,
    )
```

time: 274 us -> 63.9 us (0.23)
  waiting for transfers between devices: 183 us -> 24.9 us
  blocking collectives: 49.7 us -> 0 us
  starting transfers between devices: 0.12 us -> 21.3 us
  Pallas kernels: 0 us -> 16.7 us
  matrix products: 14.8 us -> 0 us
  between operations: 14.5 us -> 0.77 us
  local copies, waits for them, and re-layouts: 5.88 us -> 0.01 us
  other arithmetic: 5.48 us -> 0 us
    psum x2 -> x0, waiting for transfers between devices: 165 us -> none  [the longest x1 106 us: on_device(): newbasis = lax.psum(basis_term, ('replica', 'section')) / replicas]
    psum x2 -> x0, blocking collectives: 25.5 us -> none  [the longest x1 14.8 us: on_device(): square_sum = lax.psum(jnp.sum(approx * approx), ('tensor', 'section'))]
    ppermute x0 -> x20, waiting for transfers between devices: none -> 24.9 us  [the longest x14 18.1 us: swap(): return lax.ppermute(x, axis, [(i, i ^ distance) for i in range(count)])]
    all_gather x1 -> x0, blocking collectives: 24.1 us -> none  [on_device(): lax.all_gather(local_gain, ('tensor', 'section'), axis=1, tiled=True)]
    ppermute x0 -> x20, starting transfers between devices: none -> 21.3 us  [the longest x14 13.8 us: swap(): return lax.ppermute(x, axis, [(i, i ^ distance) for i in range(count)])]
    all_gather x1 -> x0, waiting for transfers between devices: 17.5 us -> none  [on_device(): new_weight = lax.all_gather(local_weight, 'section', axis=0, tiled=True)]
    pallas_call x0 -> x13, Pallas kernels: none -> 16.7 us  [the longest x1 6.1 us: on_device(): pl.pallas_call(own_kernel, out_shape=[pltpu.HBM((rows, cols), BF16), pltp...]
    dot_general x4 -> x0, matrix products: 14.8 us -> none  [the longest x1 4.81 us: on_device(): approx = jnp.dot(ortho, newbasis.T, precision=highest)]
  transfers between devices with their start and end apart: 3 -> 20, of which waited for: 3 -> 11; matrix products, arithmetic and copies ran while one was open for 0% -> 0% of each run, Pallas kernels for 0% -> 17%
where the time goes in v3:
time: 63.9 us; the launch traced here: 63.7 us
  waiting for transfers between devices  24.9 us (39%)
  starting transfers between devices  21.3 us (33%)
  Pallas kernels  16.7 us (26%)
  between operations  0.77 us (1%)
    ppermute x14, waiting for transfers between devices, swap(): return lax.ppermute(x, axis, [(i, i ^ distance) for i in range(count)])  18.1 us
    ppermute x14, starting transfers between devices, swap(): return lax.ppermute(x, axis, [(i, i ^ distance) for i in range(count)])  13.8 us
    ppermute x6, starting transfers between devices, beside(): return lax.ppermute(x, ('replica', 'section'), pairs)  7.5 us
    ppermute x6, waiting for transfers between devices, beside(): return lax.ppermute(x, ('replica', 'section'), pairs)  6.86 us
    pallas_call x1, Pallas kernels, on_device(): pl.pallas_call(own_kernel, out_shape=[pltpu.HBM((rows, cols), BF16), pltp...  6.1 us
    pallas_call x1, Pallas kernels, on_device(): call(start_kernel, 'start', [pltpu.VMEM((half, cols), F32)] * 2 + [shape(...  3.21 us
    pallas_call x2, Pallas kernels, on_device(): call(functools.partial(settle_kernel, sources, cross, late), 'settle', [p...  1.97 us
    pallas_call x1, Pallas kernels, on_device(): call(near_kernel, 'near', [pltpu.HBM(out.shape, BF16)], [WHOLE] * 6 + [IN...  1.34 us
  transfers between devices with their start and end apart: 20, of which 11 were waited for; matrix products, arithmetic and copies ran while one was open for 0% of the time, Pallas kernels for 17%

profile of v3, /device:TPU:0, one launch (start us, length us, event | category | flops | bytes accessed | tf_op | source)
XLA Modules:
  0.0 63.7 jit_solution(8118603124175255846)
XLA Ops:
  0.6 0.0 copy-start.1
  0.6 0.0 copy-start.2
  0.7 0.0 copy-start
  0.7 3.2 %start.1 = (f32[512,512]{1,0:T(8,128)S(1)}, f32[512,512]{1,0:T(8,128)S(1)}, f32[384,512]{1,0:T(8,128)S(1)}, f32[136,128]{1,0:T(8,128)S(1)}, f32[128,128]{1,0:T(8...) custom-call(bf16[1024,512]{1,0:T(8,128)(2,1)} %weight_ref.1, f32[1024,512]{1,0:T(8,128)} %momentum_ref.1, ...), custom_call_target="tpu_custom_call" | custom-call | tf_op jit(solution)/shard_map/start/pallas_call | solution.py:369
  3.9 3.0 %collective-permute-start.8 = (f32[512,512]{1,0:T(8,128)S(1)}, f32[512,512]{1,0:T(8,128)S(1)}, u32[]{:S(2)}, u32[]{:S(2)}) collective-permute-start(f32[512,512]{1,0:T(8,128)S(1)} %get-tuple-element.37), channel_id=1, source_target_pairs={{0,1},{1,0},{2,3},{3,2},{8,10},{9,11},{10,8},{11,9},{16,17},{17,16... | collective-permute-start | bytes 3145736 | tf_op jit(solution)/shard_map/ppermute | solution.py:46
  6.9 1.5 %collective-permute-start.9 = (f32[512,512]{1,0:T(8,128)S(1)}, f32[512,512]{1,0:T(8,128)S(1)}, u32[]{:S(2)}, u32[]{:S(2)}) collective-permute-start(f32[512,512]{1,0:T(8,128)S(1)} %get-tuple-element.38), channel_id=1, source_target_pairs={{0,2},{1,3},{2,0},{3,1},{8,9},{9,8},{10,11},{11,10},{16,18},{17,19... | collective-permute-start | bytes 3145736 | tf_op jit(solution)/shard_map/ppermute | solution.py:46
  8.4 0.0 collective-permute-start
  8.4 1.3 %collective-permute-done.other_ref = f32[128,128]{1,0:T(8,128)S(1)} collective-permute-done((f32[128,128]{1,0:T(8,128)S(1)}, f32[128,128]{1,0:T(8,128)S(1)}, u32[]{:S(2)}, u32[]{:S(2)}) %collective-permute-start) | collective-permute-done | bytes 65568 | tf_op jit(solution)/shard_map/ppermute | solution.py:31
  9.7 1.6 %collective-permute-start.1 = (f32[136,128]{1,0:T(8,128)S(1)}, f32[136,128]{1,0:T(8,128)S(1)}, u32[]{:S(2)}, u32[]{:S(2)}) collective-permute-start(f32[136,128]{1,0:T(8,128)S(1)} %pair.1.refs_0_), channel_id=1, source_target_pairs={{0,8},{8,0},{16,24},{24,16},{1,9},{9,1},{17,25},{25,17},{2,10},{10... | collective-permute-start | bytes 208904 | tf_op jit(solution)/shard_map/ppermute | solution.py:31
  11.3 2.6 %collective-permute-start.2 = (f32[136,128]{1,0:T(8,128)S(1)}, f32[136,128]{1,0:T(8,128)S(1)}, u32[]{:S(2)}, u32[]{:S(2)}) collective-permute-start(f32[136,128]{1,0:T(8,128)S(1)} %pair.1.refs_0_), channel_id=1, source_target_pairs={{0,16},{8,24},{16,0},{24,8},{1,17},{9,25},{17,1},{25,9},{2,18},{10... | collective-permute-start | bytes 208904 | tf_op jit(solution)/shard_map/ppermute | solution.py:31
  13.9 0.2 collective-permute-start.3
  14.1 0.0 collective-permute-done.1.refs_1_
  14.1 5.0 %collective-permute-done.2.refs_2_ = f32[136,128]{1,0:T(8,128)S(1)} collective-permute-done((f32[136,128]{1,0:T(8,128)S(1)}, f32[136,128]{1,0:T(8,128)S(1)}, u32[]{:S(2)}, u32[]{:S(2)}) %collective-permute-start.2) | collective-permute-done | bytes 69664 | tf_op jit(solution)/shard_map/ppermute | solution.py:31
  19.1 1.0 %collective-permute-done.3.refs_3_ = f32[136,128]{1,0:T(8,128)S(1)} collective-permute-done((f32[136,128]{1,0:T(8,128)S(1)}, f32[136,128]{1,0:T(8,128)S(1)}, u32[]{:S(2)}, u32[]{:S(2)}) %collective-permute-start.3) | collective-permute-done | bytes 69664 | tf_op jit(solution)/shard_map/ppermute | solution.py:31
  20.1 0.0 copy-done.1
  20.1 0.0 copy-done.2
  20.1 0.6 sum.1
  20.7 0.0 collective-permute-start.4
  20.7 1.3 %collective-permute-done.4.other_ref = f32[128,128]{1,0:T(8,128)S(1)} collective-permute-done((f32[128,128]{1,0:T(8,128)S(1)}, f32[128,128]{1,0:T(8,128)S(1)}, u32[]{:S(2)}, u32[]{:S(2)}) %collective-permute-start.4) | collective-permute-done | bytes 65568 | tf_op jit(solution)/shard_map/ppermute | solution.py:31
  22.0 0.0 copy-done
  22.0 0.8 %right.1 = (f32[128,128]{1,0:T(8,128)S(1)}, f32[8,128]{1,0:T(8,128)S(1)}, f32[64,512]{1,0:T(8,128)S(1)}) custom-call(f32[128,128]{1,0:T(8,128)S(1)} %get-tuple-element.31.mine_ref, f32[128,128]{1,0:T(8,128)S(1)} %collective-permute-done.4.other_ref, f32[32,32]{1,0:T(8,128)S(1)} %copy-done, bf16[1024,512]{1,0:T(8,128)(2,1)S(1)} %get-tuple-element.32.grads_ref, ...), custom_call_target="tpu_custom_call" | custom-call | tf_op jit(solution)/shard_map/right/pallas_call | solution.py:395
  22.8 1.2 %collective-permute-start.5 = (f32[128,128]{1,0:T(8,128)S(1)}, f32[128,128]{1,0:T(8,128)S(1)}, u32[]{:S(2)}, u32[]{:S(2)}) collective-permute-start(f32[128,128]{1,0:T(8,128)S(1)} %get-tuple-element.34.refs_0_), channel_id=1, source_target_pairs={{0,8},{8,0},{16,24},{24,16},{1,9},{9,1},{17,25},{25,17},{2,10},{10... | collective-permute-start | bytes 196616 | tf_op jit(solution)/shard_map/ppermute | solution.py:31
  24.0 1.7 %collective-permute-start.6 = (f32[128,128]{1,0:T(8,128)S(1)}, f32[128,128]{1,0:T(8,128)S(1)}, u32[]{:S(2)}, u32[]{:S(2)}) collective-permute-start(f32[128,128]{1,0:T(8,128)S(1)} %get-tuple-element.34.refs_0_), channel_id=1, source_target_pairs={{0,16},{8,24},{16,0},{24,8},{1,17},{9,25},{17,1},{25,9},{2,18},{10... | collective-permute-start | bytes 196616 | tf_op jit(solution)/shard_map/ppermute | solution.py:31
  25.7 1.6 %collective-permute-start.7 = (f32[128,128]{1,0:T(8,128)S(1)}, f32[128,128]{1,0:T(8,128)S(1)}, u32[]{:S(2)}, u32[]{:S(2)}) collective-permute-start(f32[128,128]{1,0:T(8,128)S(1)} %get-tuple-element.34.refs_0_), channel_id=1, source_target_pairs={{0,24},{8,16},{16,8},{24,0},{1,25},{9,17},{17,9},{25,1},{2,26},{10... | collective-permute-start | bytes 196616 | tf_op jit(solution)/shard_map/ppermute | solution.py:31
  27.2 0.0 collective-permute-done.5.refs_1_
  27.2 0.5 collective-permute-start.14
  27.8 4.5 %collective-permute-done.6.refs_2_ = f32[128,128]{1,0:T(8,128)S(1)} collective-permute-done((f32[128,128]{1,0:T(8,128)S(1)}, f32[128,128]{1,0:T(8,128)S(1)}, u32[]{:S(2)}, u32[]{:S(2)}) %collective-permute-start.6) | collective-permute-done | bytes 65568 | tf_op jit(solution)/shard_map/ppermute | solution.py:31
  32.3 0.5 collective-permute-start.15
  32.8 0.0 collective-permute-done.7.refs_3_
  32.8 0.0 collective-permute-done.8.refs_6_.back_ref
  32.8 0.0 collective-permute-done.9.refs_7_.front_ref
  32.8 0.6 collective-permute-start.10
  33.4 1.6 %collective-permute-start.11 = (f32[144,128]{1,0:T(8,128)S(1)}, f32[144,128]{1,0:T(8,128)S(1)}, u32[]{:S(2)}, u32[]{:S(2)}) collective-permute-start(f32[144,128]{1,0:T(8,128)S(1)} %middle.1.refs_0_), channel_id=1, source_target_pairs={{0,2},{1,3},{2,0},{3,1},{4,6},{5,7},{6,4},{7,5},{8,10},{9,11},{10,... | collective-permute-start | bytes 221192 | tf_op jit(solution)/shard_map/ppermute | solution.py:31
  35.0 1.3 %collective-permute-start.12 = (f32[144,128]{1,0:T(8,128)S(1)}, f32[144,128]{1,0:T(8,128)S(1)}, u32[]{:S(2)}, u32[]{:S(2)}) collective-permute-start(f32[144,128]{1,0:T(8,128)S(1)} %middle.1.refs_0_), channel_id=1, source_target_pairs={{0,3},{1,2},{2,1},{3,0},{4,7},{5,6},{6,5},{7,4},{8,11},{9,10},{10,... | collective-permute-start | bytes 221192 | tf_op jit(solution)/shard_map/ppermute | solution.py:31
  36.4 0.9 %collective-permute-done.10.refs_1_ = f32[144,128]{1,0:T(8,128)S(1)} collective-permute-done((f32[144,128]{1,0:T(8,128)S(1)}, f32[144,128]{1,0:T(8,128)S(1)}, u32[]{:S(2)}, u32[]{:S(2)}) %collective-permute-start.10) | collective-permute-done | bytes 73760 | tf_op jit(solution)/shard_map/ppermute | solution.py:31
  37.2 1.1 %collective-permute-done.11.refs_2_ = f32[144,128]{1,0:T(8,128)S(1)} collective-permute-done((f32[144,128]{1,0:T(8,128)S(1)}, f32[144,128]{1,0:T(8,128)S(1)}, u32[]{:S(2)}, u32[]{:S(2)}) %collective-permute-start.11) | collective-permute-done | bytes 73760 | tf_op jit(solution)/shard_map/ppermute | solution.py:31
  38.3 2.0 %collective-permute-done.12.refs_3_ = f32[144,128]{1,0:T(8,128)S(1)} collective-permute-done((f32[144,128]{1,0:T(8,128)S(1)}, f32[144,128]{1,0:T(8,128)S(1)}, u32[]{:S(2)}, u32[]{:S(2)}) %collective-permute-start.12) | collective-permute-done | bytes 73760 | tf_op jit(solution)/shard_map/ppermute | solution.py:31
  40.3 0.3 factor.1
  40.6 0.1 collective-permute-start.13
  40.7 0.0 collective-permute-done.14.back_left_ref
  40.7 0.0 collective-permute-done.15.front_left_ref
  40.7 1.1 %collective-permute-done.13.other_ref = f32[8,128]{1,0:T(8,128)S(1)} collective-permute-done((f32[8,128]{1,0:T(8,128)S(1)}, f32[8,128]{1,0:T(8,128)S(1)}, u32[]{:S(2)}, u32[]{:S(2)}) %collective-permute-start.13) | collective-permute-done | bytes 4128 | tf_op jit(solution)/shard_map/ppermute | solution.py:31
  41.8 1.2 %after.1 = (bf16[704,512]{1,0:T(8,128)(2,1)S(1)}, bf16[704,512]{1,0:T(8,128)(2,1)S(1)}, f32[8,128]{1,0:T(8,128)S(1)}, s32[1]{0:T(128)}) custom-call(f32[32,512]{1,0:T(8,128)S(1)} %get-tuple-element.39.newbasis_ref, f32[8,128]{1,0:T(8,128)S(1)} %get-tuple-element.40.gram_ref, f32[8,128]{1,0:T(8,128)S(1)} %get-tuple-element.41.mine_ref, ...), custom_call_target="tpu_custom_call" | custom-call | tf_op jit(solution)/shard_map/after/pallas_call | solution.py:419
  43.1 1.6 %collective-permute-start.18 = (bf16[704,512]{1,0:T(8,128)(2,1)S(1)}, bf16[704,512]{1,0:T(8,128)(2,1)S(1)}, u32[]{:S(2)}, u32[]{:S(2)}) collective-permute-start(bf16[704,512]{1,0:T(8,128)(2,1)S(1)} %get-tuple-element.46), channel_id=1, source_target_pairs={{0,1},{1,0},{2,3},{3,2},{8,10},{9,11},{10,8},{11,9},{16,17},{17,16... | collective-permute-start | bytes 2162696 | tf_op jit(solution)/shard_map/ppermute | solution.py:46
  44.6 0.4 collective-permute-start.16
  45.0 0.4 cross.1
  45.4 1.3 %collective-permute-start.17 = (bf16[640,512]{1,0:T(8,128)(2,1)S(1)}, bf16[640,512]{1,0:T(8,128)(2,1)S(1)}, u32[]{:S(2)}, u32[]{:S(2)}) collective-permute-start(bf16[640,512]{1,0:T(8,128)(2,1)S(1)} %cross.1), channel_id=1, source_target_pairs={{0,8},{8,0},{16,24},{24,16},{1,9},{9,1},{17,25},{25,17},{2,10},{10... | collective-permute-start | bytes 1966088 | tf_op jit(solution)/shard_map/ppermute | solution.py:31
  46.8 0.0 collective-permute-start.19
  46.8 6.1 %own.1 = (bf16[1024,512]{1,0:T(8,128)(2,1)}, f32[1024,512]{1,0:T(8,128)}, bf16[4096,512]{1,0:T(8,128)(2,1)}) custom-call(s32[1]{0:T(128)} %get-tuple-element.47.place_ref, f32[8,128]{1,0:T(8,128)S(1)} %get-tuple-element.45.scale_ref, f32[32,512]{1,0:T(8,128)S(1)} %get-tuple-element.39.newbasis_ref, f32[64,512]{1,0:T(8,128)S(1)} %get-tuple-element.42.own_ref, ...), custom_call_target="tpu_custom_call" | custom-call | tf_op jit(solution)/shard_map/own/pallas_call | solution.py:437
  52.9 1.3 %near.1.refs_1_ = bf16[4096,512]{1,0:T(8,128)(2,1)} custom-call(f32[8,128]{1,0:T(8,128)S(1)} %get-tuple-element.45.scale_ref, f32[32,512]{1,0:T(8,128)S(1)} %get-tuple-element.39.newbasis_ref, f32[64,512]{1,0:T(8,128)S(1)} %collective-permute-done.14.back_left_ref, ...), custom_call_target="tpu_custom_call", output_to_operand_aliasing={{}: (6, {})} | custom-call | tf_op jit(solution)/shard_map/near/pallas_call | solution.py:454
  54.2 0.0 collective-permute-done.19.other_ref
  54.2 0.6 gain.1
  54.8 6.5 %collective-permute-done.18.refs_0_ = bf16[704,512]{1,0:T(8,128)(2,1)S(1)} collective-permute-done((bf16[704,512]{1,0:T(8,128)(2,1)S(1)}, bf16[704,512]{1,0:T(8,128)(2,1)S(1)}, u32[]{:S(2)}, u32[]{:S(2)}) %collective-permute-start.18) | collective-permute-done | bytes 720928 | tf_op jit(solution)/shard_map/ppermute | solution.py:46
  61.3 0.9 %settle.2.refs_2_ = bf16[4096,512]{1,0:T(8,128)(2,1)} custom-call(bf16[704,512]{1,0:T(8,128)(2,1)S(1)} %collective-permute-done.18.refs_0_, bf16[4096,512]{1,0:T(8,128)(2,1)} %near.1.refs_1_), custom_call_target="tpu_custom_call", output_to_operand_aliasing={{}: (1, {})} | custom-call | tf_op jit(solution)/shard_map/settle/pallas_call | solution.py:464
  62.2 0.0 collective-permute-done.17.refs_1_
  62.2 0.3 collective-permute-done.16.refs_0_
  62.6 1.1 %settle.3 = bf16[4096,512]{1,0:T(8,128)(2,1)} custom-call(bf16[704,512]{1,0:T(8,128)(2,1)S(1)} %collective-permute-done.16.refs_0_, bf16[640,512]{1,0:T(8,128)(2,1)S(1)} %collective-permute-done.17.refs_1_, bf16[4096,512]{1,0:T(8,128)(2,1)} %settle.2.refs_2_), custom_call_target="tpu_custom_call", output_to_operand_aliasing={{}: (2, {})} | custom-call | tf_op jit(solution)/shard_map/settle/pallas_call | solution.py:464
  (2 shorter events, 0.0 us)
Async XLA Ops:
  0.6 19.5 %copy-start.1 = (f32[2,512]{1,0:T(2,128)S(1)}, f32[2,512]{1,0:T(2,128)}, u32[]{:S(2)}) copy-start(f32[2,512]{1,0:T(2,128)} %refs_4_.1) | copy-start | bytes 12292
  0.6 19.5 %copy-start.2 = (f32[2,512]{1,0:T(2,128)S(1)}, f32[2,512]{1,0:T(2,128)}, u32[]{:S(2)}) copy-start(f32[2,512]{1,0:T(2,128)} %refs_5_.1) | copy-start | bytes 12292
  0.7 21.3 %copy-start = (f32[32,32]{1,0:T(8,128)S(1)}, f32[32,32]{1,0:T(8,128)}, u32[]{:S(2)}) copy-start(f32[32,32]{1,0:T(8,128)} %root_ref.1) | copy-start | bytes 12292
  3.9 28.9 %collective-permute-start.8 = (f32[512,512]{1,0:T(8,128)S(1)}, f32[512,512]{1,0:T(8,128)S(1)}, u32[]{:S(2)}, u32[]{:S(2)}) collective-permute-start(f32[512,512]{1,0:T(8,128)S(1)} %get-tuple-element.37), channel_id=1, source_target_pairs={{0,1},{1,0},{2,3},{3,2},{8,10},{9,11},{10,8},{11,9},{16,17},{17,16... | collective-permute-start | bytes 3145736 | tf_op jit(solution)/shard_map/ppermute | solution.py:46
  6.9 25.9 %collective-permute-start.9 = (f32[512,512]{1,0:T(8,128)S(1)}, f32[512,512]{1,0:T(8,128)S(1)}, u32[]{:S(2)}, u32[]{:S(2)}) collective-permute-start(f32[512,512]{1,0:T(8,128)S(1)} %get-tuple-element.38), channel_id=1, source_target_pairs={{0,2},{1,3},{2,0},{3,1},{8,9},{9,8},{10,11},{11,10},{16,18},{17,19... | collective-permute-start | bytes 3145736 | tf_op jit(solution)/shard_map/ppermute | solution.py:46
  8.4 1.3 %collective-permute-start = (f32[128,128]{1,0:T(8,128)S(1)}, f32[128,128]{1,0:T(8,128)S(1)}, u32[]{:S(2)}, u32[]{:S(2)}) collective-permute-start(f32[128,128]{1,0:T(8,128)S(1)} %get-tuple-element.30), channel_id=1, source_target_pairs={{0,4},{4,0},{1,5},{5,1},{2,6},{6,2},{3,7},{7,3},{8,12},{12,8},{9,1... | collective-permute-start | bytes 196616 | tf_op jit(solution)/shard_map/ppermute | solution.py:31
  9.7 4.5 %collective-permute-start.1 = (f32[136,128]{1,0:T(8,128)S(1)}, f32[136,128]{1,0:T(8,128)S(1)}, u32[]{:S(2)}, u32[]{:S(2)}) collective-permute-start(f32[136,128]{1,0:T(8,128)S(1)} %pair.1.refs_0_), channel_id=1, source_target_pairs={{0,8},{8,0},{16,24},{24,16},{1,9},{9,1},{17,25},{25,17},{2,10},{10... | collective-permute-start | bytes 208904 | tf_op jit(solution)/shard_map/ppermute | solution.py:31
  11.3 7.8 %collective-permute-start.2 = (f32[136,128]{1,0:T(8,128)S(1)}, f32[136,128]{1,0:T(8,128)S(1)}, u32[]{:S(2)}, u32[]{:S(2)}) collective-permute-start(f32[136,128]{1,0:T(8,128)S(1)} %pair.1.refs_0_), channel_id=1, source_target_pairs={{0,16},{8,24},{16,0},{24,8},{1,17},{9,25},{17,1},{25,9},{2,18},{10... | collective-permute-start | bytes 208904 | tf_op jit(solution)/shard_map/ppermute | solution.py:31
  13.9 6.2 %collective-permute-start.3 = (f32[136,128]{1,0:T(8,128)S(1)}, f32[136,128]{1,0:T(8,128)S(1)}, u32[]{:S(2)}, u32[]{:S(2)}) collective-permute-start(f32[136,128]{1,0:T(8,128)S(1)} %pair.1.refs_0_), channel_id=1, source_target_pairs={{0,24},{8,16},{16,8},{24,0},{1,25},{9,17},{17,9},{25,1},{2,26},{10... | collective-permute-start | bytes 208904 | tf_op jit(solution)/shard_map/ppermute | solution.py:31
  20.7 1.3 %collective-permute-start.4 = (f32[128,128]{1,0:T(8,128)S(1)}, f32[128,128]{1,0:T(8,128)S(1)}, u32[]{:S(2)}, u32[]{:S(2)}) collective-permute-start(f32[128,128]{1,0:T(8,128)S(1)} %get-tuple-element.31.mine_ref), channel_id=1, source_target_pairs={{0,4},{4,0},{1,5},{5,1},{2,6},{6,2},{3,7},{7,3},{8,12},{12,8},{9,1... | collective-permute-start | bytes 196616 | tf_op jit(solution)/shard_map/ppermute | solution.py:31
  22.8 4.4 %collective-permute-start.5 = (f32[128,128]{1,0:T(8,128)S(1)}, f32[128,128]{1,0:T(8,128)S(1)}, u32[]{:S(2)}, u32[]{:S(2)}) collective-permute-start(f32[128,128]{1,0:T(8,128)S(1)} %get-tuple-element.34.refs_0_), channel_id=1, source_target_pairs={{0,8},{8,0},{16,24},{24,16},{1,9},{9,1},{17,25},{25,17},{2,10},{10... | collective-permute-start | bytes 196616 | tf_op jit(solution)/shard_map/ppermute | solution.py:31
  24.0 8.2 %collective-permute-start.6 = (f32[128,128]{1,0:T(8,128)S(1)}, f32[128,128]{1,0:T(8,128)S(1)}, u32[]{:S(2)}, u32[]{:S(2)}) collective-permute-start(f32[128,128]{1,0:T(8,128)S(1)} %get-tuple-element.34.refs_0_), channel_id=1, source_target_pairs={{0,16},{8,24},{16,0},{24,8},{1,17},{9,25},{17,1},{25,9},{2,18},{10... | collective-permute-start | bytes 196616 | tf_op jit(solution)/shard_map/ppermute | solution.py:31
  25.7 7.1 %collective-permute-start.7 = (f32[128,128]{1,0:T(8,128)S(1)}, f32[128,128]{1,0:T(8,128)S(1)}, u32[]{:S(2)}, u32[]{:S(2)}) collective-permute-start(f32[128,128]{1,0:T(8,128)S(1)} %get-tuple-element.34.refs_0_), channel_id=1, source_target_pairs={{0,24},{8,16},{16,8},{24,0},{1,25},{9,17},{17,9},{25,1},{2,26},{10... | collective-permute-start | bytes 196616 | tf_op jit(solution)/shard_map/ppermute | solution.py:31
  27.2 13.5 %collective-permute-start.14 = (f32[64,512]{1,0:T(8,128)S(1)}, f32[64,512]{1,0:T(8,128)S(1)}, u32[]{:S(2)}, u32[]{:S(2)}) collective-permute-start(f32[64,512]{1,0:T(8,128)S(1)} %get-tuple-element.42.own_ref), channel_id=1, source_target_pairs={{0,1},{1,0},{2,3},{3,2},{8,10},{9,11},{10,8},{11,9},{16,17},{17,16... | collective-permute-start | bytes 393224 | tf_op jit(solution)/shard_map/ppermute | solution.py:46
  32.3 8.5 %collective-permute-start.15 = (f32[64,512]{1,0:T(8,128)S(1)}, f32[64,512]{1,0:T(8,128)S(1)}, u32[]{:S(2)}, u32[]{:S(2)}) collective-permute-start(f32[64,512]{1,0:T(8,128)S(1)} %get-tuple-element.42.own_ref), channel_id=1, source_target_pairs={{0,2},{1,3},{2,0},{3,1},{8,9},{9,8},{10,11},{11,10},{16,18},{17,19... | collective-permute-start | bytes 393224 | tf_op jit(solution)/shard_map/ppermute | solution.py:46
  32.8 4.4 %collective-permute-start.10 = (f32[144,128]{1,0:T(8,128)S(1)}, f32[144,128]{1,0:T(8,128)S(1)}, u32[]{:S(2)}, u32[]{:S(2)}) collective-permute-start(f32[144,128]{1,0:T(8,128)S(1)} %middle.1.refs_0_), channel_id=1, source_target_pairs={{0,1},{1,0},{2,3},{3,2},{4,5},{5,4},{6,7},{7,6},{8,9},{9,8},{10,11... | collective-permute-start | bytes 221192 | tf_op jit(solution)/shard_map/ppermute | solution.py:31
  33.4 4.9 %collective-permute-start.11 = (f32[144,128]{1,0:T(8,128)S(1)}, f32[144,128]{1,0:T(8,128)S(1)}, u32[]{:S(2)}, u32[]{:S(2)}) collective-permute-start(f32[144,128]{1,0:T(8,128)S(1)} %middle.1.refs_0_), channel_id=1, source_target_pairs={{0,2},{1,3},{2,0},{3,1},{4,6},{5,7},{6,4},{7,5},{8,10},{9,11},{10,... | collective-permute-start | bytes 221192 | tf_op jit(solution)/shard_map/ppermute | solution.py:31
  35.0 5.3 %collective-permute-start.12 = (f32[144,128]{1,0:T(8,128)S(1)}, f32[144,128]{1,0:T(8,128)S(1)}, u32[]{:S(2)}, u32[]{:S(2)}) collective-permute-start(f32[144,128]{1,0:T(8,128)S(1)} %middle.1.refs_0_), channel_id=1, source_target_pairs={{0,3},{1,2},{2,1},{3,0},{4,7},{5,6},{6,5},{7,4},{8,11},{9,10},{10,... | collective-permute-start | bytes 221192 | tf_op jit(solution)/shard_map/ppermute | solution.py:31
  40.6 1.2 %collective-permute-start.13 = (f32[8,128]{1,0:T(8,128)S(1)}, f32[8,128]{1,0:T(8,128)S(1)}, u32[]{:S(2)}, u32[]{:S(2)}) collective-permute-start(f32[8,128]{1,0:T(8,128)S(1)} %get-tuple-element.41.mine_ref), channel_id=1, source_target_pairs={{0,4},{4,0},{1,5},{5,1},{2,6},{6,2},{3,7},{7,3},{8,12},{12,8},{9,1... | collective-permute-start | bytes 12296 | tf_op jit(solution)/shard_map/ppermute | solution.py:31
  43.1 18.3 %collective-permute-start.18 = (bf16[704,512]{1,0:T(8,128)(2,1)S(1)}, bf16[704,512]{1,0:T(8,128)(2,1)S(1)}, u32[]{:S(2)}, u32[]{:S(2)}) collective-permute-start(bf16[704,512]{1,0:T(8,128)(2,1)S(1)} %get-tuple-element.46), channel_id=1, source_target_pairs={{0,1},{1,0},{2,3},{3,2},{8,10},{9,11},{10,8},{11,9},{16,17},{17,16... | collective-permute-start | bytes 2162696 | tf_op jit(solution)/shard_map/ppermute | solution.py:46
  44.6 17.9 %collective-permute-start.16 = (bf16[704,512]{1,0:T(8,128)(2,1)S(1)}, bf16[704,512]{1,0:T(8,128)(2,1)S(1)}, u32[]{:S(2)}, u32[]{:S(2)}) collective-permute-start(bf16[704,512]{1,0:T(8,128)(2,1)S(1)} %get-tuple-element.44), channel_id=1, source_target_pairs={{0,2},{1,3},{2,0},{3,1},{8,9},{9,8},{10,11},{11,10},{16,18},{17,19... | collective-permute-start | bytes 2162696 | tf_op jit(solution)/shard_map/ppermute | solution.py:46
  45.4 16.8 %collective-permute-start.17 = (bf16[640,512]{1,0:T(8,128)(2,1)S(1)}, bf16[640,512]{1,0:T(8,128)(2,1)S(1)}, u32[]{:S(2)}, u32[]{:S(2)}) collective-permute-start(bf16[640,512]{1,0:T(8,128)(2,1)S(1)} %cross.1), channel_id=1, source_target_pairs={{0,8},{8,0},{16,24},{24,16},{1,9},{9,1},{17,25},{25,17},{2,10},{10... | collective-permute-start | bytes 1966088 | tf_op jit(solution)/shard_map/ppermute | solution.py:31
  46.8 7.4 %collective-permute-start.19 = (f32[2,2048]{1,0:T(2,128)S(1)}, f32[2,2048]{1,0:T(2,128)S(1)}, u32[]{:S(2)}, u32[]{:S(2)}) collective-permute-start(f32[2,2048]{1,0:T(2,128)S(1)} %get-tuple-element.51.wide_ref), channel_id=1, source_target_pairs={{0,4},{4,0},{1,5},{5,1},{2,6},{6,2},{3,7},{7,3},{8,12},{12,8},{9,1... | collective-permute-start | bytes 49160 | tf_op jit(solution)/shard_map/ppermute | solution.py:31

commit v4 on v3

v4 whole, which is shorter than its diff:
```python
import functools

import jax
import jax.numpy as jnp
from jax import lax
from jax.experimental import pallas as pl
from jax.experimental.pallas import tpu as pltpu
from jax.sharding import PartitionSpec as P

HIGHEST = lax.Precision.HIGHEST
F32 = jnp.float32
BF16 = jnp.bfloat16
KEEP = 0.05 * 0.9 * 0.9
MOVE = 0.05 * (1.0 + 0.9)
MORE = 10
PASSED = 6
CROSS = 14
BLOCKS = 2
LANES = 128
FAR = 8 * 10**9
WHOLE = pl.BlockSpec(memory_space=pltpu.VMEM)
ANYWHERE = pl.BlockSpec(memory_space=pl.ANY)
SCALAR = pl.BlockSpec(memory_space=pltpu.SMEM)
IN_HBM = pl.BlockSpec(memory_space=pltpu.HBM)
PARAMS = pltpu.CompilerParams(vmem_limit_bytes=16 * 2**20)


def hbm(x):
    return pltpu.with_memory_space_constraint(x, pltpu.HBM)


def swap(x, axis, distance):
    count = lax.axis_size(axis)
    return lax.ppermute(x, axis, [(i, i ^ distance) for i in range(count)])


BACK = (1, 2)
FRONT = (2, 1)


def beside(x, sides):
    sections = lax.axis_size("section")
    layers = lax.axis_size("replica")
    pairs = [
        (layer * sections + i, layer * sections + (i ^ sides[layer % 2]))
        for layer in range(layers)
        for i in range(sections)
    ]
    return lax.ppermute(x, ("replica", "section"), pairs)


def beside_index(sides):
    odd = (lax.axis_index("replica") & 1) == 1
    return lax.axis_index("section") ^ jnp.where(odd, sides[1], sides[0])


def partners(x, axis):
    count = lax.axis_size(axis)
    while count > 4:
        count //= 2
        x = x + swap(x, axis, count)
    return [swap(x, axis, distance) for distance in range(count - 1, 0, -1)] + [x]


def added(parts):
    while len(parts) > 1:
        parts = [a + b for a, b in zip(parts[::2], parts[1::2])]
    return parts[0]


def pieces(x):
    one = x.astype(BF16)
    rest = x - one.astype(F32)
    two = rest.astype(BF16)
    three = (rest - two.astype(F32)).astype(BF16)
    return one, two, three


def dot(a, b, dims):
    return lax.dot_general(a, b, ((dims[0], dims[1]), ((), ())), preferred_element_type=F32)


def dot_full(a, b, dims):
    return lax.dot_general(a, b, ((dims[0], dims[1]), ((), ())), precision=HIGHEST, preferred_element_type=F32)


def folded(x):
    rank = x.shape[0] // 3
    return x[:rank] + x[rank : 2 * rank] + x[2 * rank :]


def tall(x):
    return jnp.concatenate([x[:, i : i + LANES] for i in range(0, x.shape[1], LANES)], axis=0)


def wide(x, count):
    return jnp.concatenate([x[i : i + count] for i in range(0, x.shape[0], count)], axis=1)


def fetch(copies, sems):
    started = []
    for index, (source, target) in enumerate(copies):
        copy = pltpu.make_async_copy(source, target, sems.at[index])
        copy.start()
        started.append(copy)
    return started


def base_of(weight, momentum):
    return weight.astype(F32) - KEEP * momentum


def left_stack(ortho):
    one, two, three = pieces(ortho)
    return jnp.concatenate([one, one, two, one, two, three], axis=0)


def right_stack(newbasis):
    one, two, three = pieces(newbasis)
    return jnp.concatenate([one, two, one, three, two, one], axis=0)


def product(ortho, right):
    return dot(left_stack(ortho), right, ((0,), (0,)))


def moved(base, scale, approx):
    return (base - (MOVE * scale) * approx).astype(BF16)


def start_kernel(weight_any, momentum_any, grads_any, error_any, basis_any, gains_any, back_ref, front_ref, late_ref, grads_ref, error_ref, basis_ref, gains_ref, weight_ref, momentum_ref, sems):
    rows = weight_any.shape[0]
    half = back_ref.shape[0]
    late = late_ref.shape[0] // 2
    block = rows // BLOCKS
    copies = []
    for part in range(BLOCKS):
        span = pl.ds(part * block, block)
        copies.append((weight_any.at[span], weight_ref.at[span]))
        copies.append((momentum_any.at[span], momentum_ref.at[span]))
    copies += [(grads_any, grads_ref), (error_any, error_ref), (basis_any, basis_ref), (gains_any, gains_ref)]
    copies = fetch(copies, sems)
    for part in range(BLOCKS):
        copies[2 * part].wait()
        copies[2 * part + 1].wait()
        start, stop = part * block, (part + 1) * block
        base = base_of(weight_ref[start:stop, :], momentum_ref[start:stop, :])
        for low, high, ref, shift in (
            (0, half, front_ref, 0),
            (half, rows, back_ref, half),
            (0, late, late_ref, 0),
            (rows - late, rows, late_ref, rows - 2 * late),
        ):
            low, high = max(low, start), min(high, stop)
            if low < high:
                ref[low - shift : high - shift, :] = base[low - start : high - start, :]
    for copy in copies[2 * BLOCKS :]:
        copy.wait()


def left_kernel(basis_ref, gains_ref, grads_ref, error_ref, kept_ref, given_ref):
    half = grads_ref.shape[0] // 2
    summed = given_ref.shape[0]
    stack = jnp.concatenate(pieces(basis_ref[...]), axis=0)
    terms = []
    for part in range(2):
        span = pl.ds(part * half, half)
        term = dot(stack, grads_ref[span, :], ((1,), (1,))) + dot(stack, error_ref[span, :], ((1,), (1,)))
        terms.append(tall(folded(term)))
    first = lax.axis_index("tensor") == 0
    kept_ref[:summed, :] = jnp.where(first, terms[0], terms[1])
    kept_ref[summed:, :] = tall(gains_ref[...])
    given_ref[...] = jnp.where(first, terms[1], terms[0])


def pair_kernel(kept_ref, other_ref, out_ref):
    summed = other_ref.shape[0]
    out_ref[:summed, :] = kept_ref[:summed, :] + other_ref[...]
    out_ref[summed:, :] = kept_ref[summed:, :]


def sum_kernel(replicas, *refs):
    *parts, mine_ref, gains_ref = refs
    mean = added([part[...] for part in parts]) / replicas
    summed = mine_ref.shape[0]
    mine_ref[...] = mean[:summed]
    gains_ref[...] = mean[summed:]


def gain_kernel(mean_ref, gain_ref, gain_momentum_ref, new_gain_momentum_ref, tail_ref):
    mean = wide(mean_ref[...], 2)
    new_gain_momentum = 0.9 * gain_momentum_ref[...] + mean
    new_gain_momentum_ref[...] = new_gain_momentum
    tail_ref[...] = tall(gain_ref[...] - 0.02 * (mean + 0.9 * new_gain_momentum))


def right_kernel(mine_ref, other_ref, root_ref, grads_ref, error_ref, _, term_ref, gram_ref, ortho_ref, half_ref):
    rank = root_ref.shape[0]
    half = grads_ref.shape[0] // 2
    first = lax.axis_index("tensor") == 0
    mine = wide(mine_ref[...], rank)
    other = wide(other_ref[...], rank)
    lowp = (jnp.where(first, mine, other), jnp.where(first, other, mine))
    orthos = [dot_full(root_ref[...], x, ((0,), (0,))) for x in lowp]
    stacks = [jnp.concatenate(pieces(x), axis=0) for x in orthos]
    term = jnp.zeros((3 * rank, grads_ref.shape[1]), F32)
    for part, stack in enumerate(stacks):
        span = pl.ds(part * half, half)
        term += dot(stack, grads_ref[span, :], ((1,), (0,))) + dot(stack, error_ref[span, :], ((1,), (0,)))
    term_ref[...] = tall(folded(term))
    gram_ref[...] = wide(sum(dot_full(x, x, ((1,), (1,))) for x in orthos), rank // 4)
    half_ref[...] = tall(jnp.where(first, orthos[0], orthos[1]))
    for part in range(2):
        ortho_ref[pl.ds(part * rank, rank), :] = orthos[part]


def middle_kernel(count, *refs):
    parts, (gram_ref, tail_ref, ortho_ref, _, _, out_ref, long_ref) = refs[:count], refs[count:]
    joined = jnp.concatenate([added([part[...] for part in parts]), gram_ref[...], tail_ref[...]], axis=0)
    out_ref[...] = joined
    long_ref[: joined.shape[0], :] = joined
    long_ref[joined.shape[0] :, :] = ortho_ref[...]


def relay_kernel(_, late_ref, back_ref, front_ref, more_back_ref, more_front_ref, pass_ref):
    more = more_back_ref.shape[0]
    passed = pass_ref.shape[0] // 2
    more_back_ref[...] = late_ref[:more, :]
    more_front_ref[...] = late_ref[late_ref.shape[0] - more :, :]
    pass_ref[:passed, :] = back_ref[:passed, :]
    pass_ref[passed:, :] = front_ref[front_ref.shape[0] - passed :, :]


def far_kernel(in_ref, out_ref):
    out_ref[...] = in_ref[...]


def factor_kernel(replicas, *refs):
    *parts, newbasis_ref, gram_ref, mixed_ref, wide_ref = refs
    rank, cols = newbasis_ref.shape
    summed = rank * cols // LANES
    values = [part[: summed + 16, :] for part in parts]
    mean = added(values)
    newbasis = wide(mean[:summed], rank) / replicas
    newbasis_ref[...] = newbasis
    right = dot_full(newbasis, newbasis, ((1,), (1,)))
    gram_ref[...] = mean[summed : summed + 8]
    two, one = (part[summed + 16 :, :] for part in parts[1:3])
    odd = (lax.axis_index("replica") & 1) == 1
    mixed_ref[:summed, :] = jnp.where(odd, two, one)
    mixed_ref[summed : 2 * summed, :] = jnp.where(odd, one, two)
    mixed_ref[2 * summed :, :] = wide(right, rank // 4)
    section = lax.axis_index("section")
    for distance, value in enumerate(values[::-1]):
        gain = wide(value[summed + 8 :], 2)
        for place in range(len(values)):

            @pl.when(section == place ^ distance)
            def _(place=place, gain=gain):
                wide_ref[:, place * cols : (place + 1) * cols] = gain


def after_kernel(entries, newbasis_ref, gram_ref, mine_ref, other_ref, own_ref, late_ref, back_ref, front_ref, to_back_ref, to_front_ref, scale_ref, back_left_ref, front_left_ref, section_ref):
    rank = newbasis_ref.shape[0]
    half = own_ref.shape[1]
    late = to_back_ref.shape[0] - half
    more = late_ref.shape[0] // 2 - late
    summed = rank * half // LANES
    squares = (gram_ref[...] / entries) * (mine_ref[2 * summed :, :] + other_ref[2 * summed :, :])
    mean = jnp.sum(jnp.sum(squares, axis=1, keepdims=True), axis=0, keepdims=True)
    scale = lax.rsqrt(mean + 1e-06)
    scale_ref[...] = jnp.broadcast_to(scale, scale_ref.shape)
    section_ref[0] = lax.axis_index("section")
    right = right_stack(newbasis_ref[...])
    first = lax.axis_index("tensor") == 0
    for left_ref, start in ((back_left_ref, 0), (front_left_ref, summed)):
        mine = wide(mine_ref[start : start + summed, :], rank)
        other = wide(other_ref[start : start + summed, :], rank)
        left_ref[:rank, :] = jnp.where(first, mine, other)
        left_ref[rank:, :] = jnp.where(first, other, mine)
    to_back_ref[:half, :] = moved(front_ref[...], scale, product(front_left_ref[:rank, :], right))
    to_back_ref[half:, :] = moved(late_ref[more : more + late, :], scale, product(own_ref[:rank, more : more + late], right))
    to_front_ref[:half, :] = moved(back_ref[...], scale, product(back_left_ref[rank:, :], right))
    start = half - late - more
    ortho = own_ref[rank:, start : start + late]
    to_front_ref[half:, :] = moved(late_ref[more + late : more + 2 * late, :], scale, product(ortho, right))


def cross_kernel(passed, scale_ref, newbasis_ref, back_left_ref, front_left_ref, back_ref, front_ref, _, __, ___, out_ref):
    rank = newbasis_ref.shape[0]
    half = back_left_ref.shape[1]
    count = out_ref.shape[0] // 2
    scale = scale_ref[0:1, 0:1]
    right = right_stack(newbasis_ref[...])
    ortho = back_left_ref[rank:, passed : passed + count]
    out_ref[:count, :] = moved(back_ref[passed : passed + count, :], scale, product(ortho, right))
    start = half - passed - count
    ortho = front_left_ref[:rank, start : start + count]
    out_ref[count:, :] = moved(front_ref[start : start + count, :], scale, product(ortho, right))


def own_kernel(place_ref, scale_ref, newbasis_ref, own_ref, weight_ref, momentum_ref, grads_ref, error_ref, new_error_ref, new_momentum_ref, out_ref):
    del place_ref
    rank, cols = newbasis_ref.shape
    block = weight_ref.shape[0]
    step = pl.program_id(0)
    per = cols // block
    start = (step // per) * rank
    columns = pl.ds(pl.multiple_of((step % per) * block, block), block)
    scale = scale_ref[0:1, 0:1]
    ortho = own_ref[pl.ds(pl.multiple_of(start, rank), rank), columns]
    approx = product(ortho, right_stack(newbasis_ref[...]))
    merged = grads_ref[...].astype(F32) + error_ref[...].astype(F32)
    new_error_ref[...] = (merged - approx).astype(BF16)
    momentum = momentum_ref[...]
    new_momentum_ref[...] = 0.9 * momentum + scale * approx
    out_ref[...] = moved(base_of(weight_ref[...], momentum), scale, approx)


def near_kernel(scale_ref, newbasis_ref, back_left_ref, front_left_ref, back_ref, front_ref, more_back_ref, more_front_ref, came_ref, held_ref, out_ref, done_ref, sems):
    del held_ref
    rank = newbasis_ref.shape[0]
    half = back_left_ref.shape[1]
    more = more_back_ref.shape[0]
    passed = came_ref.shape[0] // 2
    rows = 2 * half
    scale = scale_ref[0:1, 0:1]
    right = right_stack(newbasis_ref[...])
    back_side = beside_index(BACK) * rows
    front_side = beside_index(FRONT) * rows
    copies = []
    start = 0
    for index, (base, ortho, to) in enumerate(
        (
            (back_ref[...], back_left_ref[rank:, :], back_side + half),
            (front_ref[...], front_left_ref[:rank, :], front_side),
            (more_back_ref[...], back_left_ref[:rank, :more], back_side),
            (more_front_ref[...], front_left_ref[rank:, half - more :], front_side + rows - more),
            (came_ref[:passed, :], front_left_ref[rank:, :passed], front_side + half),
            (came_ref[passed:, :], back_left_ref[:rank, half - passed :], back_side + half - passed),
        )
    ):
        size = base.shape[0]
        span = pl.ds(start, size)
        done_ref[span, :] = moved(base, scale, product(ortho, right))
        to = pl.multiple_of(to, 16)
        copy = pltpu.make_async_copy(done_ref.at[span], out_ref.at[pl.ds(to, size)], sems.at[index])
        copy.start()
        copies.append(copy)
        start += size
    for copy in copies:
        copy.wait()


def settle_kernel(more, cross, late, from_back_ref, from_front_ref, cross_ref, held_ref, out_ref, sems):
    del held_ref
    rows = out_ref.shape[0] // lax.axis_size("section")
    half = rows // 2
    back_side = beside_index(BACK) * rows
    front_side = beside_index(FRONT) * rows
    across = (lax.axis_index("section") ^ 3) * rows
    last = rows - more - late
    copies = []
    for ref, start, size, to in (
        (from_back_ref, 0, half, across),
        (from_back_ref, half, late, back_side + more),
        (from_front_ref, 0, half, across + half),
        (from_front_ref, half, late, front_side + last),
        (cross_ref, 0, cross, front_side + last - cross),
        (cross_ref, cross, cross, back_side + more + late),
    ):
        to = pl.multiple_of(to, 16)
        copies.append((ref.at[pl.ds(start, size)], out_ref.at[pl.ds(to, size)]))
    for copy in fetch(copies, sems):
        copy.wait()


def gains_kernel(wide_ref, other_ref, out_ref):
    cols = wide_ref.shape[1]
    first = lax.axis_index("tensor") == 0
    mine = wide_ref[...]
    other = other_ref[...]
    out_ref[:, :cols] = jnp.where(first, mine, other)
    out_ref[:, cols:] = jnp.where(first, other, mine)


def shape(dims, kind=F32):
    return jax.ShapeDtypeStruct(dims, kind)


def call(kernel, name, out_shape, in_specs, **more):
    out_specs = more.pop("out_specs", [WHOLE] * len(out_shape))
    flops = more.pop("flops", 0)
    return pl.pallas_call(
        kernel,
        out_shape=out_shape,
        in_specs=in_specs,
        out_specs=out_specs,
        compiler_params=PARAMS,
        name=name,
        cost_estimate=pl.CostEstimate(flops=flops, bytes_accessed=0, transcendentals=0),
        **more,
    )


def on_device(weight, grads, error, momentum, basis, gram_root, gain, gain_momentum, gain_grads):
    replicas = lax.axis_size("replica")
    tensors = lax.axis_size("tensor")
    sections = lax.axis_size("section")
    rows, cols = weight.shape
    rank = basis.shape[1]
    half = rows // 2
    more = rows * MORE // 64
    passed = rows * PASSED // 64
    cross = rows * CROSS // 64
    late = half - more - passed - cross
    summed = rank * half // LANES
    weight, momentum, grads, error = (hbm(x) for x in (weight, momentum, grads[0], error[0]))

    back, front, late_rows, held_grads, held_error, held_basis, held_gains = call(
        start_kernel,
        "start",
        [pltpu.VMEM((half, cols), F32)] * 2
        + [pltpu.VMEM((2 * (more + late), cols), F32)]
        + [pltpu.VMEM((rows, cols), BF16)] * 2
        + [shape((rank, cols)), shape((2, cols))],
        [IN_HBM] * 6,
        scratch_shapes=[
            pltpu.VMEM((rows, cols), BF16),
            pltpu.VMEM((rows, cols), F32),
            pltpu.SemaphoreType.DMA((2 * BLOCKS + 4,)),
        ],
    )(weight, momentum, grads, error, hbm(basis.T), hbm(gain_grads[0]))
    back = beside(back, BACK)
    front = beside(front, FRONT)

    kept, given = call(
        left_kernel, "left", [shape((summed + 8, LANES)), shape((summed, LANES))], [WHOLE] * 4
    )(held_basis, held_gains, held_grads, held_error)
    (pair,) = call(pair_kernel, "pair", [shape(kept.shape)], [WHOLE] * 2)(kept, swap(given, "tensor", 1))
    parts = partners(pair, "replica")
    mine, gain_mean = call(
        functools.partial(sum_kernel, replicas),
        "sum",
        [shape((summed, LANES)), shape((8, LANES))],
        [WHOLE] * len(parts),
    )(*parts)
    new_gain_momentum, tail = call(gain_kernel, "gain", [shape((2, cols)), shape((8, LANES))], [WHOLE] * 3)(
        gain_mean, gain, gain_momentum
    )

    term, gram, ortho, ortho_half = call(
        right_kernel,
        "right",
        [shape((summed, LANES)), shape((8, LANES)), shape((2 * rank, half)), shape((summed, LANES))],
        [WHOLE] * 5 + [ANYWHERE],
    )(mine, swap(mine, "tensor", 1), gram_root, held_grads, held_error, tail)
    parts = partners(term, "replica")
    joined, long = call(
        functools.partial(middle_kernel, len(parts)),
        "middle",
        [shape((summed + 16, LANES)), shape((2 * summed + 16, LANES))],
        [WHOLE] * (len(parts) + 3) + [ANYWHERE] * 2,
    )(*parts, gram, tail, ortho_half, back, front)
    parts = [swap(joined, "section", 3), swap(long, "section", 2), swap(long, "section", 1), joined]
    more_back, more_front, came = call(
        relay_kernel,
        "relay",
        [shape((more, cols))] * 2 + [shape((2 * passed, cols))],
        [ANYWHERE] + [WHOLE] * 3,
    )(joined, late_rows, back, front)
    more_back = beside(more_back, BACK)
    more_front = beside(more_front, FRONT)
    came = swap(came, "replica", 1)
    (parts[0],) = call(far_kernel, "far", [shape(joined.shape)], [WHOLE], flops=FAR)(parts[0])
    newbasis, gram, mixed, gains = call(
        functools.partial(factor_kernel, replicas),
        "factor",
        [shape((rank, cols)), shape((8, LANES)), shape((2 * summed + 8, LANES)), shape((2, sections * cols))],
        [WHOLE] * len(parts),
    )(*parts)

    entries = rows * cols * tensors * sections
    to_back, to_front, scale, back_left, front_left, where = call(
        functools.partial(after_kernel, entries),
        "after",
        [shape((half + late, cols), BF16)] * 2
        + [shape((8, LANES))]
        + [shape((2 * rank, half))] * 2
        + [shape((1,), jnp.int32)],
        [WHOLE] * 8,
        out_specs=[WHOLE] * 5 + [SCALAR],
    )(newbasis, gram, mixed, swap(mixed, "tensor", 1), ortho, late_rows, back, front)
    late_back = beside(to_back, BACK)
    late_front = beside(to_front, FRONT)
    (to_cross,) = call(
        functools.partial(cross_kernel, passed),
        "cross",
        [shape((2 * cross, cols), BF16)],
        [WHOLE] * 6 + [ANYWHERE] * 3,
    )(scale, newbasis, back_left, front_left, back, front, more_back, more_front, came)
    late_cross = swap(to_cross, "replica", 1)

    blocks = 4
    block = rows // blocks
    step = pl.BlockSpec((block, cols), lambda i, place: (i, 0))
    fixed = [pl.BlockSpec(x.shape, lambda i, place: (0, 0)) for x in (scale, newbasis, ortho)]
    new_error, new_momentum, out = pl.pallas_call(
        own_kernel,
        out_shape=[
            pltpu.HBM((rows, cols), BF16),
            pltpu.HBM((rows, cols), F32),
            pltpu.HBM((sections * rows, cols), BF16),
        ],
        grid_spec=pltpu.PrefetchScalarGridSpec(
            num_scalar_prefetch=1,
            grid=(blocks,),
            in_specs=fixed + [step] * 4,
            out_specs=[step, step, pl.BlockSpec((block, cols), lambda i, place: (place[0] * blocks + i, 0))],
        ),
        compiler_params=PARAMS,
        name="own",
        cost_estimate=pl.CostEstimate(flops=0, bytes_accessed=0, transcendentals=0),
    )(where, scale, newbasis, ortho, weight, momentum, grads, error)
    (out,) = call(
        near_kernel,
        "near",
        [pltpu.HBM(out.shape, BF16)],
        [WHOLE] * 9 + [IN_HBM],
        out_specs=[IN_HBM],
        scratch_shapes=[pltpu.VMEM((2 * (half + more + passed), cols), BF16), pltpu.SemaphoreType.DMA((6,))],
        input_output_aliases={9: 0},
    )(scale, newbasis, back_left, front_left, back, front, more_back, more_front, came, hbm(out))
    (out,) = call(
        functools.partial(settle_kernel, more, cross, late),
        "settle",
        [pltpu.HBM(out.shape, BF16)],
        [WHOLE] * 3 + [IN_HBM],
        out_specs=[IN_HBM],
        scratch_shapes=[pltpu.SemaphoreType.DMA((6,))],
        input_output_aliases={3: 0},
    )(late_back, late_front, late_cross, hbm(out))
    (new_gain,) = call(gains_kernel, "gains", [shape((2, tensors * sections * cols))], [WHOLE] * 2)(
        gains, swap(gains, "tensor", 1)
    )
    return (out, new_error[None], new_momentum, new_gain, new_gain_momentum)


def solution(mesh):
    placed = (
        P("section", "tensor"),
        P("replica", "section", "tensor"),
        P("replica", "section", "tensor"),
        P("section", "tensor"),
        P("tensor", None),
        P(),
        P(None, ("tensor", "section")),
        P(None, ("tensor", "section")),
        P("replica", None, ("tensor", "section")),
    )
    return jax.shard_map(
        on_device,
        mesh=mesh,
        in_specs=placed,
        out_specs=(
            P(None, "tensor"),
            P("replica", "section", "tensor"),
            P("section", "tensor"),
            P(),
            P(None, ("tensor", "section")),
        ),
        check_vma=False,
    )
```

time: 63.9 us -> 59.7 us (0.934)
  waiting for transfers between devices: 24.9 us -> 18.3 us
  starting transfers between devices: 21.3 us -> 24.4 us
  Pallas kernels: 16.7 us -> 16 us
    ppermute x6, waiting for transfers between devices: 6.86 us -> 2.34 us  [beside(): return lax.ppermute(x, ('replica', 'section'), pairs)]
    ppermute x14 -> x15, waiting for transfers between devices: 18.1 us -> 15.9 us  [swap(): return lax.ppermute(x, axis, [(i, i ^ distance) for i in range(count)])]
    ppermute x6, starting transfers between devices: 7.5 us -> 9.46 us  [beside(): return lax.ppermute(x, ('replica', 'section'), pairs)]
    ppermute x14 -> x15, starting transfers between devices: 13.8 us -> 15 us  [swap(): return lax.ppermute(x, axis, [(i, i ^ distance) for i in range(count)])]
    pallas_call x6 -> x9, Pallas kernels: 7.58 us -> 7.78 us  [the longest x1 2.58 us: on_device(): call(start_kernel, 'start', [pltpu.VMEM((half, cols), F32)] * 2 + [pltpu....]
  transfers between devices with their start and end apart: 20 -> 21, of which waited for: 11 -> 13; matrix products, arithmetic and copies ran while one was open for 0% -> 0% of each run, Pallas kernels for 17% -> 21%
where the time goes in v4:
time: 59.7 us; the launch traced here: 59.5 us
  starting transfers between devices  24.4 us (41%)
  waiting for transfers between devices  18.3 us (31%)
  Pallas kernels  16 us (27%)
  between operations  0.79 us (1%)
    ppermute x15, waiting for transfers between devices, swap(): return lax.ppermute(x, axis, [(i, i ^ distance) for i in range(count)])  15.9 us
    ppermute x15, starting transfers between devices, swap(): return lax.ppermute(x, axis, [(i, i ^ distance) for i in range(count)])  15 us
    ppermute x6, starting transfers between devices, beside(): return lax.ppermute(x, ('replica', 'section'), pairs)  9.46 us
    pallas_call x1, Pallas kernels, on_device(): pl.pallas_call(own_kernel, out_shape=[pltpu.HBM((rows, cols), BF16), pltp...  6.09 us
    pallas_call x1, Pallas kernels, on_device(): call(start_kernel, 'start', [pltpu.VMEM((half, cols), F32)] * 2 + [pltpu....  2.58 us
    ppermute x6, waiting for transfers between devices, beside(): return lax.ppermute(x, ('replica', 'section'), pairs)  2.34 us
    pallas_call x1, Pallas kernels, on_device(): call(near_kernel, 'near', [pltpu.HBM(out.shape, BF16)], [WHOLE] * 9 + [IN...  1.52 us
  transfers between devices with their start and end apart: 21, of which 13 were waited for; matrix products, arithmetic and copies ran while one was open for 0% of the time, Pallas kernels for 21%

profile of v4, /device:TPU:0, one launch (start us, length us, event | category | flops | bytes accessed | tf_op | source)
XLA Modules:
  0.0 59.5 jit_solution(7026642218118566086)
XLA Ops:
  0.6 0.0 copy-start.1
  0.6 0.0 copy-start.2
  0.7 0.0 copy-start
  0.7 2.6 %start.1 = (f32[512,512]{1,0:T(8,128)S(1)}, f32[512,512]{1,0:T(8,128)S(1)}, f32[384,512]{1,0:T(8,128)S(1)}, bf16[1024,512]{1,0:T(8,128)(2,1)S(1)}, bf16[1024,512...) custom-call(bf16[1024,512]{1,0:T(8,128)(2,1)} %weight_ref.1, f32[1024,512]{1,0:T(8,128)} %momentum_ref.1, ...), custom_call_target="tpu_custom_call" | custom-call | tf_op jit(solution)/shard_map/start/pallas_call | solution.py:420
  3.3 3.0 %collective-permute-start.8 = (f32[512,512]{1,0:T(8,128)S(1)}, f32[512,512]{1,0:T(8,128)S(1)}, u32[]{:S(2)}, u32[]{:S(2)}) collective-permute-start(f32[512,512]{1,0:T(8,128)S(1)} %get-tuple-element.52), channel_id=1, source_target_pairs={{0,1},{1,0},{2,3},{3,2},{8,10},{9,11},{10,8},{11,9},{16,17},{17,16... | collective-permute-start | bytes 3145736 | tf_op jit(solution)/shard_map/ppermute | solution.py:49
  6.3 1.5 %collective-permute-start.9 = (f32[512,512]{1,0:T(8,128)S(1)}, f32[512,512]{1,0:T(8,128)S(1)}, u32[]{:S(2)}, u32[]{:S(2)}) collective-permute-start(f32[512,512]{1,0:T(8,128)S(1)} %get-tuple-element.53), channel_id=1, source_target_pairs={{0,2},{1,3},{2,0},{3,1},{8,9},{9,8},{10,11},{11,10},{16,18},{17,19... | collective-permute-start | bytes 3145736 | tf_op jit(solution)/shard_map/ppermute | solution.py:49
  7.8 0.7 %left.1 = (f32[136,128]{1,0:T(8,128)S(1)}, f32[128,128]{1,0:T(8,128)S(1)}) custom-call(f32[32,512]{1,0:T(8,128)S(1)} %get-tuple-element.40.basis_ref, f32[2,512]{1,0:T(2,128)S(1)} %get-tuple-element.41.gains_ref, bf16[1024,512]{1,0:T(8,128)(2,1)S(1)} %get-tuple-element.42.grads_ref, bf16[1024,512]{1,0:T(8,128)(2,1)S(1)} %get-tuple-element.43.error_ref), custom_call_target="tpu_custom_call" | custom-call | tf_op jit(solution)/shard_map/left/pallas_call | solution.py:437
  8.5 0.1 collective-permute-start
  8.6 1.2 %collective-permute-done.other_ref = f32[128,128]{1,0:T(8,128)S(1)} collective-permute-done((f32[128,128]{1,0:T(8,128)S(1)}, f32[128,128]{1,0:T(8,128)S(1)}, u32[]{:S(2)}, u32[]{:S(2)}) %collective-permute-start) | collective-permute-done | bytes 65568 | tf_op jit(solution)/shard_map/ppermute | solution.py:34
  9.9 3.7 %collective-permute-start.1 = (f32[136,128]{1,0:T(8,128)S(1)}, f32[136,128]{1,0:T(8,128)S(1)}, u32[]{:S(2)}, u32[]{:S(2)}) collective-permute-start(f32[136,128]{1,0:T(8,128)S(1)} %pair.1.refs_3_), channel_id=1, source_target_pairs={{0,24},{8,16},{16,8},{24,0},{1,25},{9,17},{17,9},{25,1},{2,26},{10... | collective-permute-start | bytes 208904 | tf_op jit(solution)/shard_map/ppermute | solution.py:34
  13.5 0.0 collective-permute-start.2
  13.5 0.8 %collective-permute-start.3 = (f32[136,128]{1,0:T(8,128)S(1)}, f32[136,128]{1,0:T(8,128)S(1)}, u32[]{:S(2)}, u32[]{:S(2)}) collective-permute-start(f32[136,128]{1,0:T(8,128)S(1)} %pair.1.refs_3_), channel_id=1, source_target_pairs={{0,8},{8,0},{16,24},{24,16},{1,9},{9,1},{17,25},{25,17},{2,10},{10... | collective-permute-start | bytes 208904 | tf_op jit(solution)/shard_map/ppermute | solution.py:34
  14.3 2.1 %collective-permute-done.1.refs_0_ = f32[136,128]{1,0:T(8,128)S(1)} collective-permute-done((f32[136,128]{1,0:T(8,128)S(1)}, f32[136,128]{1,0:T(8,128)S(1)}, u32[]{:S(2)}, u32[]{:S(2)}) %collective-permute-start.1) | collective-permute-done | bytes 69664 | tf_op jit(solution)/shard_map/ppermute | solution.py:34
  16.4 3.3 %collective-permute-done.2.refs_1_ = f32[136,128]{1,0:T(8,128)S(1)} collective-permute-done((f32[136,128]{1,0:T(8,128)S(1)}, f32[136,128]{1,0:T(8,128)S(1)}, u32[]{:S(2)}, u32[]{:S(2)}) %collective-permute-start.2) | collective-permute-done | bytes 69664 | tf_op jit(solution)/shard_map/ppermute | solution.py:34
  19.7 0.0 collective-permute-done.3.refs_2_
  19.8 0.1 collective-permute-start.4
  19.8 0.0 copy-done.1
  19.9 0.0 copy-done.2
  19.9 0.6 %gain.1 = (f32[2,512]{1,0:T(2,128)}, f32[8,128]{1,0:T(8,128)S(1)}) custom-call(f32[8,128]{1,0:T(8,128)S(1)} %get-tuple-element.47.mean_ref, f32[2,512]{1,0:T(2,128)S(1)} %copy-done.1, f32[2,512]{1,0:T(2,128)S(1)} %copy-done.2), custom_call_target="tpu_custom_call" | custom-call | tf_op jit(solution)/shard_map/gain/pallas_call | solution.py:448
  20.5 0.6 %collective-permute-done.4.other_ref = f32[128,128]{1,0:T(8,128)S(1)} collective-permute-done((f32[128,128]{1,0:T(8,128)S(1)}, f32[128,128]{1,0:T(8,128)S(1)}, u32[]{:S(2)}, u32[]{:S(2)}) %collective-permute-start.4) | collective-permute-done | bytes 65568 | tf_op jit(solution)/shard_map/ppermute | solution.py:34
  21.1 0.0 copy-done
  21.1 0.8 %right.1 = (f32[128,128]{1,0:T(8,128)S(1)}, f32[8,128]{1,0:T(8,128)S(1)}, f32[64,512]{1,0:T(8,128)S(1)}, f32[128,128]{1,0:T(8,128)S(1)}) custom-call(f32[128,128]{1,0:T(8,128)S(1)} %get-tuple-element.46.mine_ref, f32[128,128]{1,0:T(8,128)S(1)} %collective-permute-done.4.other_ref, f32[32,32]{1,0:T(8,128)S(1)} %copy-done, ...), custom_call_target="tpu_custom_call" | custom-call | tf_op jit(solution)/shard_map/right/pallas_call | solution.py:452
  21.9 2.5 %collective-permute-start.5 = (f32[128,128]{1,0:T(8,128)S(1)}, f32[128,128]{1,0:T(8,128)S(1)}, u32[]{:S(2)}, u32[]{:S(2)}) collective-permute-start(f32[128,128]{1,0:T(8,128)S(1)} %get-tuple-element.49.refs_3_), channel_id=1, source_target_pairs={{0,24},{8,16},{16,8},{24,0},{1,25},{9,17},{17,9},{25,1},{2,26},{10... | collective-permute-start | bytes 196616 | tf_op jit(solution)/shard_map/ppermute | solution.py:34
  24.4 0.1 collective-permute-start.6
  24.5 1.9 %collective-permute-start.7 = (f32[128,128]{1,0:T(8,128)S(1)}, f32[128,128]{1,0:T(8,128)S(1)}, u32[]{:S(2)}, u32[]{:S(2)}) collective-permute-start(f32[128,128]{1,0:T(8,128)S(1)} %get-tuple-element.49.refs_3_), channel_id=1, source_target_pairs={{0,8},{8,0},{16,24},{24,16},{1,9},{9,1},{17,25},{25,17},{2,10},{10... | collective-permute-start | bytes 196616 | tf_op jit(solution)/shard_map/ppermute | solution.py:34
  26.3 2.4 %collective-permute-done.5.refs_0_ = f32[128,128]{1,0:T(8,128)S(1)} collective-permute-done((f32[128,128]{1,0:T(8,128)S(1)}, f32[128,128]{1,0:T(8,128)S(1)}, u32[]{:S(2)}, u32[]{:S(2)}) %collective-permute-start.5) | collective-permute-done | bytes 65568 | tf_op jit(solution)/shard_map/ppermute | solution.py:34
  28.7 2.2 %collective-permute-done.6.refs_1_ = f32[128,128]{1,0:T(8,128)S(1)} collective-permute-done((f32[128,128]{1,0:T(8,128)S(1)}, f32[128,128]{1,0:T(8,128)S(1)}, u32[]{:S(2)}, u32[]{:S(2)}) %collective-permute-start.6) | collective-permute-done | bytes 65568 | tf_op jit(solution)/shard_map/ppermute | solution.py:34
  30.9 0.0 collective-permute-done.7.refs_2_
  30.9 0.0 collective-permute-done.8.refs_7_.back_ref
  30.9 0.0 collective-permute-done.9.refs_8_.front_ref
  31.0 1.5 %collective-permute-start.10 = (f32[144,128]{1,0:T(8,128)S(1)}, f32[144,128]{1,0:T(8,128)S(1)}, u32[]{:S(2)}, u32[]{:S(2)}) collective-permute-start(f32[144,128]{1,0:T(8,128)S(1)} %get-tuple-element.54.refs_3_._), channel_id=1, source_target_pairs={{0,3},{1,2},{2,1},{3,0},{4,7},{5,6},{6,5},{7,4},{8,11},{9,10},{10,... | collective-permute-start | bytes 221192 | tf_op jit(solution)/shard_map/ppermute | solution.py:34
  32.5 0.6 collective-permute-start.11
  33.0 1.5 %collective-permute-start.12 = (f32[272,128]{1,0:T(8,128)S(1)}, f32[272,128]{1,0:T(8,128)S(1)}, u32[]{:S(2)}, u32[]{:S(2)}) collective-permute-start(f32[272,128]{1,0:T(8,128)S(1)} %get-tuple-element.55), channel_id=1, source_target_pairs={{0,1},{1,0},{2,3},{3,2},{4,5},{5,4},{6,7},{7,6},{8,9},{9,8},{10,11... | collective-permute-start | bytes 417800 | tf_op jit(solution)/shard_map/ppermute | solution.py:34
  34.5 0.1 relay.1
  34.6 1.6 %collective-permute-start.18 = (f32[192,512]{1,0:T(8,128)S(1)}, f32[192,512]{1,0:T(8,128)S(1)}, u32[]{:S(2)}, u32[]{:S(2)}) collective-permute-start(f32[192,512]{1,0:T(8,128)S(1)} %get-tuple-element.68), channel_id=1, source_target_pairs={{0,8},{8,0},{16,24},{24,16},{1,9},{9,1},{17,25},{25,17},{2,10},{10... | collective-permute-start | bytes 1179656 | tf_op jit(solution)/shard_map/ppermute | solution.py:34
  36.2 1.5 %collective-permute-start.16 = (f32[160,512]{1,0:T(8,128)S(1)}, f32[160,512]{1,0:T(8,128)S(1)}, u32[]{:S(2)}, u32[]{:S(2)}) collective-permute-start(f32[160,512]{1,0:T(8,128)S(1)} %get-tuple-element.66), channel_id=1, source_target_pairs={{0,1},{1,0},{2,3},{3,2},{8,10},{9,11},{10,8},{11,9},{16,17},{17,16... | collective-permute-start | bytes 983048 | tf_op jit(solution)/shard_map/ppermute | solution.py:49
  37.7 0.0 collective-permute-done.10.in_ref
  37.7 0.8 %collective-permute-start.17 = (f32[160,512]{1,0:T(8,128)S(1)}, f32[160,512]{1,0:T(8,128)S(1)}, u32[]{:S(2)}, u32[]{:S(2)}) collective-permute-start(f32[160,512]{1,0:T(8,128)S(1)} %get-tuple-element.67), channel_id=1, source_target_pairs={{0,2},{1,3},{2,0},{3,1},{8,9},{9,8},{10,11},{11,10},{16,18},{17,19... | collective-permute-start | bytes 983048 | tf_op jit(solution)/shard_map/ppermute | solution.py:49
  38.5 0.5 collective-permute-done.11.refs_1_
  38.9 1.1 %collective-permute-done.12.refs_2_ = f32[272,128]{1,0:T(8,128)S(1)} collective-permute-done((f32[272,128]{1,0:T(8,128)S(1)}, f32[272,128]{1,0:T(8,128)S(1)}, u32[]{:S(2)}, u32[]{:S(2)}) %collective-permute-start.12) | collective-permute-done | bytes 139296 | tf_op jit(solution)/shard_map/ppermute | solution.py:34
  40.0 0.3 factor.1
  40.3 0.1 collective-permute-start.13
  40.4 1.3 %collective-permute-done.13.other_ref = f32[264,128]{1,0:T(8,128)S(1)} collective-permute-done((f32[264,128]{1,0:T(8,128)S(1)}, f32[264,128]{1,0:T(8,128)S(1)}, u32[]{:S(2)}, u32[]{:S(2)}) %collective-permute-start.13) | collective-permute-done | bytes 135200 | tf_op jit(solution)/shard_map/ppermute | solution.py:34
  41.7 0.9 %after.1 = (bf16[544,512]{1,0:T(8,128)(2,1)S(1)}, bf16[544,512]{1,0:T(8,128)(2,1)S(1)}, f32[8,128]{1,0:T(8,128)S(1)}, f32[64,512]{1,0:T(8,128)S(1)}, f32[64,512]{1,0:T(8,128)S(1)}, /*index=5*/s32[1]{0:T(128)}) custom-call(f32[32,512]{1,0:T(8,128)S(1)} %get-tuple-element.56.newbasis_ref, f32[8,128]{1,0:T(8,128)S(1)} %get-tuple-element.57.gram_ref, ...), custom_call_target="tpu_custom_call" | custom-call | tf_op jit(solution)/shard_map/after/pallas_call | solution.py:484
  42.6 1.2 %collective-permute-start.14 = (bf16[544,512]{1,0:T(8,128)(2,1)S(1)}, bf16[544,512]{1,0:T(8,128)(2,1)S(1)}, u32[]{:S(2)}, u32[]{:S(2)}) collective-permute-start(bf16[544,512]{1,0:T(8,128)(2,1)S(1)} %get-tuple-element.61), channel_id=1, source_target_pairs={{0,1},{1,0},{2,3},{3,2},{8,10},{9,11},{10,8},{11,9},{16,17},{17,16... | collective-permute-start | bytes 1671176 | tf_op jit(solution)/shard_map/ppermute | solution.py:49
  43.9 1.5 %collective-permute-start.15 = (bf16[544,512]{1,0:T(8,128)(2,1)S(1)}, bf16[544,512]{1,0:T(8,128)(2,1)S(1)}, u32[]{:S(2)}, u32[]{:S(2)}) collective-permute-start(bf16[544,512]{1,0:T(8,128)(2,1)S(1)} %get-tuple-element.62), channel_id=1, source_target_pairs={{0,2},{1,3},{2,0},{3,1},{8,9},{9,8},{10,11},{11,10},{16,18},{17,19... | collective-permute-start | bytes 1671176 | tf_op jit(solution)/shard_map/ppermute | solution.py:49
  45.3 0.9 %collective-permute-done.16._.more_back_ref = f32[160,512]{1,0:T(8,128)S(1)} collective-permute-done((f32[160,512]{1,0:T(8,128)S(1)}, f32[160,512]{1,0:T(8,128)S(1)}, u32[]{:S(2)}, u32[]{:S(2)}) %collective-permute-start.16) | collective-permute-done | bytes 327712 | tf_op jit(solution)/shard_map/ppermute | solution.py:49
  46.3 0.0 collective-permute-done.17.__.more_front_ref
  46.3 0.0 collective-permute-done.18.___.came_ref
  46.3 0.5 cross.1
  46.8 0.7 %collective-permute-start.19 = (bf16[448,512]{1,0:T(8,128)(2,1)S(1)}, bf16[448,512]{1,0:T(8,128)(2,1)S(1)}, u32[]{:S(2)}, u32[]{:S(2)}) collective-permute-start(bf16[448,512]{1,0:T(8,128)(2,1)S(1)} %cross.1), channel_id=1, source_target_pairs={{0,8},{8,0},{16,24},{24,16},{1,9},{9,1},{17,25},{25,17},{2,10},{10... | collective-permute-start | bytes 1376264 | tf_op jit(solution)/shard_map/ppermute | solution.py:34
  47.5 0.0 collective-permute-start.20
  47.5 1.2 %collective-permute-done.20.other_ref = f32[2,2048]{1,0:T(2,128)S(1)} collective-permute-done((f32[2,2048]{1,0:T(2,128)S(1)}, f32[2,2048]{1,0:T(2,128)S(1)}, u32[]{:S(2)}, u32[]{:S(2)}) %collective-permute-start.20) | collective-permute-done | bytes 16416 | tf_op jit(solution)/shard_map/ppermute | solution.py:34
  48.7 0.6 %gains.1 = f32[2,4096]{1,0:T(2,128)} custom-call(f32[2,2048]{1,0:T(2,128)S(1)} %get-tuple-element.73.wide_ref, f32[2,2048]{1,0:T(2,128)S(1)} %collective-permute-done.20.other_ref), custom_call_target="tpu_custom_call" | custom-call | tf_op jit(solution)/shard_map/gains/pallas_call | solution.py:543
  49.3 6.1 %own.1 = (bf16[1024,512]{1,0:T(8,128)(2,1)}, f32[1024,512]{1,0:T(8,128)}, bf16[4096,512]{1,0:T(8,128)(2,1)}) custom-call(s32[1]{0:T(128)} %get-tuple-element.69.place_ref, f32[8,128]{1,0:T(8,128)S(1)} %get-tuple-element.63.scale_ref, f32[32,512]{1,0:T(8,128)S(1)} %get-tuple-element.56.newbasis_ref, f32[64,512]{1,0:T(8,128)S(1)} %get-tuple-element.59.own_ref, ...), custom_call_target="tpu_custom_call" | custom-call | tf_op jit(solution)/shard_map/own/pallas_call | solution.py:508
  55.4 1.5 %near.1.held_ref = bf16[4096,512]{1,0:T(8,128)(2,1)} custom-call(f32[8,128]{1,0:T(8,128)S(1)} %get-tuple-element.63.scale_ref, f32[32,512]{1,0:T(8,128)S(1)} %get-tuple-element.56.newbasis_ref, f32[64,512]{1,0:T(8,128)S(1)} %get-tuple-element.64.back_left_ref, f32[64,512]{1,0:T(8,128)S(1)} %get-tuple-element.65.front_left_ref, ...), custom_call_target="tpu_custom_call", output_to_operand_aliasing={{}: (9, {})} | custom-call | tf_op jit(solution)/shard_map/near/pallas_call | solution.py:525
  56.9 0.9 %collective-permute-done.14.from_back_ref = bf16[544,512]{1,0:T(8,128)(2,1)S(1)} collective-permute-done((bf16[544,512]{1,0:T(8,128)(2,1)S(1)}, bf16[544,512]{1,0:T(8,128)(2,1)S(1)}, u32[]{:S(2)}, u32[]{:S(2)}) %collective-permute-start.14) | collective-permute-done | bytes 557088 | tf_op jit(solution)/shard_map/ppermute | solution.py:49
  57.8 0.4 collective-permute-done.15.from_front_ref
  58.3 0.0 collective-permute-done.19.cross_ref
  58.3 1.2 %settle.1 = bf16[4096,512]{1,0:T(8,128)(2,1)} custom-call(bf16[544,512]{1,0:T(8,128)(2,1)S(1)} %collective-permute-done.14.from_back_ref, bf16[544,512]{1,0:T(8,128)(2,1)S(1)} %collective-permute-done.15.from_front_ref, bf16[448,512]{1,0:T(8,128)(2,1)S(1)} %collective-permute-done.19.cross_ref, ...), custom_call_target="tpu_custom_call", output_to_operand_aliasing={{}: (3, {})} | custom-call | tf_op jit(solution)/shard_map/settle/pallas_call | solution.py:534
  (4 shorter events, 0.1 us)
Async XLA Ops:
  0.6 19.2 %copy-start.1 = (f32[2,512]{1,0:T(2,128)S(1)}, f32[2,512]{1,0:T(2,128)}, u32[]{:S(2)}) copy-start(f32[2,512]{1,0:T(2,128)} %gain_ref.1) | copy-start | bytes 12292
  0.6 19.2 %copy-start.2 = (f32[2,512]{1,0:T(2,128)S(1)}, f32[2,512]{1,0:T(2,128)}, u32[]{:S(2)}) copy-start(f32[2,512]{1,0:T(2,128)} %gain_momentum_ref.1) | copy-start | bytes 12292
  0.7 20.4 %copy-start = (f32[32,32]{1,0:T(8,128)S(1)}, f32[32,32]{1,0:T(8,128)}, u32[]{:S(2)}) copy-start(f32[32,32]{1,0:T(8,128)} %root_ref.1) | copy-start | bytes 12292
  3.3 27.7 %collective-permute-start.8 = (f32[512,512]{1,0:T(8,128)S(1)}, f32[512,512]{1,0:T(8,128)S(1)}, u32[]{:S(2)}, u32[]{:S(2)}) collective-permute-start(f32[512,512]{1,0:T(8,128)S(1)} %get-tuple-element.52), channel_id=1, source_target_pairs={{0,1},{1,0},{2,3},{3,2},{8,10},{9,11},{10,8},{11,9},{16,17},{17,16... | collective-permute-start | bytes 3145736 | tf_op jit(solution)/shard_map/ppermute | solution.py:49
  6.3 24.7 %collective-permute-start.9 = (f32[512,512]{1,0:T(8,128)S(1)}, f32[512,512]{1,0:T(8,128)S(1)}, u32[]{:S(2)}, u32[]{:S(2)}) collective-permute-start(f32[512,512]{1,0:T(8,128)S(1)} %get-tuple-element.53), channel_id=1, source_target_pairs={{0,2},{1,3},{2,0},{3,1},{8,9},{9,8},{10,11},{11,10},{16,18},{17,19... | collective-permute-start | bytes 3145736 | tf_op jit(solution)/shard_map/ppermute | solution.py:49
  8.5 1.3 %collective-permute-start = (f32[128,128]{1,0:T(8,128)S(1)}, f32[128,128]{1,0:T(8,128)S(1)}, u32[]{:S(2)}, u32[]{:S(2)}) collective-permute-start(f32[128,128]{1,0:T(8,128)S(1)} %get-tuple-element.45), channel_id=1, source_target_pairs={{0,4},{4,0},{1,5},{5,1},{2,6},{6,2},{3,7},{7,3},{8,12},{12,8},{9,1... | collective-permute-start | bytes 196616 | tf_op jit(solution)/shard_map/ppermute | solution.py:34
  9.9 6.5 %collective-permute-start.1 = (f32[136,128]{1,0:T(8,128)S(1)}, f32[136,128]{1,0:T(8,128)S(1)}, u32[]{:S(2)}, u32[]{:S(2)}) collective-permute-start(f32[136,128]{1,0:T(8,128)S(1)} %pair.1.refs_3_), channel_id=1, source_target_pairs={{0,24},{8,16},{16,8},{24,0},{1,25},{9,17},{17,9},{25,1},{2,26},{10... | collective-permute-start | bytes 208904 | tf_op jit(solution)/shard_map/ppermute | solution.py:34
  13.5 6.2 %collective-permute-start.2 = (f32[136,128]{1,0:T(8,128)S(1)}, f32[136,128]{1,0:T(8,128)S(1)}, u32[]{:S(2)}, u32[]{:S(2)}) collective-permute-start(f32[136,128]{1,0:T(8,128)S(1)} %pair.1.refs_3_), channel_id=1, source_target_pairs={{0,16},{8,24},{16,0},{24,8},{1,17},{9,25},{17,1},{25,9},{2,18},{10... | collective-permute-start | bytes 208904 | tf_op jit(solution)/shard_map/ppermute | solution.py:34
  13.5 6.2 %collective-permute-start.3 = (f32[136,128]{1,0:T(8,128)S(1)}, f32[136,128]{1,0:T(8,128)S(1)}, u32[]{:S(2)}, u32[]{:S(2)}) collective-permute-start(f32[136,128]{1,0:T(8,128)S(1)} %pair.1.refs_3_), channel_id=1, source_target_pairs={{0,8},{8,0},{16,24},{24,16},{1,9},{9,1},{17,25},{25,17},{2,10},{10... | collective-permute-start | bytes 208904 | tf_op jit(solution)/shard_map/ppermute | solution.py:34
  19.8 1.3 %collective-permute-start.4 = (f32[128,128]{1,0:T(8,128)S(1)}, f32[128,128]{1,0:T(8,128)S(1)}, u32[]{:S(2)}, u32[]{:S(2)}) collective-permute-start(f32[128,128]{1,0:T(8,128)S(1)} %get-tuple-element.46.mine_ref), channel_id=1, source_target_pairs={{0,4},{4,0},{1,5},{5,1},{2,6},{6,2},{3,7},{7,3},{8,12},{12,8},{9,1... | collective-permute-start | bytes 196616 | tf_op jit(solution)/shard_map/ppermute | solution.py:34
  21.9 6.8 %collective-permute-start.5 = (f32[128,128]{1,0:T(8,128)S(1)}, f32[128,128]{1,0:T(8,128)S(1)}, u32[]{:S(2)}, u32[]{:S(2)}) collective-permute-start(f32[128,128]{1,0:T(8,128)S(1)} %get-tuple-element.49.refs_3_), channel_id=1, source_target_pairs={{0,24},{8,16},{16,8},{24,0},{1,25},{9,17},{17,9},{25,1},{2,26},{10... | collective-permute-start | bytes 196616 | tf_op jit(solution)/shard_map/ppermute | solution.py:34
  24.4 6.5 %collective-permute-start.6 = (f32[128,128]{1,0:T(8,128)S(1)}, f32[128,128]{1,0:T(8,128)S(1)}, u32[]{:S(2)}, u32[]{:S(2)}) collective-permute-start(f32[128,128]{1,0:T(8,128)S(1)} %get-tuple-element.49.refs_3_), channel_id=1, source_target_pairs={{0,16},{8,24},{16,0},{24,8},{1,17},{9,25},{17,1},{25,9},{2,18},{10... | collective-permute-start | bytes 196616 | tf_op jit(solution)/shard_map/ppermute | solution.py:34
  24.5 6.5 %collective-permute-start.7 = (f32[128,128]{1,0:T(8,128)S(1)}, f32[128,128]{1,0:T(8,128)S(1)}, u32[]{:S(2)}, u32[]{:S(2)}) collective-permute-start(f32[128,128]{1,0:T(8,128)S(1)} %get-tuple-element.49.refs_3_), channel_id=1, source_target_pairs={{0,8},{8,0},{16,24},{24,16},{1,9},{9,1},{17,25},{25,17},{2,10},{10... | collective-permute-start | bytes 196616 | tf_op jit(solution)/shard_map/ppermute | solution.py:34
  31.0 6.7 %collective-permute-start.10 = (f32[144,128]{1,0:T(8,128)S(1)}, f32[144,128]{1,0:T(8,128)S(1)}, u32[]{:S(2)}, u32[]{:S(2)}) collective-permute-start(f32[144,128]{1,0:T(8,128)S(1)} %get-tuple-element.54.refs_3_._), channel_id=1, source_target_pairs={{0,3},{1,2},{2,1},{3,0},{4,7},{5,6},{6,5},{7,4},{8,11},{9,10},{10,... | collective-permute-start | bytes 221192 | tf_op jit(solution)/shard_map/ppermute | solution.py:34
  32.5 6.4 %collective-permute-start.11 = (f32[272,128]{1,0:T(8,128)S(1)}, f32[272,128]{1,0:T(8,128)S(1)}, u32[]{:S(2)}, u32[]{:S(2)}) collective-permute-start(f32[272,128]{1,0:T(8,128)S(1)} %get-tuple-element.55), channel_id=1, source_target_pairs={{0,2},{1,3},{2,0},{3,1},{4,6},{5,7},{6,4},{7,5},{8,10},{9,11},{10,... | collective-permute-start | bytes 417800 | tf_op jit(solution)/shard_map/ppermute | solution.py:34
  33.0 6.9 %collective-permute-start.12 = (f32[272,128]{1,0:T(8,128)S(1)}, f32[272,128]{1,0:T(8,128)S(1)}, u32[]{:S(2)}, u32[]{:S(2)}) collective-permute-start(f32[272,128]{1,0:T(8,128)S(1)} %get-tuple-element.55), channel_id=1, source_target_pairs={{0,1},{1,0},{2,3},{3,2},{4,5},{5,4},{6,7},{7,6},{8,9},{9,8},{10,11... | collective-permute-start | bytes 417800 | tf_op jit(solution)/shard_map/ppermute | solution.py:34
  34.6 11.7 %collective-permute-start.18 = (f32[192,512]{1,0:T(8,128)S(1)}, f32[192,512]{1,0:T(8,128)S(1)}, u32[]{:S(2)}, u32[]{:S(2)}) collective-permute-start(f32[192,512]{1,0:T(8,128)S(1)} %get-tuple-element.68), channel_id=1, source_target_pairs={{0,8},{8,0},{16,24},{24,16},{1,9},{9,1},{17,25},{25,17},{2,10},{10... | collective-permute-start | bytes 1179656 | tf_op jit(solution)/shard_map/ppermute | solution.py:34
  36.2 10.1 %collective-permute-start.16 = (f32[160,512]{1,0:T(8,128)S(1)}, f32[160,512]{1,0:T(8,128)S(1)}, u32[]{:S(2)}, u32[]{:S(2)}) collective-permute-start(f32[160,512]{1,0:T(8,128)S(1)} %get-tuple-element.66), channel_id=1, source_target_pairs={{0,1},{1,0},{2,3},{3,2},{8,10},{9,11},{10,8},{11,9},{16,17},{17,16... | collective-permute-start | bytes 983048 | tf_op jit(solution)/shard_map/ppermute | solution.py:49
  37.7 8.6 %collective-permute-start.17 = (f32[160,512]{1,0:T(8,128)S(1)}, f32[160,512]{1,0:T(8,128)S(1)}, u32[]{:S(2)}, u32[]{:S(2)}) collective-permute-start(f32[160,512]{1,0:T(8,128)S(1)} %get-tuple-element.67), channel_id=1, source_target_pairs={{0,2},{1,3},{2,0},{3,1},{8,9},{9,8},{10,11},{11,10},{16,18},{17,19... | collective-permute-start | bytes 983048 | tf_op jit(solution)/shard_map/ppermute | solution.py:49
  40.3 1.4 %collective-permute-start.13 = (f32[264,128]{1,0:T(8,128)S(1)}, f32[264,128]{1,0:T(8,128)S(1)}, u32[]{:S(2)}, u32[]{:S(2)}) collective-permute-start(f32[264,128]{1,0:T(8,128)S(1)} %get-tuple-element.58.mine_ref), channel_id=1, source_target_pairs={{0,4},{4,0},{1,5},{5,1},{2,6},{6,2},{3,7},{7,3},{8,12},{12,8},{9,1... | collective-permute-start | bytes 405512 | tf_op jit(solution)/shard_map/ppermute | solution.py:34
  42.6 15.2 %collective-permute-start.14 = (bf16[544,512]{1,0:T(8,128)(2,1)S(1)}, bf16[544,512]{1,0:T(8,128)(2,1)S(1)}, u32[]{:S(2)}, u32[]{:S(2)}) collective-permute-start(bf16[544,512]{1,0:T(8,128)(2,1)S(1)} %get-tuple-element.61), channel_id=1, source_target_pairs={{0,1},{1,0},{2,3},{3,2},{8,10},{9,11},{10,8},{11,9},{16,17},{17,16... | collective-permute-start | bytes 1671176 | tf_op jit(solution)/shard_map/ppermute | solution.py:49
  43.9 14.4 %collective-permute-start.15 = (bf16[544,512]{1,0:T(8,128)(2,1)S(1)}, bf16[544,512]{1,0:T(8,128)(2,1)S(1)}, u32[]{:S(2)}, u32[]{:S(2)}) collective-permute-start(bf16[544,512]{1,0:T(8,128)(2,1)S(1)} %get-tuple-element.62), channel_id=1, source_target_pairs={{0,2},{1,3},{2,0},{3,1},{8,9},{9,8},{10,11},{11,10},{16,18},{17,19... | collective-permute-start | bytes 1671176 | tf_op jit(solution)/shard_map/ppermute | solution.py:49
  46.8 11.5 %collective-permute-start.19 = (bf16[448,512]{1,0:T(8,128)(2,1)S(1)}, bf16[448,512]{1,0:T(8,128)(2,1)S(1)}, u32[]{:S(2)}, u32[]{:S(2)}) collective-permute-start(bf16[448,512]{1,0:T(8,128)(2,1)S(1)} %cross.1), channel_id=1, source_target_pairs={{0,8},{8,0},{16,24},{24,16},{1,9},{9,1},{17,25},{25,17},{2,10},{10... | collective-permute-start | bytes 1376264 | tf_op jit(solution)/shard_map/ppermute | solution.py:34
  47.5 1.2 %collective-permute-start.20 = (f32[2,2048]{1,0:T(2,128)S(1)}, f32[2,2048]{1,0:T(2,128)S(1)}, u32[]{:S(2)}, u32[]{:S(2)}) collective-permute-start(f32[2,2048]{1,0:T(2,128)S(1)} %get-tuple-element.73.wide_ref), channel_id=1, source_target_pairs={{0,4},{4,0},{1,5},{5,1},{2,6},{6,2},{3,7},{7,3},{8,12},{12,8},{9,1... | collective-permute-start | bytes 49160 | tf_op jit(solution)/shard_map/ppermute | solution.py:34

commit v5 on v4

--- a/solution.py
+++ b/solution.py
@@ -12,8 +12,8 @@
 BF16 = jnp.bfloat16
 KEEP = 0.05 * 0.9 * 0.9
 MOVE = 0.05 * (1.0 + 0.9)
-MORE = 10
-PASSED = 6
+MORE = 9
+PASSED = 7
 CROSS = 14
 BLOCKS = 2
 LANES = 128
@@ -215,7 +215,7 @@
 
 
 def middle_kernel(count, *refs):
-    parts, (gram_ref, tail_ref, ortho_ref, _, _, out_ref, long_ref) = refs[:count], refs[count:]
+    parts, (gram_ref, tail_ref, ortho_ref, out_ref, long_ref) = refs[:count], refs[count:]
     joined = jnp.concatenate([added([part[...] for part in parts]), gram_ref[...], tail_ref[...]], axis=0)
     out_ref[...] = joined
     long_ref[: joined.shape[0], :] = joined
@@ -460,8 +460,8 @@
         functools.partial(middle_kernel, len(parts)),
         "middle",
         [shape((summed + 16, LANES)), shape((2 * summed + 16, LANES))],
-        [WHOLE] * (len(parts) + 3) + [ANYWHERE] * 2,
-    )(*parts, gram, tail, ortho_half, back, front)
+        [WHOLE] * (len(parts) + 3),
+    )(*parts, gram, tail, ortho_half)
     parts = [swap(joined, "section", 3), swap(long, "section", 2), swap(long, "section", 1), joined]
     more_back, more_front, came = call(
         relay_kernel,

time: 59.7 us -> 58.9 us (0.987)
  starting transfers between devices: 24.4 us -> 21 us
  waiting for transfers between devices: 18.3 us -> 20.9 us
    ppermute x15, waiting for transfers between devices: 15.9 us -> 19 us  [swap(): return lax.ppermute(x, axis, [(i, i ^ distance) for i in range(count)])]
    ppermute x6, starting transfers between devices: 9.46 us -> 7.44 us  [beside(): return lax.ppermute(x, ('replica', 'section'), pairs)]
    ppermute x15, starting transfers between devices: 15 us -> 13.5 us  [swap(): return lax.ppermute(x, axis, [(i, i ^ distance) for i in range(count)])]
  transfers between devices with their start and end apart: 21 -> 21, of which waited for: 13 -> 17; matrix products, arithmetic and copies ran while one was open for 0% -> 0% of each run, Pallas kernels for 21% -> 21%
where the time goes in v5:
time: 58.9 us; the launch traced here: 58.7 us
  starting transfers between devices  21 us (36%)
  waiting for transfers between devices  20.9 us (35%)
  Pallas kernels  16 us (27%)
  between operations  0.78 us (1%)
    ppermute x15, waiting for transfers between devices, swap(): return lax.ppermute(x, axis, [(i, i ^ distance) for i in range(count)])  19 us
    ppermute x15, starting transfers between devices, swap(): return lax.ppermute(x, axis, [(i, i ^ distance) for i in range(count)])  13.5 us
    ppermute x6, starting transfers between devices, beside(): return lax.ppermute(x, ('replica', 'section'), pairs)  7.44 us
    pallas_call x1, Pallas kernels, on_device(): pl.pallas_call(own_kernel, out_shape=[pltpu.HBM((rows, cols), BF16), pltp...  6.09 us
    pallas_call x1, Pallas kernels, on_device(): call(start_kernel, 'start', [pltpu.VMEM((half, cols), F32)] * 2 + [pltpu....  2.58 us
    ppermute x6, waiting for transfers between devices, beside(): return lax.ppermute(x, ('replica', 'section'), pairs)  1.91 us
    pallas_call x1, Pallas kernels, on_device(): call(near_kernel, 'near', [pltpu.HBM(out.shape, BF16)], [WHOLE] * 9 + [IN...  1.54 us
    pallas_call x1, Pallas kernels, on_device(): call(functools.partial(settle_kernel, more, cross, late), 'settle', [pltp...  1.18 us
  transfers between devices with their start and end apart: 21, of which 17 were waited for; matrix products, arithmetic and copies ran while one was open for 0% of the time, Pallas kernels for 21%

profile of v5, /device:TPU:0, one launch (start us, length us, event | category | flops | bytes accessed | tf_op | source)
XLA Modules:
  0.0 58.7 jit_solution(15773842298279292179)
XLA Ops:
  0.6 0.0 copy-start.1
  0.6 0.0 copy-start.2
  0.7 0.0 copy-start
  0.7 2.6 %start.1 = (f32[512,512]{1,0:T(8,128)S(1)}, f32[512,512]{1,0:T(8,128)S(1)}, f32[352,512]{1,0:T(8,128)S(1)}, bf16[1024,512]{1,0:T(8,128)(2,1)S(1)}, bf16[1024,512...) custom-call(bf16[1024,512]{1,0:T(8,128)(2,1)} %weight_ref.1, f32[1024,512]{1,0:T(8,128)} %momentum_ref.1, ...), custom_call_target="tpu_custom_call" | custom-call | tf_op jit(solution)/shard_map/start/pallas_call | solution.py:420
  3.3 3.0 %collective-permute-start.12 = (f32[512,512]{1,0:T(8,128)S(1)}, f32[512,512]{1,0:T(8,128)S(1)}, u32[]{:S(2)}, u32[]{:S(2)}) collective-permute-start(f32[512,512]{1,0:T(8,128)S(1)} %get-tuple-element.59), channel_id=1, source_target_pairs={{0,1},{1,0},{2,3},{3,2},{8,10},{9,11},{10,8},{11,9},{16,17},{17,16... | collective-permute-start | bytes 3145736 | tf_op jit(solution)/shard_map/ppermute | solution.py:49
  6.3 1.5 %collective-permute-start.13 = (f32[512,512]{1,0:T(8,128)S(1)}, f32[512,512]{1,0:T(8,128)S(1)}, u32[]{:S(2)}, u32[]{:S(2)}) collective-permute-start(f32[512,512]{1,0:T(8,128)S(1)} %get-tuple-element.60), channel_id=1, source_target_pairs={{0,2},{1,3},{2,0},{3,1},{8,9},{9,8},{10,11},{11,10},{16,18},{17,19... | collective-permute-start | bytes 3145736 | tf_op jit(solution)/shard_map/ppermute | solution.py:49
  7.8 0.7 %left.1 = (f32[136,128]{1,0:T(8,128)S(1)}, f32[128,128]{1,0:T(8,128)S(1)}) custom-call(f32[32,512]{1,0:T(8,128)S(1)} %get-tuple-element.40.basis_ref, f32[2,512]{1,0:T(2,128)S(1)} %get-tuple-element.41.gains_ref, bf16[1024,512]{1,0:T(8,128)(2,1)S(1)} %get-tuple-element.42.grads_ref, bf16[1024,512]{1,0:T(8,128)(2,1)S(1)} %get-tuple-element.43.error_ref), custom_call_target="tpu_custom_call" | custom-call | tf_op jit(solution)/shard_map/left/pallas_call | solution.py:437
  8.5 0.1 collective-permute-start
  8.6 1.2 %collective-permute-done.other_ref = f32[128,128]{1,0:T(8,128)S(1)} collective-permute-done((f32[128,128]{1,0:T(8,128)S(1)}, f32[128,128]{1,0:T(8,128)S(1)}, u32[]{:S(2)}, u32[]{:S(2)}) %collective-permute-start) | collective-permute-done | bytes 65568 | tf_op jit(solution)/shard_map/ppermute | solution.py:34
  9.9 3.7 %collective-permute-start.1 = (f32[136,128]{1,0:T(8,128)S(1)}, f32[136,128]{1,0:T(8,128)S(1)}, u32[]{:S(2)}, u32[]{:S(2)}) collective-permute-start(f32[136,128]{1,0:T(8,128)S(1)} %pair.1.refs_3_), channel_id=1, source_target_pairs={{0,24},{8,16},{16,8},{24,0},{1,25},{9,17},{17,9},{25,1},{2,26},{10... | collective-permute-start | bytes 208904 | tf_op jit(solution)/shard_map/ppermute | solution.py:34
  13.5 0.0 collective-permute-start.2
  13.5 0.8 %collective-permute-start.3 = (f32[136,128]{1,0:T(8,128)S(1)}, f32[136,128]{1,0:T(8,128)S(1)}, u32[]{:S(2)}, u32[]{:S(2)}) collective-permute-start(f32[136,128]{1,0:T(8,128)S(1)} %pair.1.refs_3_), channel_id=1, source_target_pairs={{0,8},{8,0},{16,24},{24,16},{1,9},{9,1},{17,25},{25,17},{2,10},{10... | collective-permute-start | bytes 208904 | tf_op jit(solution)/shard_map/ppermute | solution.py:34
  14.3 2.1 %collective-permute-done.1.refs_0_ = f32[136,128]{1,0:T(8,128)S(1)} collective-permute-done((f32[136,128]{1,0:T(8,128)S(1)}, f32[136,128]{1,0:T(8,128)S(1)}, u32[]{:S(2)}, u32[]{:S(2)}) %collective-permute-start.1) | collective-permute-done | bytes 69664 | tf_op jit(solution)/shard_map/ppermute | solution.py:34
  16.4 3.3 %collective-permute-done.2.refs_1_ = f32[136,128]{1,0:T(8,128)S(1)} collective-permute-done((f32[136,128]{1,0:T(8,128)S(1)}, f32[136,128]{1,0:T(8,128)S(1)}, u32[]{:S(2)}, u32[]{:S(2)}) %collective-permute-start.2) | collective-permute-done | bytes 69664 | tf_op jit(solution)/shard_map/ppermute | solution.py:34
  19.7 0.0 collective-permute-done.3.refs_2_
  19.8 0.1 collective-permute-start.4
  19.8 0.0 copy-done.1
  19.9 0.0 copy-done.2
  19.9 0.6 %gain.1 = (f32[2,512]{1,0:T(2,128)}, f32[8,128]{1,0:T(8,128)S(1)}) custom-call(f32[8,128]{1,0:T(8,128)S(1)} %get-tuple-element.47.mean_ref, f32[2,512]{1,0:T(2,128)S(1)} %copy-done.1, f32[2,512]{1,0:T(2,128)S(1)} %copy-done.2), custom_call_target="tpu_custom_call" | custom-call | tf_op jit(solution)/shard_map/gain/pallas_call | solution.py:448
  20.5 0.6 %collective-permute-done.4.other_ref = f32[128,128]{1,0:T(8,128)S(1)} collective-permute-done((f32[128,128]{1,0:T(8,128)S(1)}, f32[128,128]{1,0:T(8,128)S(1)}, u32[]{:S(2)}, u32[]{:S(2)}) %collective-permute-start.4) | collective-permute-done | bytes 65568 | tf_op jit(solution)/shard_map/ppermute | solution.py:34
  21.1 0.0 copy-done
  21.1 0.8 %right.1 = (f32[128,128]{1,0:T(8,128)S(1)}, f32[8,128]{1,0:T(8,128)S(1)}, f32[64,512]{1,0:T(8,128)S(1)}, f32[128,128]{1,0:T(8,128)S(1)}) custom-call(f32[128,128]{1,0:T(8,128)S(1)} %get-tuple-element.46.mine_ref, f32[128,128]{1,0:T(8,128)S(1)} %collective-permute-done.4.other_ref, f32[32,32]{1,0:T(8,128)S(1)} %copy-done, ...), custom_call_target="tpu_custom_call" | custom-call | tf_op jit(solution)/shard_map/right/pallas_call | solution.py:452
  21.9 2.5 %collective-permute-start.5 = (f32[128,128]{1,0:T(8,128)S(1)}, f32[128,128]{1,0:T(8,128)S(1)}, u32[]{:S(2)}, u32[]{:S(2)}) collective-permute-start(f32[128,128]{1,0:T(8,128)S(1)} %get-tuple-element.49.refs_3_), channel_id=1, source_target_pairs={{0,24},{8,16},{16,8},{24,0},{1,25},{9,17},{17,9},{25,1},{2,26},{10... | collective-permute-start | bytes 196616 | tf_op jit(solution)/shard_map/ppermute | solution.py:34
  24.4 0.1 collective-permute-start.6
  24.5 1.9 %collective-permute-start.7 = (f32[128,128]{1,0:T(8,128)S(1)}, f32[128,128]{1,0:T(8,128)S(1)}, u32[]{:S(2)}, u32[]{:S(2)}) collective-permute-start(f32[128,128]{1,0:T(8,128)S(1)} %get-tuple-element.49.refs_3_), channel_id=1, source_target_pairs={{0,8},{8,0},{16,24},{24,16},{1,9},{9,1},{17,25},{25,17},{2,10},{10... | collective-permute-start | bytes 196616 | tf_op jit(solution)/shard_map/ppermute | solution.py:34
  26.3 2.4 %collective-permute-done.5.refs_0_ = f32[128,128]{1,0:T(8,128)S(1)} collective-permute-done((f32[128,128]{1,0:T(8,128)S(1)}, f32[128,128]{1,0:T(8,128)S(1)}, u32[]{:S(2)}, u32[]{:S(2)}) %collective-permute-start.5) | collective-permute-done | bytes 65568 | tf_op jit(solution)/shard_map/ppermute | solution.py:34
  28.7 2.2 %collective-permute-done.6.refs_1_ = f32[128,128]{1,0:T(8,128)S(1)} collective-permute-done((f32[128,128]{1,0:T(8,128)S(1)}, f32[128,128]{1,0:T(8,128)S(1)}, u32[]{:S(2)}, u32[]{:S(2)}) %collective-permute-start.6) | collective-permute-done | bytes 65568 | tf_op jit(solution)/shard_map/ppermute | solution.py:34
  30.9 0.0 collective-permute-done.7.refs_2_
  30.9 0.5 collective-permute-start.8
  31.5 1.5 %collective-permute-start.10 = (f32[272,128]{1,0:T(8,128)S(1)}, f32[272,128]{1,0:T(8,128)S(1)}, u32[]{:S(2)}, u32[]{:S(2)}) collective-permute-start(f32[272,128]{1,0:T(8,128)S(1)} %get-tuple-element.53), channel_id=1, source_target_pairs={{0,1},{1,0},{2,3},{3,2},{4,5},{5,4},{6,7},{7,6},{8,9},{9,8},{10,11... | collective-permute-start | bytes 417800 | tf_op jit(solution)/shard_map/ppermute | solution.py:34
  33.0 1.5 %collective-permute-start.9 = (f32[272,128]{1,0:T(8,128)S(1)}, f32[272,128]{1,0:T(8,128)S(1)}, u32[]{:S(2)}, u32[]{:S(2)}) collective-permute-start(f32[272,128]{1,0:T(8,128)S(1)} %get-tuple-element.53), channel_id=1, source_target_pairs={{0,2},{1,3},{2,0},{3,1},{4,6},{5,7},{6,4},{7,5},{8,10},{9,11},{10,... | collective-permute-start | bytes 417800 | tf_op jit(solution)/shard_map/ppermute | solution.py:34
  34.5 0.0 collective-permute-done.12.back_ref
  34.5 0.0 collective-permute-done.13.front_ref
  34.5 0.1 relay.1
  34.6 0.6 collective-permute-start.18
  35.1 0.5 collective-permute-start.16
  35.7 1.4 %collective-permute-done.8.in_ref = f32[144,128]{1,0:T(8,128)S(1)} collective-permute-done((f32[144,128]{1,0:T(8,128)S(1)}, f32[144,128]{1,0:T(8,128)S(1)}, u32[]{:S(2)}, u32[]{:S(2)}) %collective-permute-start.8) | collective-permute-done | bytes 73760 | tf_op jit(solution)/shard_map/ppermute | solution.py:34
  37.0 0.5 collective-permute-start.17
  37.6 1.5 %collective-permute-done.10.refs_2_ = f32[272,128]{1,0:T(8,128)S(1)} collective-permute-done((f32[272,128]{1,0:T(8,128)S(1)}, f32[272,128]{1,0:T(8,128)S(1)}, u32[]{:S(2)}, u32[]{:S(2)}) %collective-permute-start.10) | collective-permute-done | bytes 139296 | tf_op jit(solution)/shard_map/ppermute | solution.py:34
  39.1 0.8 %collective-permute-done.9.refs_1_ = f32[272,128]{1,0:T(8,128)S(1)} collective-permute-done((f32[272,128]{1,0:T(8,128)S(1)}, f32[272,128]{1,0:T(8,128)S(1)}, u32[]{:S(2)}, u32[]{:S(2)}) %collective-permute-start.9) | collective-permute-done | bytes 139296 | tf_op jit(solution)/shard_map/ppermute | solution.py:34
  39.8 0.3 factor.1
  40.2 0.1 collective-permute-start.11
  40.2 1.3 %collective-permute-done.11.other_ref = f32[264,128]{1,0:T(8,128)S(1)} collective-permute-done((f32[264,128]{1,0:T(8,128)S(1)}, f32[264,128]{1,0:T(8,128)S(1)}, u32[]{:S(2)}, u32[]{:S(2)}) %collective-permute-start.11) | collective-permute-done | bytes 135200 | tf_op jit(solution)/shard_map/ppermute | solution.py:34
  41.6 0.9 %after.1 = (bf16[544,512]{1,0:T(8,128)(2,1)S(1)}, bf16[544,512]{1,0:T(8,128)(2,1)S(1)}, f32[8,128]{1,0:T(8,128)S(1)}, f32[64,512]{1,0:T(8,128)S(1)}, f32[64,512]{1,0:T(8,128)S(1)}, /*index=5*/s32[1]{0:T(128)}) custom-call(f32[32,512]{1,0:T(8,128)S(1)} %get-tuple-element.54.newbasis_ref, f32[8,128]{1,0:T(8,128)S(1)} %get-tuple-element.55.gram_ref, ...), custom_call_target="tpu_custom_call" | custom-call | tf_op jit(solution)/shard_map/after/pallas_call | solution.py:484
  42.5 0.5 collective-permute-start.14
  43.0 1.4 %collective-permute-start.15 = (bf16[544,512]{1,0:T(8,128)(2,1)S(1)}, bf16[544,512]{1,0:T(8,128)(2,1)S(1)}, u32[]{:S(2)}, u32[]{:S(2)}) collective-permute-start(bf16[544,512]{1,0:T(8,128)(2,1)S(1)} %get-tuple-element.62), channel_id=1, source_target_pairs={{0,2},{1,3},{2,0},{3,1},{8,9},{9,8},{10,11},{11,10},{16,18},{17,19... | collective-permute-start | bytes 1671176 | tf_op jit(solution)/shard_map/ppermute | solution.py:49
  44.4 0.1 collective-permute-done.16._.more_back_ref
  44.5 1.0 %collective-permute-done.17.__.more_front_ref = f32[144,512]{1,0:T(8,128)S(1)} collective-permute-done((f32[144,512]{1,0:T(8,128)S(1)}, f32[144,512]{1,0:T(8,128)S(1)}, u32[]{:S(2)}, u32[]{:S(2)}) %collective-permute-start.17) | collective-permute-done | bytes 294944 | tf_op jit(solution)/shard_map/ppermute | solution.py:49
  45.4 0.8 %collective-permute-done.18.___.came_ref = f32[224,512]{1,0:T(8,128)S(1)} collective-permute-done((f32[224,512]{1,0:T(8,128)S(1)}, f32[224,512]{1,0:T(8,128)S(1)}, u32[]{:S(2)}, u32[]{:S(2)}) %collective-permute-start.18) | collective-permute-done | bytes 458784 | tf_op jit(solution)/shard_map/ppermute | solution.py:34
  46.3 0.5 cross.1
  46.7 0.3 collective-permute-start.19
  47.1 0.0 collective-permute-start.20
  47.1 1.2 %collective-permute-done.20.other_ref = f32[2,2048]{1,0:T(2,128)S(1)} collective-permute-done((f32[2,2048]{1,0:T(2,128)S(1)}, f32[2,2048]{1,0:T(2,128)S(1)}, u32[]{:S(2)}, u32[]{:S(2)}) %collective-permute-start.20) | collective-permute-done | bytes 16416 | tf_op jit(solution)/shard_map/ppermute | solution.py:34
  48.3 0.6 %gains.1 = f32[2,4096]{1,0:T(2,128)} custom-call(f32[2,2048]{1,0:T(2,128)S(1)} %get-tuple-element.73.wide_ref, f32[2,2048]{1,0:T(2,128)S(1)} %collective-permute-done.20.other_ref), custom_call_target="tpu_custom_call" | custom-call | tf_op jit(solution)/shard_map/gains/pallas_call | solution.py:543
  48.9 6.1 %own.1 = (bf16[1024,512]{1,0:T(8,128)(2,1)}, f32[1024,512]{1,0:T(8,128)}, bf16[4096,512]{1,0:T(8,128)(2,1)}) custom-call(s32[1]{0:T(128)} %get-tuple-element.69.place_ref, f32[8,128]{1,0:T(8,128)S(1)} %get-tuple-element.63.scale_ref, f32[32,512]{1,0:T(8,128)S(1)} %get-tuple-element.54.newbasis_ref, f32[64,512]{1,0:T(8,128)S(1)} %get-tuple-element.57.own_ref, ...), custom_call_target="tpu_custom_call" | custom-call | tf_op jit(solution)/shard_map/own/pallas_call | solution.py:508
  55.0 1.5 %near.1.held_ref = bf16[4096,512]{1,0:T(8,128)(2,1)} custom-call(f32[8,128]{1,0:T(8,128)S(1)} %get-tuple-element.63.scale_ref, f32[32,512]{1,0:T(8,128)S(1)} %get-tuple-element.54.newbasis_ref, f32[64,512]{1,0:T(8,128)S(1)} %get-tuple-element.64.back_left_ref, f32[64,512]{1,0:T(8,128)S(1)} %get-tuple-element.65.front_left_ref, ...), custom_call_target="tpu_custom_call", output_to_operand_aliasing={{}: (9, {})} | custom-call | tf_op jit(solution)/shard_map/near/pallas_call | solution.py:525
  56.5 0.7 %collective-permute-done.14.from_back_ref = bf16[544,512]{1,0:T(8,128)(2,1)S(1)} collective-permute-done((bf16[544,512]{1,0:T(8,128)(2,1)S(1)}, bf16[544,512]{1,0:T(8,128)(2,1)S(1)}, u32[]{:S(2)}, u32[]{:S(2)}) %collective-permute-start.14) | collective-permute-done | bytes 557088 | tf_op jit(solution)/shard_map/ppermute | solution.py:49
  57.3 0.1 collective-permute-done.15.from_front_ref
  57.4 0.1 collective-permute-done.19.cross_ref
  57.5 1.2 %settle.1 = bf16[4096,512]{1,0:T(8,128)(2,1)} custom-call(bf16[544,512]{1,0:T(8,128)(2,1)S(1)} %collective-permute-done.14.from_back_ref, bf16[544,512]{1,0:T(8,128)(2,1)S(1)} %collective-permute-done.15.from_front_ref, bf16[448,512]{1,0:T(8,128)(2,1)S(1)} %collective-permute-done.19.cross_ref, ...), custom_call_target="tpu_custom_call", output_to_operand_aliasing={{}: (3, {})} | custom-call | tf_op jit(solution)/shard_map/settle/pallas_call | solution.py:534
  (4 shorter events, 0.1 us)
Async XLA Ops:
  0.6 19.2 %copy-start.1 = (f32[2,512]{1,0:T(2,128)S(1)}, f32[2,512]{1,0:T(2,128)}, u32[]{:S(2)}) copy-start(f32[2,512]{1,0:T(2,128)} %gain_ref.1) | copy-start | bytes 12292
  0.6 19.2 %copy-start.2 = (f32[2,512]{1,0:T(2,128)S(1)}, f32[2,512]{1,0:T(2,128)}, u32[]{:S(2)}) copy-start(f32[2,512]{1,0:T(2,128)} %gain_momentum_ref.1) | copy-start | bytes 12292
  0.7 20.4 %copy-start = (f32[32,32]{1,0:T(8,128)S(1)}, f32[32,32]{1,0:T(8,128)}, u32[]{:S(2)}) copy-start(f32[32,32]{1,0:T(8,128)} %root_ref.1) | copy-start | bytes 12292
  3.3 31.2 %collective-permute-start.12 = (f32[512,512]{1,0:T(8,128)S(1)}, f32[512,512]{1,0:T(8,128)S(1)}, u32[]{:S(2)}, u32[]{:S(2)}) collective-permute-start(f32[512,512]{1,0:T(8,128)S(1)} %get-tuple-element.59), channel_id=1, source_target_pairs={{0,1},{1,0},{2,3},{3,2},{8,10},{9,11},{10,8},{11,9},{16,17},{17,16... | collective-permute-start | bytes 3145736 | tf_op jit(solution)/shard_map/ppermute | solution.py:49
  6.3 28.2 %collective-permute-start.13 = (f32[512,512]{1,0:T(8,128)S(1)}, f32[512,512]{1,0:T(8,128)S(1)}, u32[]{:S(2)}, u32[]{:S(2)}) collective-permute-start(f32[512,512]{1,0:T(8,128)S(1)} %get-tuple-element.60), channel_id=1, source_target_pairs={{0,2},{1,3},{2,0},{3,1},{8,9},{9,8},{10,11},{11,10},{16,18},{17,19... | collective-permute-start | bytes 3145736 | tf_op jit(solution)/shard_map/ppermute | solution.py:49
  8.5 1.3 %collective-permute-start = (f32[128,128]{1,0:T(8,128)S(1)}, f32[128,128]{1,0:T(8,128)S(1)}, u32[]{:S(2)}, u32[]{:S(2)}) collective-permute-start(f32[128,128]{1,0:T(8,128)S(1)} %get-tuple-element.45), channel_id=1, source_target_pairs={{0,4},{4,0},{1,5},{5,1},{2,6},{6,2},{3,7},{7,3},{8,12},{12,8},{9,1... | collective-permute-start | bytes 196616 | tf_op jit(solution)/shard_map/ppermute | solution.py:34
  9.9 6.5 %collective-permute-start.1 = (f32[136,128]{1,0:T(8,128)S(1)}, f32[136,128]{1,0:T(8,128)S(1)}, u32[]{:S(2)}, u32[]{:S(2)}) collective-permute-start(f32[136,128]{1,0:T(8,128)S(1)} %pair.1.refs_3_), channel_id=1, source_target_pairs={{0,24},{8,16},{16,8},{24,0},{1,25},{9,17},{17,9},{25,1},{2,26},{10... | collective-permute-start | bytes 208904 | tf_op jit(solution)/shard_map/ppermute | solution.py:34
  13.5 6.2 %collective-permute-start.2 = (f32[136,128]{1,0:T(8,128)S(1)}, f32[136,128]{1,0:T(8,128)S(1)}, u32[]{:S(2)}, u32[]{:S(2)}) collective-permute-start(f32[136,128]{1,0:T(8,128)S(1)} %pair.1.refs_3_), channel_id=1, source_target_pairs={{0,16},{8,24},{16,0},{24,8},{1,17},{9,25},{17,1},{25,9},{2,18},{10... | collective-permute-start | bytes 208904 | tf_op jit(solution)/shard_map/ppermute | solution.py:34
  13.5 6.2 %collective-permute-start.3 = (f32[136,128]{1,0:T(8,128)S(1)}, f32[136,128]{1,0:T(8,128)S(1)}, u32[]{:S(2)}, u32[]{:S(2)}) collective-permute-start(f32[136,128]{1,0:T(8,128)S(1)} %pair.1.refs_3_), channel_id=1, source_target_pairs={{0,8},{8,0},{16,24},{24,16},{1,9},{9,1},{17,25},{25,17},{2,10},{10... | collective-permute-start | bytes 208904 | tf_op jit(solution)/shard_map/ppermute | solution.py:34
  19.8 1.3 %collective-permute-start.4 = (f32[128,128]{1,0:T(8,128)S(1)}, f32[128,128]{1,0:T(8,128)S(1)}, u32[]{:S(2)}, u32[]{:S(2)}) collective-permute-start(f32[128,128]{1,0:T(8,128)S(1)} %get-tuple-element.46.mine_ref), channel_id=1, source_target_pairs={{0,4},{4,0},{1,5},{5,1},{2,6},{6,2},{3,7},{7,3},{8,12},{12,8},{9,1... | collective-permute-start | bytes 196616 | tf_op jit(solution)/shard_map/ppermute | solution.py:34
  21.9 6.8 %collective-permute-start.5 = (f32[128,128]{1,0:T(8,128)S(1)}, f32[128,128]{1,0:T(8,128)S(1)}, u32[]{:S(2)}, u32[]{:S(2)}) collective-permute-start(f32[128,128]{1,0:T(8,128)S(1)} %get-tuple-element.49.refs_3_), channel_id=1, source_target_pairs={{0,24},{8,16},{16,8},{24,0},{1,25},{9,17},{17,9},{25,1},{2,26},{10... | collective-permute-start | bytes 196616 | tf_op jit(solution)/shard_map/ppermute | solution.py:34
  24.4 6.5 %collective-permute-start.6 = (f32[128,128]{1,0:T(8,128)S(1)}, f32[128,128]{1,0:T(8,128)S(1)}, u32[]{:S(2)}, u32[]{:S(2)}) collective-permute-start(f32[128,128]{1,0:T(8,128)S(1)} %get-tuple-element.49.refs_3_), channel_id=1, source_target_pairs={{0,16},{8,24},{16,0},{24,8},{1,17},{9,25},{17,1},{25,9},{2,18},{10... | collective-permute-start | bytes 196616 | tf_op jit(solution)/shard_map/ppermute | solution.py:34
  24.5 6.5 %collective-permute-start.7 = (f32[128,128]{1,0:T(8,128)S(1)}, f32[128,128]{1,0:T(8,128)S(1)}, u32[]{:S(2)}, u32[]{:S(2)}) collective-permute-start(f32[128,128]{1,0:T(8,128)S(1)} %get-tuple-element.49.refs_3_), channel_id=1, source_target_pairs={{0,8},{8,0},{16,24},{24,16},{1,9},{9,1},{17,25},{25,17},{2,10},{10... | collective-permute-start | bytes 196616 | tf_op jit(solution)/shard_map/ppermute | solution.py:34
  30.9 6.1 %collective-permute-start.8 = (f32[144,128]{1,0:T(8,128)S(1)}, f32[144,128]{1,0:T(8,128)S(1)}, u32[]{:S(2)}, u32[]{:S(2)}) collective-permute-start(f32[144,128]{1,0:T(8,128)S(1)} %get-tuple-element.52.refs_3_._), channel_id=1, source_target_pairs={{0,3},{1,2},{2,1},{3,0},{4,7},{5,6},{6,5},{7,4},{8,11},{9,10},{10,... | collective-permute-start | bytes 221192 | tf_op jit(solution)/shard_map/ppermute | solution.py:34
  31.5 7.6 %collective-permute-start.10 = (f32[272,128]{1,0:T(8,128)S(1)}, f32[272,128]{1,0:T(8,128)S(1)}, u32[]{:S(2)}, u32[]{:S(2)}) collective-permute-start(f32[272,128]{1,0:T(8,128)S(1)} %get-tuple-element.53), channel_id=1, source_target_pairs={{0,1},{1,0},{2,3},{3,2},{4,5},{5,4},{6,7},{7,6},{8,9},{9,8},{10,11... | collective-permute-start | bytes 417800 | tf_op jit(solution)/shard_map/ppermute | solution.py:34
  33.0 6.9 %collective-permute-start.9 = (f32[272,128]{1,0:T(8,128)S(1)}, f32[272,128]{1,0:T(8,128)S(1)}, u32[]{:S(2)}, u32[]{:S(2)}) collective-permute-start(f32[272,128]{1,0:T(8,128)S(1)} %get-tuple-element.53), channel_id=1, source_target_pairs={{0,2},{1,3},{2,0},{3,1},{4,6},{5,7},{6,4},{7,5},{8,10},{9,11},{10,... | collective-permute-start | bytes 417800 | tf_op jit(solution)/shard_map/ppermute | solution.py:34
  34.6 11.7 %collective-permute-start.18 = (f32[224,512]{1,0:T(8,128)S(1)}, f32[224,512]{1,0:T(8,128)S(1)}, u32[]{:S(2)}, u32[]{:S(2)}) collective-permute-start(f32[224,512]{1,0:T(8,128)S(1)} %get-tuple-element.68), channel_id=1, source_target_pairs={{0,8},{8,0},{16,24},{24,16},{1,9},{9,1},{17,25},{25,17},{2,10},{10... | collective-permute-start | bytes 1376264 | tf_op jit(solution)/shard_map/ppermute | solution.py:34
  35.1 9.3 %collective-permute-start.16 = (f32[144,512]{1,0:T(8,128)S(1)}, f32[144,512]{1,0:T(8,128)S(1)}, u32[]{:S(2)}, u32[]{:S(2)}) collective-permute-start(f32[144,512]{1,0:T(8,128)S(1)} %get-tuple-element.66), channel_id=1, source_target_pairs={{0,1},{1,0},{2,3},{3,2},{8,10},{9,11},{10,8},{11,9},{16,17},{17,16... | collective-permute-start | bytes 884744 | tf_op jit(solution)/shard_map/ppermute | solution.py:49
  37.0 8.4 %collective-permute-start.17 = (f32[144,512]{1,0:T(8,128)S(1)}, f32[144,512]{1,0:T(8,128)S(1)}, u32[]{:S(2)}, u32[]{:S(2)}) collective-permute-start(f32[144,512]{1,0:T(8,128)S(1)} %get-tuple-element.67), channel_id=1, source_target_pairs={{0,2},{1,3},{2,0},{3,1},{8,9},{9,8},{10,11},{11,10},{16,18},{17,19... | collective-permute-start | bytes 884744 | tf_op jit(solution)/shard_map/ppermute | solution.py:49
  40.2 1.4 %collective-permute-start.11 = (f32[264,128]{1,0:T(8,128)S(1)}, f32[264,128]{1,0:T(8,128)S(1)}, u32[]{:S(2)}, u32[]{:S(2)}) collective-permute-start(f32[264,128]{1,0:T(8,128)S(1)} %get-tuple-element.56.mine_ref), channel_id=1, source_target_pairs={{0,4},{4,0},{1,5},{5,1},{2,6},{6,2},{3,7},{7,3},{8,12},{12,8},{9,1... | collective-permute-start | bytes 405512 | tf_op jit(solution)/shard_map/ppermute | solution.py:34
  42.5 14.7 %collective-permute-start.14 = (bf16[544,512]{1,0:T(8,128)(2,1)S(1)}, bf16[544,512]{1,0:T(8,128)(2,1)S(1)}, u32[]{:S(2)}, u32[]{:S(2)}) collective-permute-start(bf16[544,512]{1,0:T(8,128)(2,1)S(1)} %get-tuple-element.61), channel_id=1, source_target_pairs={{0,1},{1,0},{2,3},{3,2},{8,10},{9,11},{10,8},{11,9},{16,17},{17,16... | collective-permute-start | bytes 1671176 | tf_op jit(solution)/shard_map/ppermute | solution.py:49
  43.0 14.4 %collective-permute-start.15 = (bf16[544,512]{1,0:T(8,128)(2,1)S(1)}, bf16[544,512]{1,0:T(8,128)(2,1)S(1)}, u32[]{:S(2)}, u32[]{:S(2)}) collective-permute-start(bf16[544,512]{1,0:T(8,128)(2,1)S(1)} %get-tuple-element.62), channel_id=1, source_target_pairs={{0,2},{1,3},{2,0},{3,1},{8,9},{9,8},{10,11},{11,10},{16,18},{17,19... | collective-permute-start | bytes 1671176 | tf_op jit(solution)/shard_map/ppermute | solution.py:49
  46.7 10.8 %collective-permute-start.19 = (bf16[448,512]{1,0:T(8,128)(2,1)S(1)}, bf16[448,512]{1,0:T(8,128)(2,1)S(1)}, u32[]{:S(2)}, u32[]{:S(2)}) collective-permute-start(bf16[448,512]{1,0:T(8,128)(2,1)S(1)} %cross.1), channel_id=1, source_target_pairs={{0,8},{8,0},{16,24},{24,16},{1,9},{9,1},{17,25},{25,17},{2,10},{10... | collective-permute-start | bytes 1376264 | tf_op jit(solution)/shard_map/ppermute | solution.py:34
  47.1 1.2 %collective-permute-start.20 = (f32[2,2048]{1,0:T(2,128)S(1)}, f32[2,2048]{1,0:T(2,128)S(1)}, u32[]{:S(2)}, u32[]{:S(2)}) collective-permute-start(f32[2,2048]{1,0:T(2,128)S(1)} %get-tuple-element.73.wide_ref), channel_id=1, source_target_pairs={{0,4},{4,0},{1,5},{5,1},{2,6},{6,2},{3,7},{7,3},{8,12},{12,8},{9,1... | collective-permute-start | bytes 49160 | tf_op jit(solution)/shard_map/ppermute | solution.py:34

commit v6 on v5

--- a/solution.py
+++ b/solution.py
@@ -501,7 +501,7 @@
     )(scale, newbasis, back_left, front_left, back, front, more_back, more_front, came)
     late_cross = swap(to_cross, "replica", 1)
 
-    blocks = 4
+    blocks = 2
     block = rows // blocks
     step = pl.BlockSpec((block, cols), lambda i, place: (i, 0))
     fixed = [pl.BlockSpec(x.shape, lambda i, place: (0, 0)) for x in (scale, newbasis, ortho)]

time: 58.9 us -> 58.8 us (level)
  waiting for transfers between devices: 20.9 us -> 22 us
  Pallas kernels: 16 us -> 14.9 us
    ppermute x6, waiting for transfers between devices: 1.91 us -> 2.99 us  [beside(): return lax.ppermute(x, ('replica', 'section'), pairs)]
    pallas_call x1, Pallas kernels: 6.09 us -> 5.01 us  [on_device(): pl.pallas_call(own_kernel, out_shape=[pltpu.HBM((rows, cols), BF16), pltp...]
  transfers between devices with their start and end apart: 21 -> 21, of which waited for: 17 -> 17; matrix products, arithmetic and copies ran while one was open for 0% -> 0% of each run, Pallas kernels for 21% -> 19%
where the time goes in v6:
time: 58.8 us; the launch traced here: 58.7 us
  waiting for transfers between devices  22 us (37%)
  starting transfers between devices  21 us (36%)
  Pallas kernels  14.9 us (25%)
  between operations  0.78 us (1%)
    ppermute x15, waiting for transfers between devices, swap(): return lax.ppermute(x, axis, [(i, i ^ distance) for i in range(count)])  19 us
    ppermute x15, starting transfers between devices, swap(): return lax.ppermute(x, axis, [(i, i ^ distance) for i in range(count)])  13.5 us
    ppermute x6, starting transfers between devices, beside(): return lax.ppermute(x, ('replica', 'section'), pairs)  7.44 us
    pallas_call x1, Pallas kernels, on_device(): pl.pallas_call(own_kernel, out_shape=[pltpu.HBM((rows, cols), BF16), pltp...  5.01 us
    ppermute x6, waiting for transfers between devices, beside(): return lax.ppermute(x, ('replica', 'section'), pairs)  2.99 us
    pallas_call x1, Pallas kernels, on_device(): call(start_kernel, 'start', [pltpu.VMEM((half, cols), F32)] * 2 + [pltpu....  2.58 us
    pallas_call x1, Pallas kernels, on_device(): call(near_kernel, 'near', [pltpu.HBM(out.shape, BF16)], [WHOLE] * 9 + [IN...  1.53 us
    pallas_call x1, Pallas kernels, on_device(): call(functools.partial(settle_kernel, more, cross, late), 'settle', [pltp...  1.18 us
  transfers between devices with their start and end apart: 21, of which 17 were waited for; matrix products, arithmetic and copies ran while one was open for 0% of the time, Pallas kernels for 19%

profile of v6, /device:TPU:0, one launch (start us, length us, event | category | flops | bytes accessed | tf_op | source)
XLA Modules:
  0.0 58.7 jit_solution(347152995799775880)
XLA Ops:
  0.6 0.0 copy-start.1
  0.6 0.0 copy-start.2
  0.7 0.0 copy-start
  0.7 2.6 %start.1 = (f32[512,512]{1,0:T(8,128)S(1)}, f32[512,512]{1,0:T(8,128)S(1)}, f32[352,512]{1,0:T(8,128)S(1)}, bf16[1024,512]{1,0:T(8,128)(2,1)S(1)}, bf16[1024,512...) custom-call(bf16[1024,512]{1,0:T(8,128)(2,1)} %weight_ref.1, f32[1024,512]{1,0:T(8,128)} %momentum_ref.1, ...), custom_call_target="tpu_custom_call" | custom-call | tf_op jit(solution)/shard_map/start/pallas_call | solution.py:420
  3.3 3.0 %collective-permute-start.12 = (f32[512,512]{1,0:T(8,128)S(1)}, f32[512,512]{1,0:T(8,128)S(1)}, u32[]{:S(2)}, u32[]{:S(2)}) collective-permute-start(f32[512,512]{1,0:T(8,128)S(1)} %get-tuple-element.59), channel_id=1, source_target_pairs={{0,1},{1,0},{2,3},{3,2},{8,10},{9,11},{10,8},{11,9},{16,17},{17,16... | collective-permute-start | bytes 3145736 | tf_op jit(solution)/shard_map/ppermute | solution.py:49
  6.3 1.5 %collective-permute-start.13 = (f32[512,512]{1,0:T(8,128)S(1)}, f32[512,512]{1,0:T(8,128)S(1)}, u32[]{:S(2)}, u32[]{:S(2)}) collective-permute-start(f32[512,512]{1,0:T(8,128)S(1)} %get-tuple-element.60), channel_id=1, source_target_pairs={{0,2},{1,3},{2,0},{3,1},{8,9},{9,8},{10,11},{11,10},{16,18},{17,19... | collective-permute-start | bytes 3145736 | tf_op jit(solution)/shard_map/ppermute | solution.py:49
  7.8 0.7 %left.1 = (f32[136,128]{1,0:T(8,128)S(1)}, f32[128,128]{1,0:T(8,128)S(1)}) custom-call(f32[32,512]{1,0:T(8,128)S(1)} %get-tuple-element.40.basis_ref, f32[2,512]{1,0:T(2,128)S(1)} %get-tuple-element.41.gains_ref, bf16[1024,512]{1,0:T(8,128)(2,1)S(1)} %get-tuple-element.42.grads_ref, bf16[1024,512]{1,0:T(8,128)(2,1)S(1)} %get-tuple-element.43.error_ref), custom_call_target="tpu_custom_call" | custom-call | tf_op jit(solution)/shard_map/left/pallas_call | solution.py:437
  8.5 0.1 collective-permute-start
  8.6 1.2 %collective-permute-done.other_ref = f32[128,128]{1,0:T(8,128)S(1)} collective-permute-done((f32[128,128]{1,0:T(8,128)S(1)}, f32[128,128]{1,0:T(8,128)S(1)}, u32[]{:S(2)}, u32[]{:S(2)}) %collective-permute-start) | collective-permute-done | bytes 65568 | tf_op jit(solution)/shard_map/ppermute | solution.py:34
  9.9 3.7 %collective-permute-start.1 = (f32[136,128]{1,0:T(8,128)S(1)}, f32[136,128]{1,0:T(8,128)S(1)}, u32[]{:S(2)}, u32[]{:S(2)}) collective-permute-start(f32[136,128]{1,0:T(8,128)S(1)} %pair.1.refs_3_), channel_id=1, source_target_pairs={{0,24},{8,16},{16,8},{24,0},{1,25},{9,17},{17,9},{25,1},{2,26},{10... | collective-permute-start | bytes 208904 | tf_op jit(solution)/shard_map/ppermute | solution.py:34
  13.5 0.0 collective-permute-start.2
  13.5 0.8 %collective-permute-start.3 = (f32[136,128]{1,0:T(8,128)S(1)}, f32[136,128]{1,0:T(8,128)S(1)}, u32[]{:S(2)}, u32[]{:S(2)}) collective-permute-start(f32[136,128]{1,0:T(8,128)S(1)} %pair.1.refs_3_), channel_id=1, source_target_pairs={{0,8},{8,0},{16,24},{24,16},{1,9},{9,1},{17,25},{25,17},{2,10},{10... | collective-permute-start | bytes 208904 | tf_op jit(solution)/shard_map/ppermute | solution.py:34
  14.3 2.1 %collective-permute-done.1.refs_0_ = f32[136,128]{1,0:T(8,128)S(1)} collective-permute-done((f32[136,128]{1,0:T(8,128)S(1)}, f32[136,128]{1,0:T(8,128)S(1)}, u32[]{:S(2)}, u32[]{:S(2)}) %collective-permute-start.1) | collective-permute-done | bytes 69664 | tf_op jit(solution)/shard_map/ppermute | solution.py:34
  16.4 3.3 %collective-permute-done.2.refs_1_ = f32[136,128]{1,0:T(8,128)S(1)} collective-permute-done((f32[136,128]{1,0:T(8,128)S(1)}, f32[136,128]{1,0:T(8,128)S(1)}, u32[]{:S(2)}, u32[]{:S(2)}) %collective-permute-start.2) | collective-permute-done | bytes 69664 | tf_op jit(solution)/shard_map/ppermute | solution.py:34
  19.7 0.0 collective-permute-done.3.refs_2_
  19.8 0.1 collective-permute-start.4
  19.8 0.0 copy-done.1
  19.9 0.0 copy-done.2
  19.9 0.6 %gain.1 = (f32[2,512]{1,0:T(2,128)}, f32[8,128]{1,0:T(8,128)S(1)}) custom-call(f32[8,128]{1,0:T(8,128)S(1)} %get-tuple-element.47.mean_ref, f32[2,512]{1,0:T(2,128)S(1)} %copy-done.1, f32[2,512]{1,0:T(2,128)S(1)} %copy-done.2), custom_call_target="tpu_custom_call" | custom-call | tf_op jit(solution)/shard_map/gain/pallas_call | solution.py:448
  20.5 0.6 %collective-permute-done.4.other_ref = f32[128,128]{1,0:T(8,128)S(1)} collective-permute-done((f32[128,128]{1,0:T(8,128)S(1)}, f32[128,128]{1,0:T(8,128)S(1)}, u32[]{:S(2)}, u32[]{:S(2)}) %collective-permute-start.4) | collective-permute-done | bytes 65568 | tf_op jit(solution)/shard_map/ppermute | solution.py:34
  21.1 0.0 copy-done
  21.1 0.8 %right.1 = (f32[128,128]{1,0:T(8,128)S(1)}, f32[8,128]{1,0:T(8,128)S(1)}, f32[64,512]{1,0:T(8,128)S(1)}, f32[128,128]{1,0:T(8,128)S(1)}) custom-call(f32[128,128]{1,0:T(8,128)S(1)} %get-tuple-element.46.mine_ref, f32[128,128]{1,0:T(8,128)S(1)} %collective-permute-done.4.other_ref, f32[32,32]{1,0:T(8,128)S(1)} %copy-done, ...), custom_call_target="tpu_custom_call" | custom-call | tf_op jit(solution)/shard_map/right/pallas_call | solution.py:452
  21.9 2.5 %collective-permute-start.5 = (f32[128,128]{1,0:T(8,128)S(1)}, f32[128,128]{1,0:T(8,128)S(1)}, u32[]{:S(2)}, u32[]{:S(2)}) collective-permute-start(f32[128,128]{1,0:T(8,128)S(1)} %get-tuple-element.49.refs_3_), channel_id=1, source_target_pairs={{0,24},{8,16},{16,8},{24,0},{1,25},{9,17},{17,9},{25,1},{2,26},{10... | collective-permute-start | bytes 196616 | tf_op jit(solution)/shard_map/ppermute | solution.py:34
  24.4 0.1 collective-permute-start.6
  24.5 1.9 %collective-permute-start.7 = (f32[128,128]{1,0:T(8,128)S(1)}, f32[128,128]{1,0:T(8,128)S(1)}, u32[]{:S(2)}, u32[]{:S(2)}) collective-permute-start(f32[128,128]{1,0:T(8,128)S(1)} %get-tuple-element.49.refs_3_), channel_id=1, source_target_pairs={{0,8},{8,0},{16,24},{24,16},{1,9},{9,1},{17,25},{25,17},{2,10},{10... | collective-permute-start | bytes 196616 | tf_op jit(solution)/shard_map/ppermute | solution.py:34
  26.3 2.4 %collective-permute-done.5.refs_0_ = f32[128,128]{1,0:T(8,128)S(1)} collective-permute-done((f32[128,128]{1,0:T(8,128)S(1)}, f32[128,128]{1,0:T(8,128)S(1)}, u32[]{:S(2)}, u32[]{:S(2)}) %collective-permute-start.5) | collective-permute-done | bytes 65568 | tf_op jit(solution)/shard_map/ppermute | solution.py:34
  28.7 2.2 %collective-permute-done.6.refs_1_ = f32[128,128]{1,0:T(8,128)S(1)} collective-permute-done((f32[128,128]{1,0:T(8,128)S(1)}, f32[128,128]{1,0:T(8,128)S(1)}, u32[]{:S(2)}, u32[]{:S(2)}) %collective-permute-start.6) | collective-permute-done | bytes 65568 | tf_op jit(solution)/shard_map/ppermute | solution.py:34
  30.9 0.0 collective-permute-done.7.refs_2_
  30.9 0.5 collective-permute-start.8
  31.5 1.5 %collective-permute-start.10 = (f32[272,128]{1,0:T(8,128)S(1)}, f32[272,128]{1,0:T(8,128)S(1)}, u32[]{:S(2)}, u32[]{:S(2)}) collective-permute-start(f32[272,128]{1,0:T(8,128)S(1)} %get-tuple-element.53), channel_id=1, source_target_pairs={{0,1},{1,0},{2,3},{3,2},{4,5},{5,4},{6,7},{7,6},{8,9},{9,8},{10,11... | collective-permute-start | bytes 417800 | tf_op jit(solution)/shard_map/ppermute | solution.py:34
  33.0 1.5 %collective-permute-start.9 = (f32[272,128]{1,0:T(8,128)S(1)}, f32[272,128]{1,0:T(8,128)S(1)}, u32[]{:S(2)}, u32[]{:S(2)}) collective-permute-start(f32[272,128]{1,0:T(8,128)S(1)} %get-tuple-element.53), channel_id=1, source_target_pairs={{0,2},{1,3},{2,0},{3,1},{4,6},{5,7},{6,4},{7,5},{8,10},{9,11},{10,... | collective-permute-start | bytes 417800 | tf_op jit(solution)/shard_map/ppermute | solution.py:34
  34.5 0.0 collective-permute-done.12.back_ref
  34.5 0.0 collective-permute-done.13.front_ref
  34.5 0.1 relay.1
  34.6 0.6 collective-permute-start.18
  35.1 0.5 collective-permute-start.16
  35.7 1.4 %collective-permute-done.8.in_ref = f32[144,128]{1,0:T(8,128)S(1)} collective-permute-done((f32[144,128]{1,0:T(8,128)S(1)}, f32[144,128]{1,0:T(8,128)S(1)}, u32[]{:S(2)}, u32[]{:S(2)}) %collective-permute-start.8) | collective-permute-done | bytes 73760 | tf_op jit(solution)/shard_map/ppermute | solution.py:34
  37.0 0.5 collective-permute-start.17
  37.6 1.5 %collective-permute-done.10.refs_2_ = f32[272,128]{1,0:T(8,128)S(1)} collective-permute-done((f32[272,128]{1,0:T(8,128)S(1)}, f32[272,128]{1,0:T(8,128)S(1)}, u32[]{:S(2)}, u32[]{:S(2)}) %collective-permute-start.10) | collective-permute-done | bytes 139296 | tf_op jit(solution)/shard_map/ppermute | solution.py:34
  39.1 0.8 %collective-permute-done.9.refs_1_ = f32[272,128]{1,0:T(8,128)S(1)} collective-permute-done((f32[272,128]{1,0:T(8,128)S(1)}, f32[272,128]{1,0:T(8,128)S(1)}, u32[]{:S(2)}, u32[]{:S(2)}) %collective-permute-start.9) | collective-permute-done | bytes 139296 | tf_op jit(solution)/shard_map/ppermute | solution.py:34
  39.8 0.3 factor.1
  40.2 0.1 collective-permute-start.11
  40.2 1.3 %collective-permute-done.11.other_ref = f32[264,128]{1,0:T(8,128)S(1)} collective-permute-done((f32[264,128]{1,0:T(8,128)S(1)}, f32[264,128]{1,0:T(8,128)S(1)}, u32[]{:S(2)}, u32[]{:S(2)}) %collective-permute-start.11) | collective-permute-done | bytes 135200 | tf_op jit(solution)/shard_map/ppermute | solution.py:34
  41.6 0.9 %after.1 = (bf16[544,512]{1,0:T(8,128)(2,1)S(1)}, bf16[544,512]{1,0:T(8,128)(2,1)S(1)}, f32[8,128]{1,0:T(8,128)S(1)}, f32[64,512]{1,0:T(8,128)S(1)}, f32[64,512]{1,0:T(8,128)S(1)}, /*index=5*/s32[1]{0:T(128)}) custom-call(f32[32,512]{1,0:T(8,128)S(1)} %get-tuple-element.54.newbasis_ref, f32[8,128]{1,0:T(8,128)S(1)} %get-tuple-element.55.gram_ref, ...), custom_call_target="tpu_custom_call" | custom-call | tf_op jit(solution)/shard_map/after/pallas_call | solution.py:484
  42.5 0.5 collective-permute-start.14
  43.0 1.4 %collective-permute-start.15 = (bf16[544,512]{1,0:T(8,128)(2,1)S(1)}, bf16[544,512]{1,0:T(8,128)(2,1)S(1)}, u32[]{:S(2)}, u32[]{:S(2)}) collective-permute-start(bf16[544,512]{1,0:T(8,128)(2,1)S(1)} %get-tuple-element.62), channel_id=1, source_target_pairs={{0,2},{1,3},{2,0},{3,1},{8,9},{9,8},{10,11},{11,10},{16,18},{17,19... | collective-permute-start | bytes 1671176 | tf_op jit(solution)/shard_map/ppermute | solution.py:49
  44.4 0.1 collective-permute-done.16._.more_back_ref
  44.5 1.0 %collective-permute-done.17.__.more_front_ref = f32[144,512]{1,0:T(8,128)S(1)} collective-permute-done((f32[144,512]{1,0:T(8,128)S(1)}, f32[144,512]{1,0:T(8,128)S(1)}, u32[]{:S(2)}, u32[]{:S(2)}) %collective-permute-start.17) | collective-permute-done | bytes 294944 | tf_op jit(solution)/shard_map/ppermute | solution.py:49
  45.4 0.8 %collective-permute-done.18.___.came_ref = f32[224,512]{1,0:T(8,128)S(1)} collective-permute-done((f32[224,512]{1,0:T(8,128)S(1)}, f32[224,512]{1,0:T(8,128)S(1)}, u32[]{:S(2)}, u32[]{:S(2)}) %collective-permute-start.18) | collective-permute-done | bytes 458784 | tf_op jit(solution)/shard_map/ppermute | solution.py:34
  46.3 0.5 cross.1
  46.7 0.3 collective-permute-start.19
  47.1 0.0 collective-permute-start.20
  47.1 1.2 %collective-permute-done.20.other_ref = f32[2,2048]{1,0:T(2,128)S(1)} collective-permute-done((f32[2,2048]{1,0:T(2,128)S(1)}, f32[2,2048]{1,0:T(2,128)S(1)}, u32[]{:S(2)}, u32[]{:S(2)}) %collective-permute-start.20) | collective-permute-done | bytes 16416 | tf_op jit(solution)/shard_map/ppermute | solution.py:34
  48.3 0.6 %gains.1 = f32[2,4096]{1,0:T(2,128)} custom-call(f32[2,2048]{1,0:T(2,128)S(1)} %get-tuple-element.73.wide_ref, f32[2,2048]{1,0:T(2,128)S(1)} %collective-permute-done.20.other_ref), custom_call_target="tpu_custom_call" | custom-call | tf_op jit(solution)/shard_map/gains/pallas_call | solution.py:543
  48.9 5.0 %own.1 = (bf16[1024,512]{1,0:T(8,128)(2,1)}, f32[1024,512]{1,0:T(8,128)}, bf16[4096,512]{1,0:T(8,128)(2,1)}) custom-call(s32[1]{0:T(128)} %get-tuple-element.69.place_ref, f32[8,128]{1,0:T(8,128)S(1)} %get-tuple-element.63.scale_ref, f32[32,512]{1,0:T(8,128)S(1)} %get-tuple-element.54.newbasis_ref, f32[64,512]{1,0:T(8,128)S(1)} %get-tuple-element.57.own_ref, ...), custom_call_target="tpu_custom_call" | custom-call | tf_op jit(solution)/shard_map/own/pallas_call | solution.py:508
  53.9 1.5 %near.1.held_ref = bf16[4096,512]{1,0:T(8,128)(2,1)} custom-call(f32[8,128]{1,0:T(8,128)S(1)} %get-tuple-element.63.scale_ref, f32[32,512]{1,0:T(8,128)S(1)} %get-tuple-element.54.newbasis_ref, f32[64,512]{1,0:T(8,128)S(1)} %get-tuple-element.64.back_left_ref, f32[64,512]{1,0:T(8,128)S(1)} %get-tuple-element.65.front_left_ref, ...), custom_call_target="tpu_custom_call", output_to_operand_aliasing={{}: (9, {})} | custom-call | tf_op jit(solution)/shard_map/near/pallas_call | solution.py:525
  55.4 1.8 %collective-permute-done.14.from_back_ref = bf16[544,512]{1,0:T(8,128)(2,1)S(1)} collective-permute-done((bf16[544,512]{1,0:T(8,128)(2,1)S(1)}, bf16[544,512]{1,0:T(8,128)(2,1)S(1)}, u32[]{:S(2)}, u32[]{:S(2)}) %collective-permute-start.14) | collective-permute-done | bytes 557088 | tf_op jit(solution)/shard_map/ppermute | solution.py:49
  57.3 0.1 collective-permute-done.15.from_front_ref
  57.4 0.1 collective-permute-done.19.cross_ref
  57.5 1.2 %settle.1 = bf16[4096,512]{1,0:T(8,128)(2,1)} custom-call(bf16[544,512]{1,0:T(8,128)(2,1)S(1)} %collective-permute-done.14.from_back_ref, bf16[544,512]{1,0:T(8,128)(2,1)S(1)} %collective-permute-done.15.from_front_ref, bf16[448,512]{1,0:T(8,128)(2,1)S(1)} %collective-permute-done.19.cross_ref, ...), custom_call_target="tpu_custom_call", output_to_operand_aliasing={{}: (3, {})} | custom-call | tf_op jit(solution)/shard_map/settle/pallas_call | solution.py:534
  (4 shorter events, 0.1 us)
Async XLA Ops:
  0.6 19.2 %copy-start.1 = (f32[2,512]{1,0:T(2,128)S(1)}, f32[2,512]{1,0:T(2,128)}, u32[]{:S(2)}) copy-start(f32[2,512]{1,0:T(2,128)} %gain_ref.1) | copy-start | bytes 12292
  0.6 19.2 %copy-start.2 = (f32[2,512]{1,0:T(2,128)S(1)}, f32[2,512]{1,0:T(2,128)}, u32[]{:S(2)}) copy-start(f32[2,512]{1,0:T(2,128)} %gain_momentum_ref.1) | copy-start | bytes 12292
  0.7 20.4 %copy-start = (f32[32,32]{1,0:T(8,128)S(1)}, f32[32,32]{1,0:T(8,128)}, u32[]{:S(2)}) copy-start(f32[32,32]{1,0:T(8,128)} %root_ref.1) | copy-start | bytes 12292
  3.3 31.2 %collective-permute-start.12 = (f32[512,512]{1,0:T(8,128)S(1)}, f32[512,512]{1,0:T(8,128)S(1)}, u32[]{:S(2)}, u32[]{:S(2)}) collective-permute-start(f32[512,512]{1,0:T(8,128)S(1)} %get-tuple-element.59), channel_id=1, source_target_pairs={{0,1},{1,0},{2,3},{3,2},{8,10},{9,11},{10,8},{11,9},{16,17},{17,16... | collective-permute-start | bytes 3145736 | tf_op jit(solution)/shard_map/ppermute | solution.py:49
  6.3 28.2 %collective-permute-start.13 = (f32[512,512]{1,0:T(8,128)S(1)}, f32[512,512]{1,0:T(8,128)S(1)}, u32[]{:S(2)}, u32[]{:S(2)}) collective-permute-start(f32[512,512]{1,0:T(8,128)S(1)} %get-tuple-element.60), channel_id=1, source_target_pairs={{0,2},{1,3},{2,0},{3,1},{8,9},{9,8},{10,11},{11,10},{16,18},{17,19... | collective-permute-start | bytes 3145736 | tf_op jit(solution)/shard_map/ppermute | solution.py:49
  8.5 1.3 %collective-permute-start = (f32[128,128]{1,0:T(8,128)S(1)}, f32[128,128]{1,0:T(8,128)S(1)}, u32[]{:S(2)}, u32[]{:S(2)}) collective-permute-start(f32[128,128]{1,0:T(8,128)S(1)} %get-tuple-element.45), channel_id=1, source_target_pairs={{0,4},{4,0},{1,5},{5,1},{2,6},{6,2},{3,7},{7,3},{8,12},{12,8},{9,1... | collective-permute-start | bytes 196616 | tf_op jit(solution)/shard_map/ppermute | solution.py:34
  9.9 6.5 %collective-permute-start.1 = (f32[136,128]{1,0:T(8,128)S(1)}, f32[136,128]{1,0:T(8,128)S(1)}, u32[]{:S(2)}, u32[]{:S(2)}) collective-permute-start(f32[136,128]{1,0:T(8,128)S(1)} %pair.1.refs_3_), channel_id=1, source_target_pairs={{0,24},{8,16},{16,8},{24,0},{1,25},{9,17},{17,9},{25,1},{2,26},{10... | collective-permute-start | bytes 208904 | tf_op jit(solution)/shard_map/ppermute | solution.py:34
  13.5 6.2 %collective-permute-start.2 = (f32[136,128]{1,0:T(8,128)S(1)}, f32[136,128]{1,0:T(8,128)S(1)}, u32[]{:S(2)}, u32[]{:S(2)}) collective-permute-start(f32[136,128]{1,0:T(8,128)S(1)} %pair.1.refs_3_), channel_id=1, source_target_pairs={{0,16},{8,24},{16,0},{24,8},{1,17},{9,25},{17,1},{25,9},{2,18},{10... | collective-permute-start | bytes 208904 | tf_op jit(solution)/shard_map/ppermute | solution.py:34
  13.5 6.2 %collective-permute-start.3 = (f32[136,128]{1,0:T(8,128)S(1)}, f32[136,128]{1,0:T(8,128)S(1)}, u32[]{:S(2)}, u32[]{:S(2)}) collective-permute-start(f32[136,128]{1,0:T(8,128)S(1)} %pair.1.refs_3_), channel_id=1, source_target_pairs={{0,8},{8,0},{16,24},{24,16},{1,9},{9,1},{17,25},{25,17},{2,10},{10... | collective-permute-start | bytes 208904 | tf_op jit(solution)/shard_map/ppermute | solution.py:34
  19.8 1.3 %collective-permute-start.4 = (f32[128,128]{1,0:T(8,128)S(1)}, f32[128,128]{1,0:T(8,128)S(1)}, u32[]{:S(2)}, u32[]{:S(2)}) collective-permute-start(f32[128,128]{1,0:T(8,128)S(1)} %get-tuple-element.46.mine_ref), channel_id=1, source_target_pairs={{0,4},{4,0},{1,5},{5,1},{2,6},{6,2},{3,7},{7,3},{8,12},{12,8},{9,1... | collective-permute-start | bytes 196616 | tf_op jit(solution)/shard_map/ppermute | solution.py:34
  21.9 6.8 %collective-permute-start.5 = (f32[128,128]{1,0:T(8,128)S(1)}, f32[128,128]{1,0:T(8,128)S(1)}, u32[]{:S(2)}, u32[]{:S(2)}) collective-permute-start(f32[128,128]{1,0:T(8,128)S(1)} %get-tuple-element.49.refs_3_), channel_id=1, source_target_pairs={{0,24},{8,16},{16,8},{24,0},{1,25},{9,17},{17,9},{25,1},{2,26},{10... | collective-permute-start | bytes 196616 | tf_op jit(solution)/shard_map/ppermute | solution.py:34
  24.4 6.5 %collective-permute-start.6 = (f32[128,128]{1,0:T(8,128)S(1)}, f32[128,128]{1,0:T(8,128)S(1)}, u32[]{:S(2)}, u32[]{:S(2)}) collective-permute-start(f32[128,128]{1,0:T(8,128)S(1)} %get-tuple-element.49.refs_3_), channel_id=1, source_target_pairs={{0,16},{8,24},{16,0},{24,8},{1,17},{9,25},{17,1},{25,9},{2,18},{10... | collective-permute-start | bytes 196616 | tf_op jit(solution)/shard_map/ppermute | solution.py:34
  24.5 6.5 %collective-permute-start.7 = (f32[128,128]{1,0:T(8,128)S(1)}, f32[128,128]{1,0:T(8,128)S(1)}, u32[]{:S(2)}, u32[]{:S(2)}) collective-permute-start(f32[128,128]{1,0:T(8,128)S(1)} %get-tuple-element.49.refs_3_), channel_id=1, source_target_pairs={{0,8},{8,0},{16,24},{24,16},{1,9},{9,1},{17,25},{25,17},{2,10},{10... | collective-permute-start | bytes 196616 | tf_op jit(solution)/shard_map/ppermute | solution.py:34
  30.9 6.1 %collective-permute-start.8 = (f32[144,128]{1,0:T(8,128)S(1)}, f32[144,128]{1,0:T(8,128)S(1)}, u32[]{:S(2)}, u32[]{:S(2)}) collective-permute-start(f32[144,128]{1,0:T(8,128)S(1)} %get-tuple-element.52.refs_3_._), channel_id=1, source_target_pairs={{0,3},{1,2},{2,1},{3,0},{4,7},{5,6},{6,5},{7,4},{8,11},{9,10},{10,... | collective-permute-start | bytes 221192 | tf_op jit(solution)/shard_map/ppermute | solution.py:34
  31.5 7.6 %collective-permute-start.10 = (f32[272,128]{1,0:T(8,128)S(1)}, f32[272,128]{1,0:T(8,128)S(1)}, u32[]{:S(2)}, u32[]{:S(2)}) collective-permute-start(f32[272,128]{1,0:T(8,128)S(1)} %get-tuple-element.53), channel_id=1, source_target_pairs={{0,1},{1,0},{2,3},{3,2},{4,5},{5,4},{6,7},{7,6},{8,9},{9,8},{10,11... | collective-permute-start | bytes 417800 | tf_op jit(solution)/shard_map/ppermute | solution.py:34
  33.0 6.9 %collective-permute-start.9 = (f32[272,128]{1,0:T(8,128)S(1)}, f32[272,128]{1,0:T(8,128)S(1)}, u32[]{:S(2)}, u32[]{:S(2)}) collective-permute-start(f32[272,128]{1,0:T(8,128)S(1)} %get-tuple-element.53), channel_id=1, source_target_pairs={{0,2},{1,3},{2,0},{3,1},{4,6},{5,7},{6,4},{7,5},{8,10},{9,11},{10,... | collective-permute-start | bytes 417800 | tf_op jit(solution)/shard_map/ppermute | solution.py:34
  34.6 11.7 %collective-permute-start.18 = (f32[224,512]{1,0:T(8,128)S(1)}, f32[224,512]{1,0:T(8,128)S(1)}, u32[]{:S(2)}, u32[]{:S(2)}) collective-permute-start(f32[224,512]{1,0:T(8,128)S(1)} %get-tuple-element.68), channel_id=1, source_target_pairs={{0,8},{8,0},{16,24},{24,16},{1,9},{9,1},{17,25},{25,17},{2,10},{10... | collective-permute-start | bytes 1376264 | tf_op jit(solution)/shard_map/ppermute | solution.py:34
  35.1 9.3 %collective-permute-start.16 = (f32[144,512]{1,0:T(8,128)S(1)}, f32[144,512]{1,0:T(8,128)S(1)}, u32[]{:S(2)}, u32[]{:S(2)}) collective-permute-start(f32[144,512]{1,0:T(8,128)S(1)} %get-tuple-element.66), channel_id=1, source_target_pairs={{0,1},{1,0},{2,3},{3,2},{8,10},{9,11},{10,8},{11,9},{16,17},{17,16... | collective-permute-start | bytes 884744 | tf_op jit(solution)/shard_map/ppermute | solution.py:49
  37.0 8.4 %collective-permute-start.17 = (f32[144,512]{1,0:T(8,128)S(1)}, f32[144,512]{1,0:T(8,128)S(1)}, u32[]{:S(2)}, u32[]{:S(2)}) collective-permute-start(f32[144,512]{1,0:T(8,128)S(1)} %get-tuple-element.67), channel_id=1, source_target_pairs={{0,2},{1,3},{2,0},{3,1},{8,9},{9,8},{10,11},{11,10},{16,18},{17,19... | collective-permute-start | bytes 884744 | tf_op jit(solution)/shard_map/ppermute | solution.py:49
  40.2 1.4 %collective-permute-start.11 = (f32[264,128]{1,0:T(8,128)S(1)}, f32[264,128]{1,0:T(8,128)S(1)}, u32[]{:S(2)}, u32[]{:S(2)}) collective-permute-start(f32[264,128]{1,0:T(8,128)S(1)} %get-tuple-element.56.mine_ref), channel_id=1, source_target_pairs={{0,4},{4,0},{1,5},{5,1},{2,6},{6,2},{3,7},{7,3},{8,12},{12,8},{9,1... | collective-permute-start | bytes 405512 | tf_op jit(solution)/shard_map/ppermute | solution.py:34
  42.5 14.7 %collective-permute-start.14 = (bf16[544,512]{1,0:T(8,128)(2,1)S(1)}, bf16[544,512]{1,0:T(8,128)(2,1)S(1)}, u32[]{:S(2)}, u32[]{:S(2)}) collective-permute-start(bf16[544,512]{1,0:T(8,128)(2,1)S(1)} %get-tuple-element.61), channel_id=1, source_target_pairs={{0,1},{1,0},{2,3},{3,2},{8,10},{9,11},{10,8},{11,9},{16,17},{17,16... | collective-permute-start | bytes 1671176 | tf_op jit(solution)/shard_map/ppermute | solution.py:49
  43.0 14.4 %collective-permute-start.15 = (bf16[544,512]{1,0:T(8,128)(2,1)S(1)}, bf16[544,512]{1,0:T(8,128)(2,1)S(1)}, u32[]{:S(2)}, u32[]{:S(2)}) collective-permute-start(bf16[544,512]{1,0:T(8,128)(2,1)S(1)} %get-tuple-element.62), channel_id=1, source_target_pairs={{0,2},{1,3},{2,0},{3,1},{8,9},{9,8},{10,11},{11,10},{16,18},{17,19... | collective-permute-start | bytes 1671176 | tf_op jit(solution)/shard_map/ppermute | solution.py:49
  46.7 10.8 %collective-permute-start.19 = (bf16[448,512]{1,0:T(8,128)(2,1)S(1)}, bf16[448,512]{1,0:T(8,128)(2,1)S(1)}, u32[]{:S(2)}, u32[]{:S(2)}) collective-permute-start(bf16[448,512]{1,0:T(8,128)(2,1)S(1)} %cross.1), channel_id=1, source_target_pairs={{0,8},{8,0},{16,24},{24,16},{1,9},{9,1},{17,25},{25,17},{2,10},{10... | collective-permute-start | bytes 1376264 | tf_op jit(solution)/shard_map/ppermute | solution.py:34
  47.1 1.2 %collective-permute-start.20 = (f32[2,2048]{1,0:T(2,128)S(1)}, f32[2,2048]{1,0:T(2,128)S(1)}, u32[]{:S(2)}, u32[]{:S(2)}) collective-permute-start(f32[2,2048]{1,0:T(2,128)S(1)} %get-tuple-element.73.wide_ref), channel_id=1, source_target_pairs={{0,4},{4,0},{1,5},{5,1},{2,6},{6,2},{3,7},{7,3},{8,12},{12,8},{9,1... | collective-permute-start | bytes 49160 | tf_op jit(solution)/shard_map/ppermute | solution.py:34
